TPU v7x, 32 devices: a whole 2x2x4 slice. The times are simulated.
32 devices in a mesh: box: 8 (over z, y), orb: 4 (over x, core).
Axes of the slice: x: 2, y: 2, z: 4, core: 2. Of those that a mesh axis runs over, the one named last changes fastest.
Arguments:
- orbitals: bfloat16 [16, 1000, 1536], P('box', None, 'orb'), may hold values from -0.0546875 to 0.0546875
- potential: float32 [16, 1000], P('box'), may hold values from -3 to 1
- deriv_blocks: bfloat16 [3, 10, 10], replicated, may hold values from -1 to 1
- levels: int32 [16], P('box'), may hold values from 0 to 2
- box_counts: int32 [8], P('box'), may hold values from 1 to 2, as said below
- neighbours: int32 [16, 3, 2], P('box'), may hold values from -1 to 15, as said below
Outputs:
- fock: float32 [1536, 1536], P('box', 'orb')
- correlation: float32 [1536, 1536], P('box', 'orb')
- inverse_root: float32 [1536, 1536], P('box', 'orb')
Inputs may be any that keep to these rules, and one draw needn't show every extreme that they name: Each index of box holds box_counts of live slots, which are its first slots; the counts sum to 12, and some index holds 2. `neighbours`: an entry is -1 or the global slot of a live slot, other than the slot itself, on the same index of box or on the index just before or just after it; every entry of a non-live slot is -1.
All inputs are finite; a program needn't handle non-finite values.
Results may differ from a plain program's by a relative error of at most 0.0012.
Values may be sent and summed in bfloat16 or wider, within the bound.
No kernel may reach another device: no remote copies, remote signals or barrier semaphores. Data moves between devices by JAX's collectives and lax.ppermute only.
A program may use at most 128 MiB of HBM per device.

v0:
```python
import functools

import jax
import jax.numpy as jnp
import numpy as np
from jax import lax
from jax.experimental import pallas as pl
from jax.experimental.pallas import tpu as pltpu
from jax.sharding import Mesh, PartitionSpec as P

PAIR = 2
ROWS = 16
BOX = ("lvl", "pair")
f32, bf16 = jnp.float32, jnp.bfloat16


def swap(value, axis, bit):
    count = lax.axis_size(axis)
    return lax.ppermute(value, axis, [(i, i ^ bit) for i in range(count)])


def shift(value, axis, step):
    count = lax.axis_size(axis)
    return lax.ppermute(value, axis, [(i, i + step) for i in range(count) if 0 <= i + step < count])


def contract(left, right):
    return lax.dot_general(left, right, (((0,), (0,)), ((), ())), preferred_element_type=f32)


def matmul(left, right):
    return jnp.dot(left, right, preferred_element_type=f32)


def spread(value, axis, bits):
    return jnp.stack([swap(value, axis, bit) if bit else value for bit in bits])


def kinetic_kernel(edge, slots, table, scale, *refs):
    parts, (pot, fwd_in, fwd_out, back_in, back_out), out = refs[:6], refs[6:11], refs[11]
    raw, x, rounded, left_over, total, total_fix, sems = refs[12:]
    square = edge * edge
    own = PAIR * slots
    width = x.shape[3]
    copies = [pltpu.make_async_copy(part, raw.at[place], sems.at[place]) for place, part in enumerate(parts)]
    for copy in copies:
        copy.start()
    x[...] = jnp.zeros_like(x)
    total[...] = jnp.zeros_like(total)
    total_fix[...] = jnp.zeros_like(total_fix)
    for copy in copies:
        copy.wait()

    def lay_out(place, carry):
        for slot in range(slots):
            for i in range(edge):
                x[place * slots + slot, i, :square, :] = raw[place, slot, i * square : (i + 1) * square, :]
        return carry

    lax.fori_loop(0, len(parts), lay_out, 0)
    chunks = -(-square // ROWS)

    def per_slot(s, carry):
        @pl.when(table[s, 0] >= 0)
        def _():
            own_scale = scale[s]
            for a in range(3):
                source = [table[s, 1 + 3 * a + k] for k in range(3)]
                for i in range(chunks if a == 0 else edge):
                    if a == 0:
                        rows = slice(i * ROWS, (i + 1) * ROWS)
                        block = jnp.concatenate([x[t, :, rows, :].reshape(edge * ROWS, width) for t in source], axis=0)
                        exact = (own_scale * matmul(fwd_out[...], block)).reshape(edge, ROWS, width)
                        value = exact.astype(bf16)
                        rounded[:, rows, :] = value
                        left_over[:, rows, :] = (value.astype(f32) - exact).astype(bf16)
                    else:
                        block = jnp.concatenate([x[t, i] for t in source], axis=0)
                        exact = own_scale * matmul(fwd_in[a - 1], block)
                        value = exact.astype(bf16)
                        rounded[i] = value
                        left_over[i] = (value.astype(f32) - exact).astype(bf16)
                half = 0.5 * own_scale
                for k in range(3):
                    target = source[k]

                    @pl.when(target < own)
                    def _():
                        for i in range(chunks if a == 0 else edge):
                            for field, sum_ref in ((rounded, total), (left_over, total_fix)):
                                if a == 0:
                                    rows = slice(i * ROWS, (i + 1) * ROWS)
                                    term = matmul(back_out[k], field[:, rows, :].reshape(edge * ROWS, width))
                                    sum_ref[target, :, rows, :] += half * term.reshape(edge, ROWS, width)
                                else:
                                    sum_ref[target, i] += half * matmul(back_in[a - 1, k], field[i])

        return carry

    lax.fori_loop(0, table.shape[0], per_slot, 0)

    def finish(t, carry):
        for i in range(edge):
            rows = slice(i * square, (i + 1) * square)
            exact = pot[t, rows, :] * x[t, i, :square, :].astype(f32)
            lost = exact.astype(bf16).astype(f32) - exact
            whole = total[t, i, :square, :] + exact
            top = whole.astype(bf16)
            low = (whole - top.astype(f32)).astype(bf16)
            fix = (total_fix[t, i, :square, :] + lost).astype(bf16)
            out[t, rows, :] = jnp.concatenate([top, low, fix], axis=1)
        return carry

    lax.fori_loop(0, own, finish, 0)


def block_matrices(deriv_blocks):
    edge = deriv_blocks.shape[1]
    square = edge * edge
    padded = -(-square // ROWS) * ROWS
    ids = np.arange(padded)
    slow = ((ids[:, None] // edge) == np.arange(edge)).astype(np.float32)
    fast = (((ids[:, None] % edge) == np.arange(edge)) & (ids[:, None] < square)).astype(np.float32)
    ids = np.arange(edge * ROWS)
    outer = ((ids[:, None] // ROWS) == np.arange(edge)).astype(np.float32)
    within = ((ids[:, None] % ROWS) == np.arange(ROWS)).astype(np.float32)
    stacked = jnp.moveaxis(deriv_blocks, 0, 1).reshape(edge, 3 * edge)
    forward, backward = [], []
    for spot, mask in ((slow, fast), (fast, slow), (outer, within)):
        same = mask @ mask.T
        spread_out = np.kron(np.eye(3, dtype=np.float32), spot.T)
        spot_b, same_b = jnp.asarray(spot, bf16), jnp.asarray(same, f32)
        wide = matmul(matmul(spot_b, stacked).astype(bf16), jnp.asarray(spread_out, bf16))
        forward.append((wide * jnp.tile(same_b, (1, 3))).astype(bf16))
        turned = jnp.einsum("ri,kji->krj", spot_b, deriv_blocks, preferred_element_type=f32).astype(bf16)
        turned = jnp.einsum("krj,cj->krc", turned, spot_b, preferred_element_type=f32)
        backward.append((turned * same_b).astype(bf16))
    return jnp.stack(forward[:2]), forward[2], jnp.stack(backward[:2]), backward[2]


def kinetic(parts, pot, matrices, table, scale, edge):
    slots, coefficients, width = parts[0].shape
    padded = matrices[0].shape[1]
    own = PAIR * slots
    vmem = pl.BlockSpec(memory_space=pltpu.VMEM)
    smem = pl.BlockSpec(memory_space=pltpu.SMEM)
    anywhere = pl.BlockSpec(memory_space=pl.ANY)
    return pl.pallas_call(
        functools.partial(kinetic_kernel, edge, slots),
        out_shape=jax.ShapeDtypeStruct((own, coefficients, 3 * width), bf16),
        in_specs=[smem, smem] + [anywhere] * 6 + [vmem] * 5,
        out_specs=vmem,
        scratch_shapes=[
            pltpu.VMEM((6, slots, coefficients, width), bf16),
            pltpu.VMEM((6 * slots + 1, edge, padded, width), bf16),
            pltpu.VMEM((edge, padded, width), bf16),
            pltpu.VMEM((edge, padded, width), bf16),
            pltpu.VMEM((own, edge, padded, width), f32),
            pltpu.VMEM((own, edge, padded, width), f32),
            pltpu.SemaphoreType.DMA((6,)),
        ],
        compiler_params=pltpu.CompilerParams(vmem_limit_bytes=48 * 1024 * 1024),
        cost_estimate=pl.CostEstimate(flops=2 * 10**10, bytes_accessed=40 * 10**6, transcendentals=0),
    )(table, scale, *parts, pot, *matrices)


def body(orbitals, potential, deriv_blocks, levels, box_counts, neighbours):
    slots, coefficients, own_width = orbitals.shape
    edge = deriv_blocks.shape[1]
    level, pair, orb = lax.axis_index("lvl"), lax.axis_index("pair"), lax.axis_index("orb")
    level_count, orb_count = lax.axis_size("lvl"), lax.axis_size("orb")
    half = own_width // PAIR
    all_width = own_width * orb_count
    box_rows = all_width // (level_count * PAIR)
    first = pair == 0
    groups = range(orb_count)
    square_grid = level_count == orb_count and orb_count & (orb_count - 1) == 0 and box_rows == half

    live = jnp.arange(slots, dtype=jnp.int32) < box_counts[0]
    active = jnp.where(live[:, None, None], orbitals, jnp.zeros((), bf16))

    mine = jnp.where(first, active[:, :, :half], active[:, :, half:])
    theirs = jnp.where(first, active[:, :, half:], active[:, :, :half])
    facts = jnp.concatenate(
        [neighbours.reshape(slots, 6), levels[:, None], live.astype(jnp.int32)[:, None]], axis=1
    )
    beside = swap(theirs, "pair", 1)
    far = {q: swap(active, "orb", q) for q in groups if q and q % 2 == 0}
    lower, upper = shift(mine, "lvl", 1), shift(mine, "lvl", -1)
    beside_rest = swap(mine, "pair", 1)
    near_active = swap(active, "orb", 1)
    both_facts = jnp.stack([facts, swap(facts, "pair", 1)])
    other_pot = swap(potential, "pair", 1)
    lower_facts, upper_facts = shift(both_facts, "lvl", 1), shift(both_facts, "lvl", -1)
    lower_beside, upper_beside = shift(beside, "lvl", 1), shift(beside, "lvl", -1)

    box_of_level = level * PAIR
    slot_ids = jnp.arange(slots, dtype=jnp.int32)
    ids = jnp.concatenate(
        [
            (box_of_level + pair) * slots + slot_ids,
            (box_of_level + 1 - pair) * slots + slot_ids,
            (box_of_level - 1) * slots + slot_ids,
            (box_of_level + PAIR) * slots + slot_ids,
        ]
    ).astype(jnp.int32)
    there = (ids >= 0) & (ids < level_count * PAIR * slots)
    chosen = jnp.concatenate(
        [
            both_facts[0],
            both_facts[1],
            jnp.where(first, lower_facts[1], lower_facts[0]),
            jnp.where(first, upper_facts[0], upper_facts[1]),
        ]
    )

    def place(slot_id):
        box = slot_id // slots
        apart = box // PAIR - level
        base = jnp.where(apart == 0, 0, jnp.where(apart < 0, 2, 4))
        where = (base + (box % PAIR != pair)) * slots + slot_id % slots
        return jnp.where(slot_id >= 0, where, 6 * slots)

    near = place(chosen[:, :6])
    self_place = place(ids)
    table = [jnp.where(there & (chosen[:, 7] > 0), self_place, -1)]
    for a in range(3):
        table += [near[:, 2 * a], self_place, near[:, 2 * a + 1]]
    table = jnp.stack(table, axis=1).astype(jnp.int32)
    level_of = chosen[:, 6]
    scale = jnp.where(level_of == 0, 0.5, jnp.where(level_of == 1, 1.0, 2.0)).astype(f32)
    pot = jnp.concatenate([potential, other_pot])[:, :, None]
    matrices = block_matrices(deriv_blocks)

    far, beside_rest, lower, upper, near_active, table, scale, pot, matrices = lax.optimization_barrier(
        (far, beside_rest, lower, upper, near_active, table, scale, pot, matrices)
    )
    beside_all = jnp.concatenate(
        [jnp.where(first, beside, beside_rest), jnp.where(first, beside_rest, beside)], axis=2
    )
    cut = slots // 2
    far_beside = {
        q: jnp.concatenate([swap(beside_all[:cut], "orb", q), swap(far[q][cut:], "pair", 1)]) for q in far
    }
    left_own = {0: active, 1: near_active, **far}
    left_beside = {0: beside_all, 1: swap(beside_all, "orb", 1), **far_beside}
    for q in far:
        left_own[q + 1] = swap(far[q], "orb", 1)
        left_beside[q + 1] = swap(far_beside[q], "orb", 1)
    parts = [mine, beside, lower, lower_beside, upper, upper_beside]
    flat = lambda block: block.reshape(slots * coefficients, block.shape[-1])

    def row_blocks(right_own, right_beside):
        return jnp.stack(
            [
                contract(flat(right_own), flat(left_own[q])) + contract(flat(right_beside), flat(left_beside[q]))
                for q in groups
            ]
        )

    def block(blocks, q):
        return lax.dynamic_index_in_dim(blocks, q, keepdims=False)

    def natural(blocks):
        return jnp.concatenate([block(blocks, orb ^ j) for j in groups], axis=1)

    def deliver(blocks, kind):
        if not square_grid:
            strip = lax.psum(natural(blocks), "lvl")
            strip = lax.all_gather(strip, ("orb", "pair"), axis=0, tiled=True)
            strip = lax.dynamic_slice_in_dim(strip, (level * PAIR + pair) * box_rows, box_rows, axis=0)
            return lax.dynamic_slice_in_dim(strip, orb * own_width, own_width, axis=1)
        total = 0.0
        for step in range(level_count):
            to = [
                (z * orb_count + o, o * orb_count + (z ^ step)) for z in range(level_count) for o in groups
            ]
            sent = block(blocks, orb ^ level ^ step).astype(kind)
            total = total + lax.ppermute(sent, ("lvl", "orb"), to).astype(f32)
        return total

    def deliver_turned(blocks):
        sums = []
        for over in range(PAIR):
            total = 0.0
            for step in range(level_count):
                wide = block(blocks, orb ^ level ^ step)
                to_first = (pair ^ over) == 0
                sent = jnp.where(to_first, wide[:, :half], wide[:, half:]).astype(bf16)
                to = [
                    (z * PAIR + y, (z ^ step) * PAIR + (y ^ over)) for z in range(level_count) for y in range(PAIR)
                ]
                if step or over:
                    sent = lax.ppermute(sent, BOX, to)
                total = total + sent.astype(f32)
            sums.append(total.T)
        own, other = sums
        return jnp.concatenate([jnp.where(first, own, other), jnp.where(first, other, own)], axis=1)

    def natural_turned(blocks):
        strip = lax.psum(natural(blocks), "lvl")
        everywhere = lax.all_gather(strip, "pair", axis=0, tiled=True)
        rows = lax.dynamic_slice_in_dim(everywhere, (level * PAIR + pair) * box_rows, box_rows, axis=1)
        return rows.T

    def identity(rows, row0, cols, col0):
        row_ids = row0 + jnp.arange(rows, dtype=jnp.int32)
        col_ids = col0 + jnp.arange(cols, dtype=jnp.int32)
        return (row_ids[:, None] == col_ids[None, :]).astype(f32)

    offset_blocks = row_blocks(mine, beside)
    offset_blocks = offset_blocks.at[0].add(-identity(half, pair * half, own_width, 0) / level_count)
    offset = deliver(offset_blocks, bf16)
    row0, col0 = (level * PAIR + pair) * box_rows, orb * own_width
    eye = identity(box_rows, row0, own_width, col0)
    correlation = offset + eye

    right = kinetic(parts, pot, matrices, table, scale, edge)
    fock_blocks = row_blocks(right[:slots], right[slots:])
    fock = deliver(fock_blocks[:, :half] + fock_blocks[:, half : 2 * half], f32)
    fix = fock_blocks[:, 2 * half :]
    fock = fock + (deliver_turned(fix) if square_grid else natural_turned(fix))

    small = offset.astype(bf16)
    if square_grid:
        levels_of, far_of = range(level_count), range(0, orb_count, 2)
        top, low = small[: box_rows // 2], small[box_rows // 2 :]
        top = spread(spread(spread(spread(top, "lvl", levels_of), "pair", (0, 1)), "orb", far_of), "orb", (0, 1))
        low = spread(spread(spread(spread(low, "orb", far_of), "lvl", levels_of), "pair", (0, 1)), "orb", (0, 1))
        top = jnp.transpose(top, (3, 2, 4, 1, 0, 5))
        low = jnp.transpose(low, (2, 1, 4, 3, 0, 5))
        whole = jnp.stack([top, low], axis=2).reshape(all_width, all_width)
        rows_of, cols_of = whole[:box_rows], whole[:, :own_width]
        apart = level ^ orb

        def to_row_order(strip):
            pieces = []
            for z in levels_of:
                piece = lax.dynamic_slice_in_dim(strip, (apart ^ z) * own_width, own_width, axis=1)
                turned = jnp.concatenate([piece[:, half:], piece[:, :half]], axis=1)
                pieces.append(jnp.where(first, piece, turned))
            return jnp.concatenate(pieces, axis=1)

        def to_col_order(strip):
            pieces = []
            for q in groups:
                piece = lax.dynamic_slice_in_dim(strip, (apart ^ q) * own_width, own_width, axis=0)
                turned = jnp.concatenate([piece[half:], piece[:half]], axis=0)
                pieces.append(jnp.where(first, piece, turned))
            return jnp.concatenate(pieces, axis=0)

        own_square_at = lambda strip: strip[:, :own_width]
    else:
        gathered = lax.all_gather(small, "orb", axis=1, tiled=True)
        whole = lax.all_gather(gathered, BOX, axis=0, tiled=True)
        rows_of = lax.dynamic_slice_in_dim(whole, row0, box_rows, axis=0)
        cols_of = lax.dynamic_slice_in_dim(whole, col0, own_width, axis=1)
        to_row_order = to_col_order = lambda strip: strip
        own_square_at = lambda strip: lax.dynamic_slice_in_dim(strip, col0, own_width, axis=1)
    row_square = matmul(to_row_order(rows_of), whole)
    col_square = matmul(whole, to_col_order(cols_of))
    left = to_row_order((rows_of.astype(f32) - 0.25 * row_square).astype(bf16))
    right_side = (0.25 * (cols_of.astype(f32) - col_square)).astype(bf16)
    inverse_root = eye - 0.5 * offset + 0.125 * own_square_at(row_square) + matmul(left, right_side)
    return fock, correlation, inverse_root


def solution(mesh):
    levels = mesh.shape["box"] // PAIR
    split = Mesh(mesh.devices.reshape(levels, PAIR, mesh.shape["orb"]), ("lvl", "pair", "orb"))
    in_specs = (P(BOX, None, "orb"), P(BOX, None), P(), P(BOX), P(BOX), P(BOX, None, None))
    out_specs = (P(BOX, "orb"),) * 3
    return jax.shard_map(body, mesh=split, in_specs=in_specs, out_specs=out_specs, check_vma=False)
```

profile of v0, /device:TPU:24, one launch (start us, length us, event | category | flops | bytes accessed | tf_op | source)
XLA Modules:
  0.0 352.1 jit_solution(11402044507622013950)
XLA Ops:
  1.3 2.8 broadcast_select_fusion
  12.7 2.8 convolution_bitcast_fusion.15
  21.5 6.6 %collective-permute-done.5 = s32[2,8]{1,0:T(2,128)S(1)} collective-permute-done((s32[2,8]{1,0:T(2,128)S(1)}, s32[2,8]{1,0:T(2,128)S(1)}, u32[]{:S(2)}, u32[]{:S(2)}) %collective-permute-start.5) | collective-permute-done | bytes 96 | tf_op jit(solution)/shard_map/ppermute | solution.py:19
  28.1 2.3 collective-permute-start.7
  33.1 4.4 %collective-permute-done.6 = s32[2,2,8]{2,1,0:T(2,128)S(1)} collective-permute-done((s32[2,2,8]{2,1,0:T(2,128)S(1)}, s32[2,2,8]{2,1,0:T(2,128)S(1)}, u32[]{:S(2)}, u32[]{:S(2)}) %collective-permute-start.6) | collective-permute-done | bytes 160 | tf_op jit(solution)/shard_map/ppermute | solution.py:24
  39.1 2.1 collective-permute-done.8
  42.7 4.0 %collective-permute-start.3 = (bf16[2,1000,192]{1,2,0:T(8,128)(2,1)}, bf16[2,1000,192]{1,2,0:T(8,128)(2,1)S(1)}, u32[]{:S(2)}, u32[]{:S(2)}) collective-permute-start(bf16[2,1000,192]{1,2,0:T(8,128)(2,1)} %copy.115), channel_id=1, source_target_pairs={{8,0},{16,8},{24,16},{9,1},{17,9},{25,17},{10,2},{18,10},{26,18},{... | collective-permute-start | bytes 2304008 | tf_op jit(solution)/shard_map/ppermute | solution.py:24
  47.0 10.5 %collective-permute-done.9 = bf16[2,1000,192]{1,2,0:T(8,128)(2,1)} collective-permute-done((bf16[2,1000,192]{1,2,0:T(8,128)(2,1)S(1)}, bf16[2,1000,192]{1,2,0:T(8,128)(2,1)}, u32[]{:S(2)}, u32[]{:S(2)}) %collective-permute-start.9) | collective-permute-done | bytes 768032 | tf_op jit(solution)/shard_map/ppermute | solution.py:19
  58.8 5.6 %collective-permute-start.11 = (bf16[2,1000,192]{1,2,0:T(8,128)(2,1)}, bf16[2,1000,192]{1,2,0:T(8,128)(2,1)}, u32[]{:S(2)}, u32[]{:S(2)}) collective-permute-start(bf16[2,1000,192]{1,2,0:T(8,128)(2,1)} %collective-permute-done.9), channel_id=1, source_target_pairs={{8,0},{16,8},{24,16},{9,1},{17,9},{25,17},{10,2},{18,10},{26,18},{... | collective-permute-start | bytes 2304008 | tf_op jit(solution)/shard_map/ppermute | solution.py:24
  66.2 2.4 slice.221
  70.0 2.2 copy.139.refs_4_
  74.2 2.2 copy.144
  82.8 2.2 copy.138.refs_3_
  85.0 2.2 copy.140.refs_5_
  91.5 27.7 %shard_map.166 = bf16[4,1000,576]{2,1,0:T(8,128)(2,1)} custom-call(s32[8,10]{1,0:T(8,128)S(1)} %stack.161.table, f32[8]{0:T(128)S(1)} %select_reduce_fusion.scale, bf16[2,1000,192]{2,1,0:T(8,128)(2,1)S(1)} %get-tuple-element.49.refs_0_, bf16[2,1000,192]{2,1,0:T(8,128)(2,1)S(1)} %copy.136.refs_1_, bf16[2,1000,192]{2,1,0:T(8,128)(2,1)S(1)} %copy.137.refs_2_, ...), custom_call_target="tpu_custom_call" | custom-call | flops 20000000000 | bytes 40000000 | tf_op jit(solution)/shard_map/pallas_call | solution.py:148
  119.3 3.7 %convolution_bitcast_fusion.6 = f32[576,384]{1,0:T(8,128)S(1)} fusion(bf16[4,1000,576]{2,1,0:T(8,128)(2,1)} %shard_map.166, bf16[2,1000,384]{2,1,0:T(8,128)(2,1)} %pad_maximum_fusion.2), kind=kOutput, calls=%fused_computation.17 | convolution fusion | flops 884736000 | bytes 7028736 | tf_op jit(solution)/shard_map/dot_general | solution.py:28
  123.0 2.2 fusion.19
  125.2 2.8 fusion.3
  134.3 2.8 fusion.7
  139.1 2.2 convolution_bitcast_fusion.12
  141.3 2.7 fusion.21
  144.0 2.8 convolution_bitcast_fusion.4
  146.8 2.8 fusion.5
  151.1 3.1 fusion.9
  161.4 2.9 collective-permute-start.27
  172.7 3.6 %collective-permute-start.30 = (bf16[192,384]{1,0:T(8,128)(2,1)S(1)}, bf16[192,384]{1,0:T(8,128)(2,1)S(1)}, u32[]{:S(2)}, u32[]{:S(2)}) collective-permute-start(bf16[192,384]{1,0:T(8,128)(2,1)S(1)} %get-tuple-element.102), channel_id=1, source_target_pairs={{0,2},{1,10},{2,18},{3,26},{8,3},{9,11},{10,19},{11,27},{16,0},{17... | collective-permute-start | bytes 442376 | tf_op jit(solution)/shard_map/ppermute | solution.py:279
  176.3 2.2 collective-permute-start.29
  178.5 3.5 collective-permute-start.28
  183.7 14.3 %collective-permute-done.29 = bf16[192,384]{1,0:T(8,128)(2,1)S(1)} collective-permute-done((bf16[192,384]{1,0:T(8,128)(2,1)S(1)}, bf16[192,384]{1,0:T(8,128)(2,1)S(1)}, u32[]{:S(2)}, u32[]{:S(2)}) %collective-permute-start.29) | collective-permute-done | bytes 147488 | tf_op jit(solution)/shard_map/ppermute | solution.py:279
  199.3 6.9 %collective-permute-start.34 = (bf16[96,384]{1,0:T(8,128)(2,1)S(1)}, bf16[96,384]{1,0:T(8,128)(2,1)S(1)}, u32[]{:S(2)}, u32[]{:S(2)}) collective-permute-start(bf16[96,384]{1,0:T(8,128)(2,1)S(1)} %get-tuple-element.119), channel_id=1, source_target_pairs={{0,24},{8,16},{16,8},{24,0},{1,25},{9,17},{17,9},{25,1},{2,26},{10... | collective-permute-start | bytes 221192 | tf_op jit(solution)/shard_map/ppermute | solution.py:19
  206.8 3.8 %collective-permute-start.41 = (bf16[2,96,384]{2,1,0:T(8,128)(2,1)S(1)}, bf16[2,96,384]{2,1,0:T(8,128)(2,1)S(1)}, u32[]{:S(2)}, u32[]{:S(2)}) collective-permute-start(bf16[2,96,384]{2,1,0:T(8,128)(2,1)S(1)} %get-tuple-element.121), channel_id=1, source_target_pairs={{0,24},{8,16},{16,8},{24,0},{1,25},{9,17},{17,9},{25,1},{2,26},{10... | collective-permute-start | bytes 442376 | tf_op jit(solution)/shard_map/ppermute | solution.py:19
  210.6 3.7 %collective-permute-start.40 = (bf16[2,96,384]{2,1,0:T(8,128)(2,1)S(1)}, bf16[2,96,384]{2,1,0:T(8,128)(2,1)S(1)}, u32[]{:S(2)}, u32[]{:S(2)}) collective-permute-start(bf16[2,96,384]{2,1,0:T(8,128)(2,1)S(1)} %get-tuple-element.121), channel_id=1, source_target_pairs={{0,16},{8,24},{16,0},{24,8},{1,17},{9,25},{17,1},{25,9},{2,18},{10... | collective-permute-start | bytes 442376 | tf_op jit(solution)/shard_map/ppermute | solution.py:19
  214.4 3.4 collective-permute-done.33
  220.1 4.2 %collective-permute-start.26 = (bf16[192,192]{0,1:T(8,128)(2,1)}, bf16[192,192]{0,1:T(8,128)(2,1)S(1)}, u32[]{:S(2)}, u32[]{:S(2)}) collective-permute-start(bf16[192,192]{0,1:T(8,128)(2,1)} %get-tuple-element.113), channel_id=1, source_target_pairs={{0,20},{4,16},{8,28},{12,24},{16,4},{20,0},{24,12},{28,8},{1,21},{... | collective-permute-start | bytes 221192 | tf_op jit(solution)/shard_map/ppermute | solution.py:294
  224.3 2.4 collective-permute-done.40
  232.7 10.4 %collective-permute-done.42 = bf16[4,2,96,384]{3,2,1,0:T(8,128)(2,1)S(1)} collective-permute-done((bf16[4,2,96,384]{3,2,1,0:T(8,128)(2,1)S(1)}, bf16[4,2,96,384]{3,2,1,0:T(8,128)(2,1)S(1)}, u32[]{:S(2)}, u32[]{:S(2)}) %collective-permute-start.42) | collective-permute-done | bytes 589856 | tf_op jit(solution)/shard_map/ppermute | solution.py:19
  243.1 2.1 collective-permute-start.20
  246.5 2.3 fusion.98
  254.1 2.2 collective-permute-start.22
  257.3 6.4 %collective-permute-start.21 = (bf16[192,192]{0,1:T(8,128)(2,1)S(1)}, bf16[192,192]{0,1:T(8,128)(2,1)S(1)}, u32[]{:S(2)}, u32[]{:S(2)}) collective-permute-start(bf16[192,192]{0,1:T(8,128)(2,1)S(1)} %copy-done.27), channel_id=1, source_target_pairs={{0,8},{4,12},{8,0},{12,4},{16,24},{20,28},{24,16},{28,20},{1,9},{5... | collective-permute-start | bytes 221192 | tf_op jit(solution)/shard_map/ppermute | solution.py:294
  266.7 7.7 %collective-permute-start.17 = (f32[192,384]{1,0:T(8,128)}, f32[192,384]{1,0:T(8,128)S(1)}, u32[]{:S(2)}, u32[]{:S(2)}) collective-permute-start(f32[192,384]{1,0:T(8,128)} %get-tuple-element.69), channel_id=1, source_target_pairs={{0,0},{1,8},{2,16},{3,24},{8,1},{9,9},{10,17},{11,25},{16,2},{17,1... | collective-permute-start | bytes 884744 | tf_op jit(solution)/shard_map/ppermute | solution.py:279
  274.5 6.2 %collective-permute-start.18 = (f32[192,384]{1,0:T(8,128)}, f32[192,384]{1,0:T(8,128)S(1)}, u32[]{:S(2)}, u32[]{:S(2)}) collective-permute-start(f32[192,384]{1,0:T(8,128)} %get-tuple-element.66), channel_id=1, source_target_pairs={{0,1},{1,9},{2,17},{3,25},{8,0},{9,8},{10,16},{11,24},{16,3},{17,1... | collective-permute-start | bytes 884744 | tf_op jit(solution)/shard_map/ppermute | solution.py:279
  282.8 25.5 %collective-permute-done.18 = f32[192,384]{1,0:T(8,128)S(1)} collective-permute-done((f32[192,384]{1,0:T(8,128)}, f32[192,384]{1,0:T(8,128)S(1)}, u32[]{:S(2)}, u32[]{:S(2)}) %collective-permute-start.18) | collective-permute-done | bytes 294944 | tf_op jit(solution)/shard_map/ppermute | solution.py:279
  313.2 2.7 pad_maximum_fusion
  315.9 9.4 %copy.167 = bf16[4,2,2,96,2,2,384]{6,5,4,3,2,1,0:T(2,128)(2,1)} copy(bf16[4,2,2,96,2,2,384]{6,3,4,0,1,5,2:T(8,128)(2,1)} %pad_maximum_fusion) | data formatting | bytes 9437184 | tf_op jit(solution)/shard_map/stack | solution.py:332
  325.3 11.4 %reshape.519 = bf16[1536,1536]{1,0:T(8,128)(2,1)} reshape(bf16[4,2,2,96,2,2,384]{6,5,4,3,2,1,0:T(2,128)(2,1)} %copy.167) | data formatting | bytes 9437184 | tf_op jit(solution)/shard_map/reshape | solution.py:332
  341.6 2.1 subtract_convert_fusion
  345.5 6.4 %fusion.57 = f32[192,384]{1,0:T(8,128)} fusion(f32[192,1536]{1,0:T(8,128)} %get-tuple-element.135, s32[384]{0:T(512)S(1)} %iota_add_fusion, s32[192]{0:T(256)S(1)} %iota_add_fusion.1, bf16[1536,1536]{1,0:T(8,128)(2,1)} %reshape.519, bf16[384,384]{1,0:T(8,128)(2,1)S(1)} %get-tuple-element.51, bf16[384,384]{1,0:T(8,128)(2,1)S(1)} %get-tuple-element.52, ...), kind=kOutput, calls=%fused_computation.105 | convolution fusion | flops 2048901120 | bytes 8849664 | tf_op jit(solution)/shard_map/dot_general | solution.py:32
  (252 shorter events, 98.4 us)
Async XLA Ops:
  4.1 62.0 %collective-permute-start = (bf16[2,1000,384]{2,1,0:T(8,128)(2,1)}, bf16[2,1000,384]{2,1,0:T(8,128)(2,1)}, u32[]{:S(2)}, u32[]{:S(2)}) collective-permute-start(bf16[2,1000,384]{2,1,0:T(8,128)(2,1)} %broadcast_select_fusion), channel_id=1, source_target_pairs={{0,2},{1,3},{2,0},{3,1},{4,6},{5,7},{6,4},{7,5},{8,10},{9,11},{10,... | collective-permute-start | bytes 4608008 | tf_op jit(solution)/shard_map/ppermute | solution.py:19
  8.8 33.9 %collective-permute-start.1 = (bf16[2,1000,192]{1,2,0:T(8,128)(2,1)}, bf16[2,1000,192]{1,2,0:T(8,128)(2,1)}, u32[]{:S(2)}, u32[]{:S(2)}) collective-permute-start(bf16[2,1000,192]{1,2,0:T(8,128)(2,1)} %copy.115), channel_id=1, source_target_pairs={{0,4},{4,0},{1,5},{5,1},{2,6},{6,2},{3,7},{7,3},{8,12},{12,8},{9,1... | collective-permute-start | bytes 2304008 | tf_op jit(solution)/shard_map/ppermute | solution.py:19
  10.3 48.5 %collective-permute-start.2 = (bf16[2,1000,192]{1,2,0:T(8,128)(2,1)}, bf16[2,1000,192]{1,2,0:T(8,128)(2,1)}, u32[]{:S(2)}, u32[]{:S(2)}) collective-permute-start(bf16[2,1000,192]{1,2,0:T(8,128)(2,1)} %copy.115), channel_id=1, source_target_pairs={{0,8},{8,16},{16,24},{1,9},{9,17},{17,25},{2,10},{10,18},{18,26},{... | collective-permute-start | bytes 2304008 | tf_op jit(solution)/shard_map/ppermute | solution.py:24
  11.6 54.5 %collective-permute-start.4 = (bf16[2,1000,384]{2,1,0:T(8,128)(2,1)}, bf16[2,1000,384]{2,1,0:T(8,128)(2,1)}, u32[]{:S(2)}, u32[]{:S(2)}) collective-permute-start(bf16[2,1000,384]{2,1,0:T(8,128)(2,1)} %broadcast_select_fusion), channel_id=1, source_target_pairs={{0,1},{1,0},{2,3},{3,2},{4,5},{5,4},{6,7},{7,6},{8,9},{9,8},{10,11... | collective-permute-start | bytes 4608008 | tf_op jit(solution)/shard_map/ppermute | solution.py:19
  12.1 16.1 %collective-permute-start.5 = (s32[2,8]{1,0:T(2,128)S(1)}, s32[2,8]{1,0:T(2,128)S(1)}, u32[]{:S(2)}, u32[]{:S(2)}) collective-permute-start(s32[2,8]{1,0:T(2,128)S(1)} %pad_add_fusion.2), channel_id=1, source_target_pairs={{0,4},{4,0},{1,5},{5,1},{2,6},{6,2},{3,7},{7,3},{8,12},{12,8},{9,1... | collective-permute-start | bytes 200 | tf_op jit(solution)/shard_map/ppermute | solution.py:19
  17.6 23.6 %copy-start.9 = (bf16[2,1000,192]{1,2,0:T(8,128)(2,1)S(1)}, bf16[2,1000,192]{1,2,0:T(8,128)(2,1)}, u32[]{:S(2)}) copy-start(bf16[2,1000,192]{1,2,0:T(8,128)(2,1)} %copy.135) | copy-start | bytes 2304004
  28.1 3.6 %collective-permute-start.7 = (s32[2,2,8]{2,1,0:T(2,128)S(1)}, s32[2,2,8]{2,1,0:T(2,128)S(1)}, u32[]{:S(2)}, u32[]{:S(2)}) collective-permute-start(s32[2,2,8]{2,1,0:T(2,128)S(1)} %pad_add_fusion.1), channel_id=1, source_target_pairs={{8,0},{16,8},{24,16},{9,1},{17,9},{25,17},{10,2},{18,10},{26,18},{... | collective-permute-start | bytes 392 | tf_op jit(solution)/shard_map/ppermute | solution.py:24
  31.8 5.7 %collective-permute-start.6 = (s32[2,2,8]{2,1,0:T(2,128)S(1)}, s32[2,2,8]{2,1,0:T(2,128)S(1)}, u32[]{:S(2)}, u32[]{:S(2)}) collective-permute-start(s32[2,2,8]{2,1,0:T(2,128)S(1)} %pad_add_fusion.1), channel_id=1, source_target_pairs={{0,8},{8,16},{16,24},{1,9},{9,17},{17,25},{2,10},{10,18},{18,26},{... | collective-permute-start | bytes 392 | tf_op jit(solution)/shard_map/ppermute | solution.py:24
  37.5 3.7 %collective-permute-start.8 = (f32[2,1000]{1,0:T(2,128)S(1)}, f32[2,1000]{1,0:T(2,128)S(1)}, u32[]{:S(2)}, u32[]{:S(2)}) collective-permute-start(f32[2,1000]{1,0:T(2,128)S(1)} %copy-done.39), channel_id=1, source_target_pairs={{0,4},{4,0},{1,5},{5,1},{2,6},{6,2},{3,7},{7,3},{8,12},{12,8},{9,1... | collective-permute-start | bytes 24008 | tf_op jit(solution)/shard_map/ppermute | solution.py:19
  41.2 16.3 %collective-permute-start.9 = (bf16[2,1000,192]{1,2,0:T(8,128)(2,1)S(1)}, bf16[2,1000,192]{1,2,0:T(8,128)(2,1)}, u32[]{:S(2)}, u32[]{:S(2)}) collective-permute-start(bf16[2,1000,192]{1,2,0:T(8,128)(2,1)S(1)} %copy-done.9), channel_id=1, source_target_pairs={{0,4},{4,0},{1,5},{5,1},{2,6},{6,2},{3,7},{7,3},{8,12},{12,8},{9,1... | collective-permute-start | bytes 2304008 | tf_op jit(solution)/shard_map/ppermute | solution.py:19
  42.7 23.4 %collective-permute-start.3 = (bf16[2,1000,192]{1,2,0:T(8,128)(2,1)}, bf16[2,1000,192]{1,2,0:T(8,128)(2,1)S(1)}, u32[]{:S(2)}, u32[]{:S(2)}) collective-permute-start(bf16[2,1000,192]{1,2,0:T(8,128)(2,1)} %copy.115), channel_id=1, source_target_pairs={{8,0},{16,8},{24,16},{9,1},{17,9},{25,17},{10,2},{18,10},{26,18},{... | collective-permute-start | bytes 2304008 | tf_op jit(solution)/shard_map/ppermute | solution.py:24
  57.5 25.3 %collective-permute-start.10 = (bf16[2,1000,192]{1,2,0:T(8,128)(2,1)}, bf16[2,1000,192]{1,2,0:T(8,128)(2,1)}, u32[]{:S(2)}, u32[]{:S(2)}) collective-permute-start(bf16[2,1000,192]{1,2,0:T(8,128)(2,1)} %collective-permute-done.9), channel_id=1, source_target_pairs={{0,8},{8,16},{16,24},{1,9},{9,17},{17,25},{2,10},{10,18},{18,26},{... | collective-permute-start | bytes 2304008 | tf_op jit(solution)/shard_map/ppermute | solution.py:24
  58.8 26.3 %collective-permute-start.11 = (bf16[2,1000,192]{1,2,0:T(8,128)(2,1)}, bf16[2,1000,192]{1,2,0:T(8,128)(2,1)}, u32[]{:S(2)}, u32[]{:S(2)}) collective-permute-start(bf16[2,1000,192]{1,2,0:T(8,128)(2,1)} %collective-permute-done.9), channel_id=1, source_target_pairs={{8,0},{16,8},{24,16},{9,1},{17,9},{25,17},{10,2},{18,10},{26,18},{... | collective-permute-start | bytes 2304008 | tf_op jit(solution)/shard_map/ppermute | solution.py:24
  68.5 82.5 %collective-permute-start.15 = (bf16[2,1000,384]{2,1,0:T(8,128)(2,1)}, bf16[2,1000,384]{2,1,0:T(8,128)(2,1)}, u32[]{:S(2)}, u32[]{:S(2)}) collective-permute-start(bf16[2,1000,384]{2,1,0:T(8,128)(2,1)} %collective-permute-done), channel_id=1, source_target_pairs={{0,1},{1,0},{2,3},{3,2},{4,5},{5,4},{6,7},{7,6},{8,9},{9,8},{10,11... | collective-permute-start | bytes 4608008 | tf_op jit(solution)/shard_map/ppermute | solution.py:19
  79.0 49.1 %collective-permute-start.13 = (bf16[1,1000,384]{2,1,0:T(8,128)(2,1)}, bf16[1,1000,384]{2,1,0:T(8,128)(2,1)}, u32[]{:S(2)}, u32[]{:S(2)}) collective-permute-start(bf16[1,1000,384]{2,1,0:T(8,128)(2,1)} %fusion.40), channel_id=1, source_target_pairs={{0,2},{1,3},{2,0},{3,1},{4,6},{5,7},{6,4},{7,5},{8,10},{9,11},{10,... | collective-permute-start | bytes 2304008 | tf_op jit(solution)/shard_map/ppermute | solution.py:19
  79.5 49.7 %collective-permute-start.14 = (bf16[1,1000,384]{2,1,0:T(8,128)(2,1)}, bf16[1,1000,384]{2,1,0:T(8,128)(2,1)}, u32[]{:S(2)}, u32[]{:S(2)}) collective-permute-start(bf16[1,1000,384]{2,1,0:T(8,128)(2,1)} %slice.221), channel_id=1, source_target_pairs={{0,4},{4,0},{1,5},{5,1},{2,6},{6,2},{3,7},{7,3},{8,12},{12,8},{9,1... | collective-permute-start | bytes 2304008 | tf_op jit(solution)/shard_map/ppermute | solution.py:19
  82.8 56.3 %collective-permute-start.12 = (bf16[2,1000,384]{2,1,0:T(8,128)(2,1)}, bf16[2,1000,384]{2,1,0:T(8,128)(2,1)}, u32[]{:S(2)}, u32[]{:S(2)}) collective-permute-start(bf16[2,1000,384]{2,1,0:T(8,128)(2,1)} %pad_maximum_fusion.2), channel_id=1, source_target_pairs={{0,1},{1,0},{2,3},{3,2},{4,5},{5,4},{6,7},{7,6},{8,9},{9,8},{10,11... | collective-permute-start | bytes 4608008 | tf_op jit(solution)/shard_map/ppermute | solution.py:19
  130.6 19.1 %collective-permute-start.16 = (bf16[2,1000,384]{2,1,0:T(8,128)(2,1)S(1)}, bf16[2,1000,384]{2,1,0:T(8,128)(2,1)S(1)}, u32[]{:S(2)}, u32[]{:S(2)}) collective-permute-start(bf16[2,1000,384]{2,1,0:T(8,128)(2,1)S(1)} %constant_dynamic-update-slice_fusion), channel_id=1, source_target_pairs={{0,1},{1,0},{2,3},{3,2},{4,5},{5,4},{6,7},{7,6},{8,9},{9,8},{10,11... | collective-permute-start | bytes 4608008 | tf_op jit(solution)/shard_map/ppermute | solution.py:19
  161.4 87.5 %collective-permute-start.27 = (bf16[192,192]{0,1:T(8,128)(2,1)}, bf16[192,192]{0,1:T(8,128)(2,1)}, u32[]{:S(2)}, u32[]{:S(2)}) collective-permute-start(bf16[192,192]{0,1:T(8,128)(2,1)} %get-tuple-element.115), channel_id=1, source_target_pairs={{0,28},{4,24},{8,20},{12,16},{16,12},{20,8},{24,4},{28,0},{1,29},{... | collective-permute-start | bytes 221192 | tf_op jit(solution)/shard_map/ppermute | solution.py:294
  171.8 10.9 %collective-permute-start.31 = (bf16[192,384]{1,0:T(8,128)(2,1)S(1)}, bf16[192,384]{1,0:T(8,128)(2,1)S(1)}, u32[]{:S(2)}, u32[]{:S(2)}) collective-permute-start(bf16[192,384]{1,0:T(8,128)(2,1)S(1)} %get-tuple-element.101), channel_id=1, source_target_pairs={{0,3},{1,11},{2,19},{3,27},{8,2},{9,10},{10,18},{11,26},{16,1},{17... | collective-permute-start | bytes 442376 | tf_op jit(solution)/shard_map/ppermute | solution.py:279
  172.7 11.0 %collective-permute-start.30 = (bf16[192,384]{1,0:T(8,128)(2,1)S(1)}, bf16[192,384]{1,0:T(8,128)(2,1)S(1)}, u32[]{:S(2)}, u32[]{:S(2)}) collective-permute-start(bf16[192,384]{1,0:T(8,128)(2,1)S(1)} %get-tuple-element.102), channel_id=1, source_target_pairs={{0,2},{1,10},{2,18},{3,26},{8,3},{9,11},{10,19},{11,27},{16,0},{17... | collective-permute-start | bytes 442376 | tf_op jit(solution)/shard_map/ppermute | solution.py:279
  176.3 21.7 %collective-permute-start.29 = (bf16[192,384]{1,0:T(8,128)(2,1)S(1)}, bf16[192,384]{1,0:T(8,128)(2,1)S(1)}, u32[]{:S(2)}, u32[]{:S(2)}) collective-permute-start(bf16[192,384]{1,0:T(8,128)(2,1)S(1)} %get-tuple-element.103), channel_id=1, source_target_pairs={{0,1},{1,9},{2,17},{3,25},{8,0},{9,8},{10,16},{11,24},{16,3},{17,1... | collective-permute-start | bytes 442376 | tf_op jit(solution)/shard_map/ppermute | solution.py:279
  178.5 19.5 %collective-permute-start.28 = (bf16[192,384]{1,0:T(8,128)(2,1)S(1)}, bf16[192,384]{1,0:T(8,128)(2,1)S(1)}, u32[]{:S(2)}, u32[]{:S(2)}) collective-permute-start(bf16[192,384]{1,0:T(8,128)(2,1)S(1)} %get-tuple-element.100), channel_id=1, source_target_pairs={{0,0},{1,8},{2,16},{3,24},{8,1},{9,9},{10,17},{11,25},{16,2},{17,1... | collective-permute-start | bytes 442376 | tf_op jit(solution)/shard_map/ppermute | solution.py:279
  182.7 35.1 %copy-start.17 = (bf16[192,384]{1,0:T(8,128)(2,1)}, bf16[192,384]{1,0:T(8,128)(2,1)S(1)}, u32[]{:S(2)}) copy-start(bf16[192,384]{1,0:T(8,128)(2,1)S(1)} %collective-permute-done.31) | copy-start | bytes 442372
  183.7 34.1 %copy-start.19 = (bf16[192,384]{1,0:T(8,128)(2,1)}, bf16[192,384]{1,0:T(8,128)(2,1)S(1)}, u32[]{:S(2)}) copy-start(bf16[192,384]{1,0:T(8,128)(2,1)S(1)} %collective-permute-done.30) | copy-start | bytes 442372
  198.9 7.9 %collective-permute-start.38 = (bf16[96,384]{1,0:T(8,128)(2,1)S(1)}, bf16[96,384]{1,0:T(8,128)(2,1)S(1)}, u32[]{:S(2)}, u32[]{:S(2)}) collective-permute-start(bf16[96,384]{1,0:T(8,128)(2,1)S(1)} %get-tuple-element.118), channel_id=1, source_target_pairs={{0,2},{1,3},{2,0},{3,1},{4,6},{5,7},{6,4},{7,5},{8,10},{9,11},{10,... | collective-permute-start | bytes 221192 | tf_op jit(solution)/shard_map/ppermute | solution.py:19
  199.3 11.4 %collective-permute-start.34 = (bf16[96,384]{1,0:T(8,128)(2,1)S(1)}, bf16[96,384]{1,0:T(8,128)(2,1)S(1)}, u32[]{:S(2)}, u32[]{:S(2)}) collective-permute-start(bf16[96,384]{1,0:T(8,128)(2,1)S(1)} %get-tuple-element.119), channel_id=1, source_target_pairs={{0,24},{8,16},{16,8},{24,0},{1,25},{9,17},{17,9},{25,1},{2,26},{10... | collective-permute-start | bytes 221192 | tf_op jit(solution)/shard_map/ppermute | solution.py:19
  206.1 11.6 %collective-permute-start.33 = (bf16[96,384]{1,0:T(8,128)(2,1)S(1)}, bf16[96,384]{1,0:T(8,128)(2,1)S(1)}, u32[]{:S(2)}, u32[]{:S(2)}) collective-permute-start(bf16[96,384]{1,0:T(8,128)(2,1)S(1)} %get-tuple-element.119), channel_id=1, source_target_pairs={{0,16},{8,24},{16,0},{24,8},{1,17},{9,25},{17,1},{25,9},{2,18},{10... | collective-permute-start | bytes 221192 | tf_op jit(solution)/shard_map/ppermute | solution.py:19
  206.2 11.6 %collective-permute-start.32 = (bf16[96,384]{1,0:T(8,128)(2,1)S(1)}, bf16[96,384]{1,0:T(8,128)(2,1)S(1)}, u32[]{:S(2)}, u32[]{:S(2)}) collective-permute-start(bf16[96,384]{1,0:T(8,128)(2,1)S(1)} %get-tuple-element.119), channel_id=1, source_target_pairs={{0,8},{8,0},{16,24},{24,16},{1,9},{9,1},{17,25},{25,17},{2,10},{10... | collective-permute-start | bytes 221192 | tf_op jit(solution)/shard_map/ppermute | solution.py:19
  206.8 13.3 %collective-permute-start.41 = (bf16[2,96,384]{2,1,0:T(8,128)(2,1)S(1)}, bf16[2,96,384]{2,1,0:T(8,128)(2,1)S(1)}, u32[]{:S(2)}, u32[]{:S(2)}) collective-permute-start(bf16[2,96,384]{2,1,0:T(8,128)(2,1)S(1)} %get-tuple-element.121), channel_id=1, source_target_pairs={{0,24},{8,16},{16,8},{24,0},{1,25},{9,17},{17,9},{25,1},{2,26},{10... | collective-permute-start | bytes 442376 | tf_op jit(solution)/shard_map/ppermute | solution.py:19
  210.6 16.1 %collective-permute-start.40 = (bf16[2,96,384]{2,1,0:T(8,128)(2,1)S(1)}, bf16[2,96,384]{2,1,0:T(8,128)(2,1)S(1)}, u32[]{:S(2)}, u32[]{:S(2)}) collective-permute-start(bf16[2,96,384]{2,1,0:T(8,128)(2,1)S(1)} %get-tuple-element.121), channel_id=1, source_target_pairs={{0,16},{8,24},{16,0},{24,8},{1,17},{9,25},{17,1},{25,9},{2,18},{10... | collective-permute-start | bytes 442376 | tf_op jit(solution)/shard_map/ppermute | solution.py:19
  217.8 9.0 %collective-permute-start.39 = (bf16[2,96,384]{2,1,0:T(8,128)(2,1)S(1)}, bf16[2,96,384]{2,1,0:T(8,128)(2,1)S(1)}, u32[]{:S(2)}, u32[]{:S(2)}) collective-permute-start(bf16[2,96,384]{2,1,0:T(8,128)(2,1)S(1)} %get-tuple-element.121), channel_id=1, source_target_pairs={{0,8},{8,0},{16,24},{24,16},{1,9},{9,1},{17,25},{25,17},{2,10},{10... | collective-permute-start | bytes 442376 | tf_op jit(solution)/shard_map/ppermute | solution.py:19
  217.9 10.6 %collective-permute-start.35 = (bf16[4,96,384]{2,1,0:T(8,128)(2,1)S(1)}, bf16[4,96,384]{2,1,0:T(8,128)(2,1)S(1)}, u32[]{:S(2)}, u32[]{:S(2)}) collective-permute-start(bf16[4,96,384]{2,1,0:T(8,128)(2,1)S(1)} %get-tuple-element.109), channel_id=1, source_target_pairs={{0,4},{4,0},{1,5},{5,1},{2,6},{6,2},{3,7},{7,3},{8,12},{12,8},{9,1... | collective-permute-start | bytes 884744 | tf_op jit(solution)/shard_map/ppermute | solution.py:19
  220.1 29.2 %collective-permute-start.26 = (bf16[192,192]{0,1:T(8,128)(2,1)}, bf16[192,192]{0,1:T(8,128)(2,1)S(1)}, u32[]{:S(2)}, u32[]{:S(2)}) collective-permute-start(bf16[192,192]{0,1:T(8,128)(2,1)} %get-tuple-element.113), channel_id=1, source_target_pairs={{0,20},{4,16},{8,28},{12,24},{16,4},{20,0},{24,12},{28,8},{1,21},{... | collective-permute-start | bytes 221192 | tf_op jit(solution)/shard_map/ppermute | solution.py:294
  226.8 23.5 %collective-permute-start.25 = (bf16[192,192]{0,1:T(8,128)(2,1)}, bf16[192,192]{0,1:T(8,128)(2,1)S(1)}, u32[]{:S(2)}, u32[]{:S(2)}) collective-permute-start(bf16[192,192]{0,1:T(8,128)(2,1)} %get-tuple-element.111), channel_id=1, source_target_pairs={{0,12},{4,8},{8,4},{12,0},{16,28},{20,24},{24,20},{28,16},{1,13},{... | collective-permute-start | bytes 221192 | tf_op jit(solution)/shard_map/ppermute | solution.py:294
  226.9 16.2 %collective-permute-start.42 = (bf16[4,2,96,384]{3,2,1,0:T(8,128)(2,1)S(1)}, bf16[4,2,96,384]{3,2,1,0:T(8,128)(2,1)S(1)}, u32[]{:S(2)}, u32[]{:S(2)}) collective-permute-start(bf16[4,2,96,384]{3,2,1,0:T(8,128)(2,1)S(1)} %get-tuple-element.97), channel_id=1, source_target_pairs={{0,4},{4,0},{1,5},{5,1},{2,6},{6,2},{3,7},{7,3},{8,12},{12,8},{9,1... | collective-permute-start | bytes 1769480 | tf_op jit(solution)/shard_map/ppermute | solution.py:19
  229.6 16.9 %collective-permute-start.36 = (bf16[2,4,96,384]{3,2,1,0:T(8,128)(2,1)}, bf16[2,4,96,384]{3,2,1,0:T(8,128)(2,1)}, u32[]{:S(2)}, u32[]{:S(2)}) collective-permute-start(bf16[2,4,96,384]{3,2,1,0:T(8,128)(2,1)} %get-tuple-element.95), channel_id=1, source_target_pairs={{0,2},{1,3},{2,0},{3,1},{4,6},{5,7},{6,4},{7,5},{8,10},{9,11},{10,... | collective-permute-start | bytes 1769480 | tf_op jit(solution)/shard_map/ppermute | solution.py:19
  243.1 31.3 %collective-permute-start.20 = (f32[192,384]{1,0:T(8,128)}, f32[192,384]{1,0:T(8,128)}, u32[]{:S(2)}, u32[]{:S(2)}) collective-permute-start(f32[192,384]{1,0:T(8,128)} %get-tuple-element.67), channel_id=1, source_target_pairs={{0,3},{1,11},{2,19},{3,27},{8,2},{9,10},{10,18},{11,26},{16,1},{17... | collective-permute-start | bytes 884744 | tf_op jit(solution)/shard_map/ppermute | solution.py:279
  246.4 63.7 %collective-permute-start.43 = (bf16[2,4,2,96,384]{4,3,2,1,0:T(8,128)(2,1)}, bf16[2,4,2,96,384]{4,3,2,1,0:T(8,128)(2,1)}, u32[]{:S(2)}, u32[]{:S(2)}) collective-permute-start(bf16[2,4,2,96,384]{4,3,2,1,0:T(8,128)(2,1)} %get-tuple-element.65), channel_id=1, source_target_pairs={{0,1},{1,0},{2,3},{3,2},{4,5},{5,4},{6,7},{7,6},{8,9},{9,8},{10,11... | collective-permute-start | bytes 3538952 | tf_op jit(solution)/shard_map/ppermute | solution.py:19
  248.8 62.8 %collective-permute-start.37 = (bf16[2,2,4,96,384]{4,3,0,2,1:T(8,128)(2,1)}, bf16[2,2,4,96,384]{4,3,0,2,1:T(8,128)(2,1)}, u32[]{:S(2)}, u32[]{:S(2)}) collective-permute-start(bf16[2,2,4,96,384]{4,3,0,2,1:T(8,128)(2,1)} %get-tuple-element.63), channel_id=1, source_target_pairs={{0,1},{1,0},{2,3},{3,2},{4,5},{5,4},{6,7},{7,6},{8,9},{9,8},{10,11... | collective-permute-start | bytes 3538952 | tf_op jit(solution)/shard_map/ppermute | solution.py:19
  249.3 4.8 %collective-permute-start.24 = (bf16[192,192]{0,1:T(8,128)(2,1)S(1)}, bf16[192,192]{0,1:T(8,128)(2,1)S(1)}, u32[]{:S(2)}, u32[]{:S(2)}) collective-permute-start(bf16[192,192]{0,1:T(8,128)(2,1)S(1)} %select_convert_fusion.3), channel_id=1, source_target_pairs={{0,4},{4,0},{8,12},{12,8},{16,20},{20,16},{24,28},{28,24},{1,5},{5... | collective-permute-start | bytes 221192 | tf_op jit(solution)/shard_map/ppermute | solution.py:294
  250.3 24.2 %copy-start.13 = (bf16[192,192]{0,1:T(8,128)(2,1)}, bf16[192,192]{0,1:T(8,128)(2,1)S(1)}, u32[]{:S(2)}) copy-start(bf16[192,192]{0,1:T(8,128)(2,1)S(1)} %collective-permute-done.25) | copy-start | bytes 221188
  250.3 7.0 %collective-permute-start.23 = (bf16[192,192]{0,1:T(8,128)(2,1)S(1)}, bf16[192,192]{0,1:T(8,128)(2,1)S(1)}, u32[]{:S(2)}, u32[]{:S(2)}) collective-permute-start(bf16[192,192]{0,1:T(8,128)(2,1)S(1)} %copy-done.25), channel_id=1, source_target_pairs={{0,24},{4,28},{8,16},{12,20},{16,8},{20,12},{24,0},{28,4},{1,25},{... | collective-permute-start | bytes 221192 | tf_op jit(solution)/shard_map/ppermute | solution.py:294
  254.1 9.6 %collective-permute-start.22 = (bf16[192,192]{0,1:T(8,128)(2,1)S(1)}, bf16[192,192]{0,1:T(8,128)(2,1)S(1)}, u32[]{:S(2)}, u32[]{:S(2)}) collective-permute-start(bf16[192,192]{0,1:T(8,128)(2,1)S(1)} %copy-done.26), channel_id=1, source_target_pairs={{0,16},{4,20},{8,24},{12,28},{16,0},{20,4},{24,8},{28,12},{1,17},{... | collective-permute-start | bytes 221192 | tf_op jit(solution)/shard_map/ppermute | solution.py:294
  257.3 9.4 %collective-permute-start.21 = (bf16[192,192]{0,1:T(8,128)(2,1)S(1)}, bf16[192,192]{0,1:T(8,128)(2,1)S(1)}, u32[]{:S(2)}, u32[]{:S(2)}) collective-permute-start(bf16[192,192]{0,1:T(8,128)(2,1)S(1)} %copy-done.27), channel_id=1, source_target_pairs={{0,8},{4,12},{8,0},{12,4},{16,24},{20,28},{24,16},{28,20},{1,9},{5... | collective-permute-start | bytes 221192 | tf_op jit(solution)/shard_map/ppermute | solution.py:294
  263.7 19.0 %collective-permute-start.19 = (f32[192,384]{1,0:T(8,128)}, f32[192,384]{1,0:T(8,128)S(1)}, u32[]{:S(2)}, u32[]{:S(2)}) collective-permute-start(f32[192,384]{1,0:T(8,128)} %get-tuple-element.68), channel_id=1, source_target_pairs={{0,2},{1,10},{2,18},{3,26},{8,3},{9,11},{10,19},{11,27},{16,0},{17... | collective-permute-start | bytes 884744 | tf_op jit(solution)/shard_map/ppermute | solution.py:279
  266.7 16.1 %collective-permute-start.17 = (f32[192,384]{1,0:T(8,128)}, f32[192,384]{1,0:T(8,128)S(1)}, u32[]{:S(2)}, u32[]{:S(2)}) collective-permute-start(f32[192,384]{1,0:T(8,128)} %get-tuple-element.69), channel_id=1, source_target_pairs={{0,0},{1,8},{2,16},{3,24},{8,1},{9,9},{10,17},{11,25},{16,2},{17,1... | collective-permute-start | bytes 884744 | tf_op jit(solution)/shard_map/ppermute | solution.py:279
  274.5 33.8 %collective-permute-start.18 = (f32[192,384]{1,0:T(8,128)}, f32[192,384]{1,0:T(8,128)S(1)}, u32[]{:S(2)}, u32[]{:S(2)}) collective-permute-start(f32[192,384]{1,0:T(8,128)} %get-tuple-element.66), channel_id=1, source_target_pairs={{0,1},{1,9},{2,17},{3,25},{8,0},{9,8},{10,16},{11,24},{16,3},{17,1... | collective-permute-start | bytes 884744 | tf_op jit(solution)/shard_map/ppermute | solution.py:279
  (40 other events, 139.6 us)
where the time goes:
time: 359 us; the launch traced here: 352 us
  starting transfers between devices  89.5 us (25%)
  waiting for transfers between devices  87 us (24%)
  local copies, waits for them, and re-layouts  63.6 us (18%)
  matrix products  49.8 us (14%)
  other arithmetic  32 us (9%)
  Pallas kernels  27.7 us (8%)
    ppermute x8, waiting for transfers between devices, deliver(): total = total + lax.ppermute(sent, ('lvl', 'orb'), to).astype(f32)  40.8 us
    dot_general x16, matrix products, contract(): lax.dot_general(left, right, (((0,), (0,)), ((), ())), preferred_element_...  38.3 us
    ppermute x23, waiting for transfers between devices, swap(): return lax.ppermute(value, axis, [(i, i ^ bit) for i in range(count)])  35.5 us
    ppermute x23, starting transfers between devices, swap(): return lax.ppermute(value, axis, [(i, i ^ bit) for i in range(count)])  27.9 us
    pallas_call x1, Pallas kernels, kinetic(): pl.pallas_call(functools.partial(kinetic_kernel, edge, slots), out_shape=...  27.7 us
    ppermute x8, starting transfers between devices, deliver(): total = total + lax.ppermute(sent, ('lvl', 'orb'), to).astype(f32)  27.2 us
    ppermute x7, starting transfers between devices, deliver_turned(): sent = lax.ppermute(sent, BOX, to)  18.6 us
    ppermute x6, starting transfers between devices, shift(): lax.ppermute(value, axis, [(i, i + step) for i in range(count) if 0 <= i...  15.8 us
  transfers between devices with their start and end apart: 44, of which 14 were waited for; matrix products, arithmetic and copies ran while one was open for 25% of the time, Pallas kernels for 8%

commit v1 on v0

v1 whole, which is shorter than its diff:
```python
import functools

import jax
import jax.numpy as jnp
import numpy as np
from jax import lax
from jax.experimental import pallas as pl
from jax.experimental.pallas import tpu as pltpu
from jax.sharding import Mesh, PartitionSpec as P

PAIR = 2
ROWS = 16
BOX = ("lvl", "pair")
f32, bf16 = jnp.float32, jnp.bfloat16


def swap(value, axis, bit):
    count = lax.axis_size(axis)
    return lax.ppermute(value, axis, [(i, i ^ bit) for i in range(count)])


def shift(value, axis, step):
    count = lax.axis_size(axis)
    return lax.ppermute(value, axis, [(i, i + step) for i in range(count) if 0 <= i + step < count])


def contract(left, right):
    return lax.dot_general(left, right, (((0,), (0,)), ((), ())), preferred_element_type=f32)


def matmul(left, right):
    return jnp.dot(left, right, preferred_element_type=f32)


def spread(value, axis, bits):
    return jnp.stack([swap(value, axis, bit) if bit else value for bit in bits])


def params(mebibytes):
    return pltpu.CompilerParams(vmem_limit_bytes=mebibytes * 1024 * 1024)


def pack_kernel(meta, orbitals, facts, active, mine, theirs):
    slots, coefficients, width = orbitals.shape
    half, fold = width // PAIR, coefficients // 2
    first = meta[0] == 0
    for slot in range(slots):
        keep = slot < meta[1]
        for part in range(2):
            rows = slice(part * fold, (part + 1) * fold)
            here = orbitals[slot, rows, :]
            here = jnp.where(keep, here, jnp.zeros_like(here))
            active[slot, rows, :] = here
            low, high = here[:, :half], here[:, half:]
            lanes = slice(part * half, (part + 1) * half)
            mine[slot, :fold, lanes] = jnp.where(first, low, high)
            theirs[slot, :fold, lanes] = jnp.where(first, high, low)
        for out in (mine, theirs):
            out[slot, fold:, :] = jnp.broadcast_to(facts[slot : slot + 1, :], (out.shape[1] - fold, width)).astype(bf16)


def pack(meta, orbitals, facts):
    slots, coefficients, width = orbitals.shape
    fold = coefficients // 2
    padded = (fold // ROWS + 1) * ROWS
    vmem = pl.BlockSpec(memory_space=pltpu.VMEM)
    packed = jax.ShapeDtypeStruct((slots, padded, width), bf16)
    return pl.pallas_call(
        pack_kernel,
        out_shape=(jax.ShapeDtypeStruct(orbitals.shape, bf16), packed, packed),
        in_specs=[pl.BlockSpec(memory_space=pltpu.SMEM), vmem, vmem],
        out_specs=(vmem, vmem, vmem),
        compiler_params=params(24),
        name="pack",
    )(meta, orbitals, facts)


def load_left(lefts, held, sems):
    copies = [pltpu.make_async_copy(left, held.at[i], sems.at[i]) for i, left in enumerate(lefts)]
    for copy in copies:
        copy.start()
    return copies


def correlation_kernel(levels, meta, *refs):
    lefts, out, held, turned, sems = refs[:-4], refs[-4], refs[-3], refs[-2], refs[-1]
    copies = load_left(lefts, held, sems)
    groups = len(lefts) // 2
    half, width = out.shape[1:]
    first, apart = meta[0] == 0, meta[1]
    for copy in copies:
        copy.wait()
    for side in range(2):
        own = held[side * groups]
        turned[side] = jnp.where(first, own[:, :half], own[:, half:]).T

    def per_group(q, carry):
        total = matmul(turned[0], held[q]) + matmul(turned[1], held[groups + q])
        rows = lax.broadcasted_iota(jnp.int32, (half, width), 0) + jnp.where(first, 0, half)
        columns = lax.broadcasted_iota(jnp.int32, (half, width), 1)
        share = jnp.where((rows == columns) & (q == 0), 1.0 / levels, 0.0)
        out[q ^ apart] = (total - share).astype(bf16)
        return carry

    lax.fori_loop(0, groups, per_group, 0)


def fock_kernel(meta, *refs):
    lefts, right, out, held, raw, turned, sems = refs[:-6], refs[-6], refs[-5], refs[-4], refs[-3], refs[-2], refs[-1]
    copies = load_left(lefts, held, sems)
    last = pltpu.make_async_copy(right, raw, sems.at[len(lefts)])
    last.start()
    groups = len(lefts) // 2
    half, width = out.shape[2:]
    apart = meta[1]
    last.wait()
    for side in range(2):
        turned[side] = raw[side].T
    for copy in copies:
        copy.wait()

    def per_group(q, carry):
        total = matmul(turned[0], held[q]) + matmul(turned[1], held[groups + q])
        main = total[:half] + total[half : 2 * half]
        top = main.astype(bf16)
        out[q ^ apart, 0] = top
        out[q ^ apart, 1] = (main - top.astype(f32)).astype(bf16)
        out[q ^ apart, 2] = total[2 * half :].astype(bf16)
        return carry

    lax.fori_loop(0, groups, per_group, 0)


def row_products(kernel, name, meta, lefts, right, shape, tall):
    depth, width = lefts[0].shape
    smem = pl.BlockSpec(memory_space=pltpu.SMEM)
    anywhere = pl.BlockSpec(memory_space=pl.ANY)
    scratch = [pltpu.VMEM((len(lefts), depth, width), bf16)]
    if right is not None:
        scratch.append(pltpu.VMEM(right.shape, bf16))
    scratch += [pltpu.VMEM((2, tall, depth), bf16), pltpu.SemaphoreType.DMA((len(lefts) + 1,))]
    operands = list(lefts) + ([] if right is None else [right])
    return pl.pallas_call(
        kernel,
        out_shape=jax.ShapeDtypeStruct(shape, bf16),
        in_specs=[smem] + [anywhere] * len(operands),
        out_specs=pl.BlockSpec(memory_space=pltpu.VMEM),
        scratch_shapes=scratch,
        compiler_params=params(40),
        cost_estimate=pl.CostEstimate(
            flops=2 * len(lefts) * depth * width * tall, bytes_accessed=2 * len(lefts) * depth * width, transcendentals=0
        ),
        name=name,
    )(meta, *operands)


def root_kernel(meta, top, low, offset, root, whole, rows_f, cols_b):
    level, pair, orb = meta[0], meta[1], meta[2]
    fine, width = top.shape[4:]
    coarse = 2 * fine
    side = whole.shape[0]
    groups = side // width
    for core in range(2):
        for far in range(top.shape[1]):
            lanes = pl.ds(pl.multiple_of((orb ^ (2 * far + core)) * width, width), width)
            for z in range(top.shape[3]):
                for y in range(PAIR):
                    start = ((level ^ z) * PAIR + (pair ^ y)) * coarse
                    whole[pl.ds(pl.multiple_of(start, fine), fine), lanes] = top[core, far, y, z]
                    whole[pl.ds(pl.multiple_of(start + fine, fine), fine), lanes] = low[core, y, z, far]
    row0 = pl.multiple_of((level * PAIR + pair) * coarse, coarse)
    own_lanes = pl.ds(pl.multiple_of(orb * width, width), width)
    rows = whole[pl.ds(row0, coarse), :]

    def across(j, carry):
        lanes = pl.ds(pl.multiple_of(j * width, width), width)
        rows_f[:, lanes] = matmul(rows, whole[:, lanes])
        return carry

    lax.fori_loop(0, groups, across, 0)
    columns = whole[:, own_lanes]

    def down(i, carry):
        here = pl.ds(pl.multiple_of(i * coarse, coarse), coarse)
        square = matmul(whole[here, :], columns)
        cols_b[here, :] = (0.25 * (whole[here, own_lanes].astype(f32) - square)).astype(bf16)
        return carry

    lax.fori_loop(0, side // coarse, down, 0)
    left = (rows.astype(f32) - 0.25 * rows_f[...]).astype(bf16)
    value = matmul(left, cols_b[...]) + 0.125 * rows_f[:, own_lanes] - 0.5 * offset[...]
    row_ids = lax.broadcasted_iota(jnp.int32, value.shape, 0) + row0
    col_ids = lax.broadcasted_iota(jnp.int32, value.shape, 1) + orb * width
    root[...] = value + jnp.where(row_ids == col_ids, 1.0, 0.0)


def root_of(meta, top, low, offset, side):
    coarse, width = offset.shape
    vmem = pl.BlockSpec(memory_space=pltpu.VMEM)
    return pl.pallas_call(
        root_kernel,
        out_shape=jax.ShapeDtypeStruct(offset.shape, f32),
        in_specs=[pl.BlockSpec(memory_space=pltpu.SMEM), vmem, vmem, vmem],
        out_specs=vmem,
        scratch_shapes=[
            pltpu.VMEM((side, side), bf16),
            pltpu.VMEM((coarse, side), f32),
            pltpu.VMEM((side, width), bf16),
        ],
        compiler_params=params(40),
        name="root",
    )(meta, top, low, offset)


def kinetic_kernel(edge, slots, table, scale, *refs):
    parts, (pot, fwd_in, fwd_out, back_in, back_out), out = refs[:6], refs[6:11], refs[11]
    raw, x, rounded, left_over, total, total_fix, sems = refs[12:]
    square = edge * edge
    own = PAIR * slots
    width = x.shape[3]
    copies = [pltpu.make_async_copy(part, raw.at[place], sems.at[place]) for place, part in enumerate(parts)]
    for copy in copies:
        copy.start()
    x[...] = jnp.zeros_like(x)
    total[...] = jnp.zeros_like(total)
    total_fix[...] = jnp.zeros_like(total_fix)
    for copy in copies:
        copy.wait()

    def lay_out(place, carry):
        for slot in range(slots):
            for i in range(edge):
                part, row = i // (edge // 2), i % (edge // 2) * square
                x[place * slots + slot, i, :square, :] = raw[
                    place, slot, row : row + square, part * width : (part + 1) * width
                ]
        return carry

    lax.fori_loop(0, len(parts), lay_out, 0)
    chunks = -(-square // ROWS)

    def per_slot(s, carry):
        @pl.when(table[s, 0] >= 0)
        def _():
            own_scale = scale[s]
            for a in range(3):
                source = [table[s, 1 + 3 * a + k] for k in range(3)]
                for i in range(chunks if a == 0 else edge):
                    if a == 0:
                        rows = slice(i * ROWS, (i + 1) * ROWS)
                        block = jnp.concatenate([x[t, :, rows, :].reshape(edge * ROWS, width) for t in source], axis=0)
                        exact = (own_scale * matmul(fwd_out[...], block)).reshape(edge, ROWS, width)
                        value = exact.astype(bf16)
                        rounded[:, rows, :] = value
                        left_over[:, rows, :] = (value.astype(f32) - exact).astype(bf16)
                    else:
                        block = jnp.concatenate([x[t, i] for t in source], axis=0)
                        exact = own_scale * matmul(fwd_in[a - 1], block)
                        value = exact.astype(bf16)
                        rounded[i] = value
                        left_over[i] = (value.astype(f32) - exact).astype(bf16)
                half = 0.5 * own_scale
                for k in range(3):
                    target = source[k]

                    @pl.when(target < own)
                    def _():
                        for i in range(chunks if a == 0 else edge):
                            for field, sum_ref in ((rounded, total), (left_over, total_fix)):
                                if a == 0:
                                    rows = slice(i * ROWS, (i + 1) * ROWS)
                                    term = matmul(back_out[k], field[:, rows, :].reshape(edge * ROWS, width))
                                    sum_ref[target, :, rows, :] += half * term.reshape(edge, ROWS, width)
                                else:
                                    sum_ref[target, i] += half * matmul(back_in[a - 1, k], field[i])

        return carry

    lax.fori_loop(0, table.shape[0], per_slot, 0)

    def finish(t, carry):
        for i in range(edge):
            rows = slice(i * square, (i + 1) * square)
            exact = pot[t, rows, :] * x[t, i, :square, :].astype(f32)
            lost = exact.astype(bf16).astype(f32) - exact
            whole = total[t, i, :square, :] + exact
            top = whole.astype(bf16)
            low = (whole - top.astype(f32)).astype(bf16)
            fix = (total_fix[t, i, :square, :] + lost).astype(bf16)
            out[t, rows, :] = jnp.concatenate([top, low, fix], axis=1)
        return carry

    lax.fori_loop(0, own, finish, 0)


def block_matrices(deriv_blocks):
    edge = deriv_blocks.shape[1]
    square = edge * edge
    padded = -(-square // ROWS) * ROWS
    ids = np.arange(padded)
    slow = ((ids[:, None] // edge) == np.arange(edge)).astype(np.float32)
    fast = (((ids[:, None] % edge) == np.arange(edge)) & (ids[:, None] < square)).astype(np.float32)
    ids = np.arange(edge * ROWS)
    outer = ((ids[:, None] // ROWS) == np.arange(edge)).astype(np.float32)
    within = ((ids[:, None] % ROWS) == np.arange(ROWS)).astype(np.float32)
    stacked = jnp.moveaxis(deriv_blocks, 0, 1).reshape(edge, 3 * edge)
    forward, backward = [], []
    for spot, mask in ((slow, fast), (fast, slow), (outer, within)):
        same = mask @ mask.T
        spread_out = np.kron(np.eye(3, dtype=np.float32), spot.T)
        spot_b, same_b = jnp.asarray(spot, bf16), jnp.asarray(same, f32)
        wide = matmul(matmul(spot_b, stacked).astype(bf16), jnp.asarray(spread_out, bf16))
        forward.append((wide * jnp.tile(same_b, (1, 3))).astype(bf16))
        turned = jnp.einsum("ri,kji->krj", spot_b, deriv_blocks, preferred_element_type=f32).astype(bf16)
        turned = jnp.einsum("krj,cj->krc", turned, spot_b, preferred_element_type=f32)
        backward.append((turned * same_b).astype(bf16))
    return jnp.stack(forward[:2]), forward[2], jnp.stack(backward[:2]), backward[2]


def kinetic(parts, pot, matrices, table, scale, edge, coefficients):
    slots, folded, lanes = parts[0].shape
    width = lanes // 2
    padded = matrices[0].shape[1]
    own = PAIR * slots
    vmem = pl.BlockSpec(memory_space=pltpu.VMEM)
    smem = pl.BlockSpec(memory_space=pltpu.SMEM)
    anywhere = pl.BlockSpec(memory_space=pl.ANY)
    return pl.pallas_call(
        functools.partial(kinetic_kernel, edge, slots),
        out_shape=jax.ShapeDtypeStruct((own, coefficients, 3 * width), bf16),
        in_specs=[smem, smem] + [anywhere] * 6 + [vmem] * 5,
        out_specs=vmem,
        scratch_shapes=[
            pltpu.VMEM((6, slots, folded, lanes), bf16),
            pltpu.VMEM((6 * slots + 1, edge, padded, width), bf16),
            pltpu.VMEM((edge, padded, width), bf16),
            pltpu.VMEM((edge, padded, width), bf16),
            pltpu.VMEM((own, edge, padded, width), f32),
            pltpu.VMEM((own, edge, padded, width), f32),
            pltpu.SemaphoreType.DMA((6,)),
        ],
        compiler_params=params(48),
        cost_estimate=pl.CostEstimate(flops=2 * 10**10, bytes_accessed=40 * 10**6, transcendentals=0),
        name="kinetic",
    )(table, scale, *parts, pot, *matrices)


def body(orbitals, potential, deriv_blocks, levels, box_counts, neighbours):
    slots, coefficients, own_width = orbitals.shape
    edge = deriv_blocks.shape[1]
    level, pair, orb = lax.axis_index("lvl"), lax.axis_index("pair"), lax.axis_index("orb")
    level_count, orb_count = lax.axis_size("lvl"), lax.axis_size("orb")
    half, fold = own_width // PAIR, coefficients // 2
    all_width = own_width * orb_count
    box_rows = all_width // (level_count * PAIR)
    first = pair == 0
    groups = range(orb_count)
    square_grid = level_count == orb_count and box_rows == half
    row0, col0 = (level * PAIR + pair) * box_rows, orb * own_width

    slot_ids = jnp.arange(slots, dtype=jnp.int32)
    own_ids = (level * PAIR + pair) * slots + slot_ids
    none = 16 * slots
    apart_ids = jnp.where(neighbours >= 0, neighbours - own_ids[:, None, None], none).reshape(slots, 6)
    live = (slot_ids < box_counts[0]).astype(jnp.int32)
    facts = jnp.concatenate([apart_ids, levels[:, None], live[:, None]], axis=1)
    wide_facts = jnp.pad(facts.astype(f32), ((0, 0), (0, own_width - facts.shape[1])))
    active, mine, theirs = pack(jnp.stack([pair, box_counts[0]]).astype(jnp.int32), orbitals, wide_facts)

    far = {q: swap(active, "orb", q) for q in groups if q and q % 2 == 0}
    beside = swap(theirs, "pair", 1)
    lower, upper = shift(mine, "lvl", 1), shift(mine, "lvl", -1)
    beside_rest = swap(mine, "pair", 1)
    later_pot, beside = lax.optimization_barrier((potential, beside))
    lower_beside, upper_beside = shift(beside, "lvl", 1), shift(beside, "lvl", -1)
    other_pot = swap(later_pot, "pair", 1)
    matrices = block_matrices(deriv_blocks)

    far, beside_rest, lower, upper, active, matrices = lax.optimization_barrier(
        (far, beside_rest, lower, upper, active, matrices)
    )

    def unfold(packed):
        return jnp.concatenate([packed[:, :fold, :half], packed[:, :fold, half:]], axis=1)

    beside_half, rest_half = unfold(beside), unfold(beside_rest)
    beside_all = jnp.concatenate(
        [jnp.where(first, beside_half, rest_half), jnp.where(first, rest_half, beside_half)], axis=2
    )
    cut = slots // 2
    far_beside = {
        q: jnp.concatenate([swap(beside_all[:cut], "orb", q), swap(far[q][cut:], "pair", 1)]) for q in far
    }
    left_own = {0: active, 1: swap(active, "orb", 1), **far}
    left_beside = {0: beside_all, 1: swap(beside_all, "orb", 1), **far_beside}
    for q in far:
        left_own[q + 1] = swap(far[q], "orb", 1)
        left_beside[q + 1] = swap(far_beside[q], "orb", 1)
    flat = lambda block: block.reshape(slots * coefficients, block.shape[-1])
    lefts = [flat(left_own[q]) for q in groups] + [flat(left_beside[q]) for q in groups]

    def facts_of(packed):
        return packed[:, fold, : facts.shape[1]].astype(f32).astype(jnp.int32)

    box_of_level = level * PAIR
    ids = jnp.concatenate(
        [
            own_ids,
            (box_of_level + 1 - pair) * slots + slot_ids,
            (box_of_level - 1) * slots + slot_ids,
            (box_of_level + PAIR) * slots + slot_ids,
        ]
    ).astype(jnp.int32)
    chosen = jnp.concatenate(
        [
            facts,
            facts_of(beside),
            jnp.where(first, facts_of(lower_beside), facts_of(lower)),
            jnp.where(first, facts_of(upper), facts_of(upper_beside)),
        ]
    )
    there = (ids >= 0) & (ids < level_count * PAIR * slots)

    def place(slot_id):
        box = slot_id // slots
        apart = box // PAIR - level
        base = jnp.where(apart == 0, 0, jnp.where(apart < 0, 2, 4))
        return (base + (box % PAIR != pair)) * slots + slot_id % slots

    distance = chosen[:, :6]
    near = jnp.where(distance < none, place(jnp.maximum(ids, 0)[:, None] + distance), 6 * slots)
    near = jnp.clip(near, 0, 6 * slots)
    self_place = place(jnp.maximum(ids, 0))
    table = [jnp.where(there & (chosen[:, 7] > 0), self_place, -1)]
    for a in range(3):
        table += [near[:, 2 * a], self_place, near[:, 2 * a + 1]]
    table = jnp.stack(table, axis=1).astype(jnp.int32)
    level_of = chosen[:, 6]
    scale = jnp.where(level_of == 0, 0.5, jnp.where(level_of == 1, 1.0, 2.0)).astype(f32)
    pot = jnp.concatenate([potential, other_pot])[:, :, None]

    def natural(blocks):
        return jnp.concatenate([lax.dynamic_index_in_dim(blocks, orb ^ j, keepdims=False) for j in groups], axis=1)

    def deliver(blocks):
        got = []
        for step in groups:
            to = [(z * orb_count + o, o * orb_count + (z ^ step)) for z in range(level_count) for o in groups]
            got.append(lax.ppermute(blocks[step], ("lvl", "orb"), to))
        return got

    def own_block(strip):
        strip = lax.all_gather(lax.psum(strip, "lvl"), ("orb", "pair"), axis=0, tiled=True)
        strip = lax.dynamic_slice_in_dim(strip, row0, box_rows, axis=0)
        return lax.dynamic_slice_in_dim(strip, col0, own_width, axis=1)

    apart = orb ^ level if square_grid else 0 * orb
    meta = jnp.stack([pair, apart]).astype(jnp.int32)

    parts = [mine, beside, lower, lower_beside, upper, upper_beside]
    right = kinetic(parts, pot, matrices, table, scale, edge, coefficients)

    shape = (orb_count, half, own_width)
    blocks = row_products(
        functools.partial(correlation_kernel, level_count), "correlation", meta, lefts, None, shape, half
    )
    if square_grid:
        offset = sum(block.astype(f32) for block in deliver(blocks))
    else:
        offset = own_block(natural(blocks).astype(f32))
    row_ids = row0 + jnp.arange(box_rows, dtype=jnp.int32)
    col_ids = col0 + jnp.arange(own_width, dtype=jnp.int32)
    correlation = offset + (row_ids[:, None] == col_ids[None, :]).astype(f32)
    small = offset.astype(bf16)

    right = right.reshape(2, slots * coefficients, 3 * half)
    shape = (orb_count, 3, half, own_width)
    blocks = row_products(fock_kernel, "fock", meta, lefts, right, shape, 3 * half)
    if square_grid:
        sums = sum(block.astype(f32) for block in deliver(blocks))
        share = sums[2].astype(bf16)
        pieces = []
        for over in range(PAIR):
            to_first = (pair ^ over) == 0
            sent = jnp.where(to_first, share[:, :half], share[:, half:])
            to = [
                ((z * PAIR + y) * orb_count + o, (o * PAIR + (y ^ over)) * orb_count + z)
                for z in range(level_count)
                for y in range(PAIR)
                for o in groups
            ]
            pieces.append(lax.ppermute(sent, BOX + ("orb",), to).astype(f32).T)
        turned = jnp.concatenate(
            [jnp.where(first, pieces[0], pieces[1]), jnp.where(first, pieces[1], pieces[0])], axis=1
        )
        fock = sums[0] + sums[1] + turned
    else:
        fock = own_block(natural(blocks[:, 0]).astype(f32) + natural(blocks[:, 1]).astype(f32))
        share = lax.all_gather(lax.psum(natural(blocks[:, 2]).astype(f32), "lvl"), "pair", axis=0, tiled=True)
        fock = fock + lax.dynamic_slice_in_dim(share, row0, box_rows, axis=1).T

    if square_grid:
        levels_of, far_of = range(level_count), range(0, orb_count, 2)
        top, low = small[: box_rows // 2], small[box_rows // 2 :]
        top = spread(spread(spread(spread(top, "lvl", levels_of), "pair", (0, 1)), "orb", far_of), "orb", (0, 1))
        low = spread(spread(spread(spread(low, "orb", far_of), "lvl", levels_of), "pair", (0, 1)), "orb", (0, 1))
        inverse_root = root_of(jnp.stack([level, pair, orb]).astype(jnp.int32), top, low, offset, all_width)
    else:
        gathered = lax.all_gather(small, "orb", axis=1, tiled=True)
        whole = lax.all_gather(gathered, BOX, axis=0, tiled=True)
        rows_of = lax.dynamic_slice_in_dim(whole, row0, box_rows, axis=0)
        cols_of = lax.dynamic_slice_in_dim(whole, col0, own_width, axis=1)
        row_square, col_square = matmul(rows_of, whole), matmul(whole, cols_of)
        left = (rows_of.astype(f32) - 0.25 * row_square).astype(bf16)
        right_side = (0.25 * (cols_of.astype(f32) - col_square)).astype(bf16)
        own_square = lax.dynamic_slice_in_dim(row_square, col0, own_width, axis=1)
        inverse_root = correlation - 1.5 * offset + 0.125 * own_square + matmul(left, right_side)
    return fock, correlation, inverse_root


def solution(mesh):
    levels = mesh.shape["box"] // PAIR
    split = Mesh(mesh.devices.reshape(levels, PAIR, mesh.shape["orb"]), ("lvl", "pair", "orb"))
    in_specs = (P(BOX, None, "orb"), P(BOX, None), P(), P(BOX), P(BOX), P(BOX, None, None))
    out_specs = (P(BOX, "orb"),) * 3
    return jax.shard_map(body, mesh=split, in_specs=in_specs, out_specs=out_specs, check_vma=False)
```

time: 359 us -> 292 us (0.81)
  the two profiles are of different devices: /device:TPU:24 before, /device:TPU:2 now
where the time goes in v1:
time: 292 us; the launch traced here: 290 us
  starting transfers between devices  96.3 us (33%)
  waiting for transfers between devices  83.1 us (28%)
  Pallas kernels  61.4 us (21%)
  other arithmetic  22.9 us (8%)
  local copies, waits for them, and re-layouts  19.7 us (7%)
  matrix products  4.91 us (2%)
    ppermute x8, starting transfers between devices, deliver(): got.append(lax.ppermute(blocks[step], ('lvl', 'orb'), to))  51.4 us
    ppermute x22, waiting for transfers between devices, swap(): return lax.ppermute(value, axis, [(i, i ^ bit) for i in range(count)])  37.5 us
    ppermute x8, waiting for transfers between devices, deliver(): got.append(lax.ppermute(blocks[step], ('lvl', 'orb'), to))  33.5 us
    ppermute x22, starting transfers between devices, swap(): return lax.ppermute(value, axis, [(i, i ^ bit) for i in range(count)])  28.6 us
    pallas_call x2, Pallas kernels, row_products(): pl.pallas_call(kernel, out_shape=jax.ShapeDtypeStruct(shape, bf16), in_sp...  26.3 us
    pallas_call x1, Pallas kernels, kinetic(): pl.pallas_call(functools.partial(kinetic_kernel, edge, slots), out_shape=...  24.4 us
    ppermute x4, starting transfers between devices, shift(): lax.ppermute(value, axis, [(i, i + step) for i in range(count) if 0 <= i...  10.8 us
    pallas_call x1, Pallas kernels, root_of(): pl.pallas_call(root_kernel, out_shape=jax.ShapeDtypeStruct(offset.shape,...  7.87 us
  transfers between devices with their start and end apart: 36, of which 9 were waited for; matrix products, arithmetic and copies ran while one was open for 14% of the time, Pallas kernels for 14%

profile of v1, /device:TPU:2, one launch (start us, length us, event | category | flops | bytes accessed | tf_op | source)
XLA Modules:
  0.0 290.2 jit_solution(7009731821024168500)
XLA Ops:
  3.7 1.4 copy-done
  5.1 2.8 pack.1
  8.0 1.5 collective-permute-start.1
  9.5 3.5 %collective-permute-start.2 = (bf16[2,512,384]{2,1,0:T(8,128)(2,1)}, bf16[2,512,384]{2,1,0:T(8,128)(2,1)S(1)}, u32[]{:S(2)}, u32[]{:S(2)}) collective-permute-start(bf16[2,512,384]{2,1,0:T(8,128)(2,1)} %get-tuple-element.18.refs_0_), channel_id=1, source_target_pairs={{0,8},{8,16},{16,24},{1,9},{9,17},{17,25},{2,10},{10,18},{18,26},{... | collective-permute-start | bytes 2359304 | tf_op jit(solution)/shard_map/ppermute | solution.py:24
  13.0 1.3 collective-permute-start.3
  21.3 1.4 add_maximum_fusion
  23.5 2.1 fusion.1.refs_8_
  25.5 1.3 fusion.refs_10_
  26.9 17.6 %collective-permute-done.6.refs_1_ = bf16[2,512,384]{2,1,0:T(8,128)(2,1)} collective-permute-done((bf16[2,512,384]{2,1,0:T(8,128)(2,1)}, bf16[2,512,384]{2,1,0:T(8,128)(2,1)}, u32[]{:S(2)}, u32[]{:S(2)}) %collective-permute-start.6) | collective-permute-done | bytes 786464 | tf_op jit(solution)/shard_map/ppermute | solution.py:19
  44.4 1.5 collective-permute-start.13
  45.9 2.2 fusion.52
  48.9 1.3 collective-permute-start.12
  50.2 2.0 copy.57.refs_6_
  52.2 4.7 %collective-permute-start.11 = (bf16[2,512,384]{2,1,0:T(8,128)(2,1)}, bf16[2,512,384]{2,1,0:T(8,128)(2,1)S(1)}, u32[]{:S(2)}, u32[]{:S(2)}) collective-permute-start(bf16[2,512,384]{2,1,0:T(8,128)(2,1)} %collective-permute-done.6.refs_1_), channel_id=1, source_target_pairs={{0,8},{8,16},{16,24},{1,9},{9,17},{17,25},{2,10},{10,18},{18,26},{... | collective-permute-start | bytes 2359304 | tf_op jit(solution)/shard_map/ppermute | solution.py:24
  57.0 1.0 slice.111
  58.5 1.4 fusion.53
  60.5 1.8 pad_maximum_fusion.2
  62.4 1.2 fusion.13
  64.1 5.0 %collective-permute-done.12.refs_5_ = bf16[2,512,384]{2,1,0:T(8,128)(2,1)} collective-permute-done((bf16[2,512,384]{2,1,0:T(8,128)(2,1)}, bf16[2,512,384]{2,1,0:T(8,128)(2,1)}, u32[]{:S(2)}, u32[]{:S(2)}) %collective-permute-start.12) | collective-permute-done | bytes 786464 | tf_op jit(solution)/shard_map/ppermute | solution.py:24
  70.4 2.1 collective-permute-done.11.refs_3_
  75.3 11.0 %collective-permute-done.8 = bf16[1,1000,384]{2,1,0:T(8,128)(2,1)} collective-permute-done((bf16[1,1000,384]{2,1,0:T(8,128)(2,1)}, bf16[1,1000,384]{2,1,0:T(8,128)(2,1)}, u32[]{:S(2)}, u32[]{:S(2)}) %collective-permute-start.8) | collective-permute-done | bytes 768032 | tf_op jit(solution)/shard_map/ppermute | solution.py:19
  86.3 1.2 constant_dynamic-update-slice_fusion.1
  87.5 1.8 collective-permute-done.9
  89.3 1.3 constant_dynamic-update-slice_fusion
  90.7 24.4 %kinetic.1 = bf16[4,1000,576]{2,1,0:T(8,128)(2,1)} custom-call(s32[8,10]{1,0:T(8,128)S(1)} %stack.142.table, f32[8]{0:T(128)S(1)} %select_reduce_fusion.scale, bf16[2,512,384]{2,1,0:T(8,128)(2,1)} %get-tuple-element.18.refs_0_, bf16[2,512,384]{2,1,0:T(8,128)(2,1)} %collective-permute-done.6.refs_1_, bf16[2,512,384]{2,1,0:T(8,128)(2,1)S(1)} %copy-done.4, ...), custom_call_target="tpu_custom_call" | custom-call | flops 20000000000 | bytes 40000000 | tf_op jit(solution)/shard_map/kinetic/pallas_call | solution.py:328
  115.2 9.3 %correlation.1 = bf16[4,192,384]{2,1,0:T(8,128)(2,1)S(1)} custom-call(s32[2]{0:T(128)S(1)} %pad_add_fusion.1.meta, bf16[2000,384]{1,0:T(8,128)(2,1)} %bitcast.18.refs_0_, bf16[2000,384]{1,0:T(8,128)(2,1)} %bitcast.19.refs_1_, bf16[2000,384]{1,0:T(8,128)(2,1)S(1)} %bitcast.124, bf16[2000,384]{1,0:T(8,128)(2,1)} %bitcast.21.refs_3_, ...), custom_call_target="tpu_custom_call" | custom-call | flops 2359296000 | bytes 12288000 | tf_op jit(solution)/shard_map/correlation/pallas_call | solution.py:143
  124.5 11.3 %collective-permute-start.23 = (bf16[192,384]{1,0:T(8,128)(2,1)S(1)}, bf16[192,384]{1,0:T(8,128)(2,1)S(1)}, u32[]{:S(2)}, u32[]{:S(2)}) collective-permute-start(bf16[192,384]{1,0:T(8,128)(2,1)S(1)} %get-tuple-element.65), channel_id=1, source_target_pairs={{0,3},{1,11},{2,19},{3,27},{8,2},{9,10},{10,18},{11,26},{16,1},{17... | collective-permute-start | bytes 442376 | tf_op jit(solution)/shard_map/ppermute | solution.py:449
  136.4 6.2 %collective-permute-start.20 = (bf16[192,384]{1,0:T(8,128)(2,1)S(1)}, bf16[192,384]{1,0:T(8,128)(2,1)S(1)}, u32[]{:S(2)}, u32[]{:S(2)}) collective-permute-start(bf16[192,384]{1,0:T(8,128)(2,1)S(1)} %get-tuple-element.64), channel_id=1, source_target_pairs={{0,0},{1,8},{2,16},{3,24},{8,1},{9,9},{10,17},{11,25},{16,2},{17,1... | collective-permute-start | bytes 442376 | tf_op jit(solution)/shard_map/ppermute | solution.py:449
  142.6 17.0 %fock.1 = bf16[4,3,192,384]{3,2,1,0:T(8,128)(2,1)S(1)} custom-call(s32[2]{0:T(128)S(1)} %pad_add_fusion.1.meta, bf16[2000,384]{1,0:T(8,128)(2,1)} %bitcast.18.refs_0_, bf16[2000,384]{1,0:T(8,128)(2,1)} %bitcast.19.refs_1_, bf16[2000,384]{1,0:T(8,128)(2,1)S(1)} %bitcast.125, bf16[2000,384]{1,0:T(8,128)(2,1)} %bitcast.21.refs_3_, ...), custom_call_target="tpu_custom_call" | custom-call | flops 7077888000 | bytes 12288000 | tf_op jit(solution)/shard_map/fock/pallas_call | solution.py:143
  159.6 1.0 collective-permute-done.20
  161.0 2.2 collective-permute-start.17
  164.1 3.5 %collective-permute-start.24 = (bf16[96,384]{1,0:T(8,128)(2,1)S(1)}, bf16[96,384]{1,0:T(8,128)(2,1)S(1)}, u32[]{:S(2)}, u32[]{:S(2)}) collective-permute-start(bf16[96,384]{1,0:T(8,128)(2,1)S(1)} %get-tuple-element.77), channel_id=1, source_target_pairs={{0,8},{8,0},{16,24},{24,16},{1,9},{9,1},{17,25},{25,17},{2,10},{10... | collective-permute-start | bytes 221192 | tf_op jit(solution)/shard_map/ppermute | solution.py:19
  168.3 7.1 %collective-permute-done.26 = bf16[96,384]{1,0:T(8,128)(2,1)S(1)} collective-permute-done((bf16[96,384]{1,0:T(8,128)(2,1)S(1)}, bf16[96,384]{1,0:T(8,128)(2,1)S(1)}, u32[]{:S(2)}, u32[]{:S(2)}) %collective-permute-start.26) | collective-permute-done | bytes 73760 | tf_op jit(solution)/shard_map/ppermute | solution.py:19
  175.4 17.1 %collective-permute-start.32 = (bf16[2,96,384]{2,1,0:T(8,128)(2,1)}, bf16[2,96,384]{2,1,0:T(8,128)(2,1)}, u32[]{:S(2)}, u32[]{:S(2)}) collective-permute-start(bf16[2,96,384]{2,1,0:T(8,128)(2,1)} %get-tuple-element.73), channel_id=1, source_target_pairs={{0,16},{8,24},{16,0},{24,8},{1,17},{9,25},{17,1},{25,9},{2,18},{10... | collective-permute-start | bytes 442376 | tf_op jit(solution)/shard_map/ppermute | solution.py:19
  193.0 8.4 %collective-permute-start.16 = (bf16[3,192,384]{2,1,0:T(8,128)(2,1)S(1)}, bf16[3,192,384]{2,1,0:T(8,128)(2,1)S(1)}, u32[]{:S(2)}, u32[]{:S(2)}) collective-permute-start(bf16[3,192,384]{2,1,0:T(8,128)(2,1)S(1)} %get-tuple-element.48), channel_id=1, source_target_pairs={{0,2},{1,10},{2,18},{3,26},{8,3},{9,11},{10,19},{11,27},{16,0},{17... | collective-permute-start | bytes 1327112 | tf_op jit(solution)/shard_map/ppermute | solution.py:449
  201.4 2.4 collective-permute-start.15
  203.8 20.3 %collective-permute-start.14 = (bf16[3,192,384]{2,1,0:T(8,128)(2,1)S(1)}, bf16[3,192,384]{2,1,0:T(8,128)(2,1)S(1)}, u32[]{:S(2)}, u32[]{:S(2)}) collective-permute-start(bf16[3,192,384]{2,1,0:T(8,128)(2,1)S(1)} %get-tuple-element.46), channel_id=1, source_target_pairs={{0,0},{1,8},{2,16},{3,24},{8,1},{9,9},{10,17},{11,25},{16,2},{17,1... | collective-permute-start | bytes 1327112 | tf_op jit(solution)/shard_map/ppermute | solution.py:449
  224.2 1.2 fusion.48
  226.7 32.5 %collective-permute-done.14 = bf16[3,192,384]{2,1,0:T(8,128)(2,1)S(1)} collective-permute-done((bf16[3,192,384]{2,1,0:T(8,128)(2,1)S(1)}, bf16[3,192,384]{2,1,0:T(8,128)(2,1)S(1)}, u32[]{:S(2)}, u32[]{:S(2)}) %collective-permute-start.14) | collective-permute-done | bytes 442400 | tf_op jit(solution)/shard_map/ppermute | solution.py:449
  259.4 1.2 fusion.46
  260.6 1.2 fusion.47
  263.3 5.2 %collective-permute-start.18 = (bf16[192,192]{1,0:T(8,128)(2,1)S(1)}, bf16[192,192]{1,0:T(8,128)(2,1)}, u32[]{:S(2)}, u32[]{:S(2)}) collective-permute-start(bf16[192,192]{1,0:T(8,128)(2,1)S(1)} %get-tuple-element.79), channel_id=1, source_target_pairs={{0,0},{1,8},{2,16},{3,24},{4,4},{5,12},{6,20},{7,28},{8,1},{9,9},{... | collective-permute-start | bytes 221192 | tf_op jit(solution)/shard_map/ppermute | solution.py:492
  269.4 1.1 copy.62
  270.6 5.0 %collective-permute-done.19 = bf16[192,192]{1,0:T(8,128)(2,1)} collective-permute-done((bf16[192,192]{1,0:T(8,128)(2,1)}, bf16[192,192]{1,0:T(8,128)(2,1)}, u32[]{:S(2)}, u32[]{:S(2)}) %collective-permute-start.19) | collective-permute-done | bytes 73760 | tf_op jit(solution)/shard_map/ppermute | solution.py:492
  277.4 1.9 copy.60
  279.2 1.5 pad_maximum_fusion.1.low
  280.8 1.5 pad_maximum_fusion.top
  282.3 7.9 %root.1 = f32[192,384]{1,0:T(8,128)} custom-call(s32[3]{0:T(128)S(1)} %pad_add_fusion.4.meta, bf16[2,2,2,4,96,384]{5,4,3,2,1,0:T(8,128)(2,1)S(1)} %pad_maximum_fusion.top, bf16[2,2,4,2,96,384]{5,4,3,2,1,0:T(8,128)(2,1)S(1)} %pad_maximum_fusion.1.low, f32[192,384]{1,0:T(8,128)S(1)} %get-tuple-element.41.offset), custom_call_target="tpu_custom_call" | custom-call | tf_op jit(solution)/shard_map/root/pallas_call | solution.py:200
  (169 shorter events, 25.3 us)
Async XLA Ops:
  0.6 17.1 %copy-start.18 = (bf16[112,10,1]{0,1,2:T(8,128)(2,1)S(1)}, bf16[112,10,1]{0,1,2:T(8,128)(2,1)}, u32[]{:S(2)}) copy-start(bf16[112,10,1]{0,1,2:T(8,128)(2,1)} %constant.153) | copy-start | bytes 6724
  0.6 17.1 %copy-start.10 = (f32[112,112]{1,0:T(8,128)S(1)}, f32[112,112]{1,0:T(8,128)}, u32[]{:S(2)}) copy-start(f32[112,112]{1,0:T(8,128)} %constant.137.clone) | copy-start | bytes 150532
  0.7 17.4 %copy-start.23 = (bf16[112,10]{0,1:T(8,128)(2,1)S(1)}, bf16[112,10]{0,1:T(8,128)(2,1)}, u32[]{:S(2)}) copy-start(bf16[112,10]{0,1:T(8,128)(2,1)} %constant.136.clone) | copy-start | bytes 6724
  0.7 16.2 %copy-start.8 = (bf16[3,10,10]{2,0,1:T(4,128)(2,1)S(1)}, bf16[3,10,10]{2,0,1:T(4,128)(2,1)}, u32[]{:S(2)}) copy-start(bf16[3,10,10]{2,0,1:T(4,128)(2,1)} %param.17) | copy-start | bytes 1804
  1.4 15.4 %copy-start.24 = (s32[2,1]{1,0:T(2,128)}, s32[2,1]{1,0:T(2,128)S(1)}, u32[]{:S(2)}) copy-start(s32[2,1]{1,0:T(2,128)S(1)} %compare_convert_fusion) | copy-start | bytes 28
  2.2 14.4 %copy-start.26 = (s32[2,1]{1,0:T(2,128)}, s32[2,1]{1,0:T(2,128)S(1)}, u32[]{:S(2)}) copy-start(s32[2,1]{1,0:T(2,128)S(1)} %copy.44) | copy-start | bytes 28
  3.6 14.9 %copy-start.19 = (s32[2,6]{1,0:T(2,128)}, s32[2,6]{1,0:T(2,128)S(1)}, u32[]{:S(2)}) copy-start(s32[2,6]{1,0:T(2,128)S(1)} %reshape.361) | copy-start | bytes 148
  8.0 44.2 %collective-permute-start.1 = (bf16[2,512,384]{2,1,0:T(8,128)(2,1)}, bf16[2,512,384]{2,1,0:T(8,128)(2,1)}, u32[]{:S(2)}, u32[]{:S(2)}) collective-permute-start(bf16[2,512,384]{2,1,0:T(8,128)(2,1)} %get-tuple-element.18.refs_0_), channel_id=1, source_target_pairs={{0,4},{4,0},{1,5},{5,1},{2,6},{6,2},{3,7},{7,3},{8,12},{12,8},{9,1... | collective-permute-start | bytes 2359304 | tf_op jit(solution)/shard_map/ppermute | solution.py:19
  9.5 47.4 %collective-permute-start.2 = (bf16[2,512,384]{2,1,0:T(8,128)(2,1)}, bf16[2,512,384]{2,1,0:T(8,128)(2,1)S(1)}, u32[]{:S(2)}, u32[]{:S(2)}) collective-permute-start(bf16[2,512,384]{2,1,0:T(8,128)(2,1)} %get-tuple-element.18.refs_0_), channel_id=1, source_target_pairs={{0,8},{8,16},{16,24},{1,9},{9,17},{17,25},{2,10},{10,18},{18,26},{... | collective-permute-start | bytes 2359304 | tf_op jit(solution)/shard_map/ppermute | solution.py:24
  13.0 43.9 %collective-permute-start.3 = (bf16[2,512,384]{2,1,0:T(8,128)(2,1)}, bf16[2,512,384]{2,1,0:T(8,128)(2,1)}, u32[]{:S(2)}, u32[]{:S(2)}) collective-permute-start(bf16[2,512,384]{2,1,0:T(8,128)(2,1)} %get-tuple-element.18.refs_0_), channel_id=1, source_target_pairs={{8,0},{16,8},{24,16},{9,1},{17,9},{25,17},{10,2},{18,10},{26,18},{... | collective-permute-start | bytes 2359304 | tf_op jit(solution)/shard_map/ppermute | solution.py:24
  14.3 42.6 %collective-permute-start = (bf16[2,1000,384]{2,1,0:T(8,128)(2,1)}, bf16[2,1000,384]{2,1,0:T(8,128)(2,1)S(1)}, u32[]{:S(2)}, u32[]{:S(2)}) collective-permute-start(bf16[2,1000,384]{2,1,0:T(8,128)(2,1)} %get-tuple-element.19), channel_id=1, source_target_pairs={{0,2},{1,3},{2,0},{3,1},{4,6},{5,7},{6,4},{7,5},{8,10},{9,11},{10,... | collective-permute-start | bytes 4608008 | tf_op jit(solution)/shard_map/ppermute | solution.py:19
  14.9 29.5 %collective-permute-start.6 = (bf16[2,512,384]{2,1,0:T(8,128)(2,1)}, bf16[2,512,384]{2,1,0:T(8,128)(2,1)}, u32[]{:S(2)}, u32[]{:S(2)}) collective-permute-start(bf16[2,512,384]{2,1,0:T(8,128)(2,1)} %get-tuple-element.21), channel_id=1, source_target_pairs={{0,4},{4,0},{1,5},{5,1},{2,6},{6,2},{3,7},{7,3},{8,12},{12,8},{9,1... | collective-permute-start | bytes 2359304 | tf_op jit(solution)/shard_map/ppermute | solution.py:19
  23.5 26.7 %copy-start.21 = (f32[2,1000]{1,0:T(2,128)S(1)}, f32[2,1000]{1,0:T(2,128)}, u32[]{:S(2)}) copy-start(f32[2,1000]{1,0:T(2,128)} %param.16) | copy-start | bytes 24004
  44.4 4.5 %collective-permute-start.13 = (f32[2,1000]{1,0:T(2,128)}, f32[2,1000]{1,0:T(2,128)S(1)}, u32[]{:S(2)}, u32[]{:S(2)}) collective-permute-start(f32[2,1000]{1,0:T(2,128)} %param.16), channel_id=1, source_target_pairs={{0,4},{4,0},{1,5},{5,1},{2,6},{6,2},{3,7},{7,3},{8,12},{12,8},{9,1... | collective-permute-start | bytes 24008 | tf_op jit(solution)/shard_map/ppermute | solution.py:19
  48.9 20.3 %collective-permute-start.12 = (bf16[2,512,384]{2,1,0:T(8,128)(2,1)}, bf16[2,512,384]{2,1,0:T(8,128)(2,1)}, u32[]{:S(2)}, u32[]{:S(2)}) collective-permute-start(bf16[2,512,384]{2,1,0:T(8,128)(2,1)} %collective-permute-done.6.refs_1_), channel_id=1, source_target_pairs={{8,0},{16,8},{24,16},{9,1},{17,9},{25,17},{10,2},{18,10},{26,18},{... | collective-permute-start | bytes 2359304 | tf_op jit(solution)/shard_map/ppermute | solution.py:24
  52.2 20.3 %collective-permute-start.11 = (bf16[2,512,384]{2,1,0:T(8,128)(2,1)}, bf16[2,512,384]{2,1,0:T(8,128)(2,1)S(1)}, u32[]{:S(2)}, u32[]{:S(2)}) collective-permute-start(bf16[2,512,384]{2,1,0:T(8,128)(2,1)} %collective-permute-done.6.refs_1_), channel_id=1, source_target_pairs={{0,8},{8,16},{16,24},{1,9},{9,17},{17,25},{2,10},{10,18},{18,26},{... | collective-permute-start | bytes 2359304 | tf_op jit(solution)/shard_map/ppermute | solution.py:24
  56.9 58.2 %collective-permute-start.5 = (bf16[2,1000,384]{2,1,0:T(8,128)(2,1)S(1)}, bf16[2,1000,384]{2,1,0:T(8,128)(2,1)}, u32[]{:S(2)}, u32[]{:S(2)}) collective-permute-start(bf16[2,1000,384]{2,1,0:T(8,128)(2,1)S(1)} %collective-permute-done), channel_id=1, source_target_pairs={{0,1},{1,0},{2,3},{3,2},{4,5},{5,4},{6,7},{7,6},{8,9},{9,8},{10,11... | collective-permute-start | bytes 4608008 | tf_op jit(solution)/shard_map/ppermute | solution.py:19
  58.0 57.1 %collective-permute-start.4 = (bf16[2,1000,384]{2,1,0:T(8,128)(2,1)}, bf16[2,1000,384]{2,1,0:T(8,128)(2,1)}, u32[]{:S(2)}, u32[]{:S(2)}) collective-permute-start(bf16[2,1000,384]{2,1,0:T(8,128)(2,1)} %get-tuple-element.19), channel_id=1, source_target_pairs={{0,1},{1,0},{2,3},{3,2},{4,5},{5,4},{6,7},{7,6},{8,9},{9,8},{10,11... | collective-permute-start | bytes 4608008 | tf_op jit(solution)/shard_map/ppermute | solution.py:19
  62.3 52.9 %collective-permute-start.7 = (bf16[2,1000,384]{2,1,0:T(8,128)(2,1)}, bf16[2,1000,384]{2,1,0:T(8,128)(2,1)}, u32[]{:S(2)}, u32[]{:S(2)}) collective-permute-start(bf16[2,1000,384]{2,1,0:T(8,128)(2,1)} %pad_maximum_fusion.2), channel_id=1, source_target_pairs={{0,1},{1,0},{2,3},{3,2},{4,5},{5,4},{6,7},{7,6},{8,9},{9,8},{10,11... | collective-permute-start | bytes 4608008 | tf_op jit(solution)/shard_map/ppermute | solution.py:19
  69.2 17.1 %collective-permute-start.8 = (bf16[1,1000,384]{2,1,0:T(8,128)(2,1)}, bf16[1,1000,384]{2,1,0:T(8,128)(2,1)}, u32[]{:S(2)}, u32[]{:S(2)}) collective-permute-start(bf16[1,1000,384]{2,1,0:T(8,128)(2,1)} %fusion.13), channel_id=1, source_target_pairs={{0,2},{1,3},{2,0},{3,1},{4,6},{5,7},{6,4},{7,5},{8,10},{9,11},{10,... | collective-permute-start | bytes 2304008 | tf_op jit(solution)/shard_map/ppermute | solution.py:19
  72.5 16.9 %collective-permute-start.9 = (bf16[1,1000,384]{2,1,0:T(8,128)(2,1)}, bf16[1,1000,384]{2,1,0:T(8,128)(2,1)}, u32[]{:S(2)}, u32[]{:S(2)}) collective-permute-start(bf16[1,1000,384]{2,1,0:T(8,128)(2,1)} %slice.111), channel_id=1, source_target_pairs={{0,4},{4,0},{1,5},{5,1},{2,6},{6,2},{3,7},{7,3},{8,12},{12,8},{9,1... | collective-permute-start | bytes 2304008 | tf_op jit(solution)/shard_map/ppermute | solution.py:19
  75.2 15.5 %copy-start.1 = (bf16[2,3,112,112]{3,2,1,0:T(8,128)(2,1)S(1)}, bf16[2,3,112,112]{3,2,1,0:T(8,128)(2,1)}, u32[]{:S(2)}) copy-start(bf16[2,3,112,112]{3,2,1,0:T(8,128)(2,1)} %pad_maximum_fusion.12.refs_9_) | copy-start | bytes 451588
  75.2 15.5 %copy-start.2 = (bf16[160,480]{1,0:T(8,128)(2,1)S(1)}, bf16[160,480]{1,0:T(8,128)(2,1)}, u32[]{:S(2)}) copy-start(bf16[160,480]{1,0:T(8,128)(2,1)} %fusion.1.refs_8_) | copy-start | bytes 460804
  75.3 15.5 %copy-start.4 = (bf16[2,512,384]{2,1,0:T(8,128)(2,1)S(1)}, bf16[2,512,384]{2,1,0:T(8,128)(2,1)}, u32[]{:S(2)}) copy-start(bf16[2,512,384]{2,1,0:T(8,128)(2,1)} %copy-done.3) | copy-start | bytes 2359300
  75.3 15.5 %copy-start.6 = (bf16[2,512,384]{2,1,0:T(8,128)(2,1)S(1)}, bf16[2,512,384]{2,1,0:T(8,128)(2,1)}, u32[]{:S(2)}) copy-start(bf16[2,512,384]{2,1,0:T(8,128)(2,1)} %copy-done.5) | copy-start | bytes 2359300
  90.6 24.6 %collective-permute-start.10 = (bf16[2,1000,384]{2,1,0:T(8,128)(2,1)S(1)}, bf16[2,1000,384]{2,1,0:T(8,128)(2,1)S(1)}, u32[]{:S(2)}, u32[]{:S(2)}) collective-permute-start(bf16[2,1000,384]{2,1,0:T(8,128)(2,1)S(1)} %constant_dynamic-update-slice_fusion), channel_id=1, source_target_pairs={{0,1},{1,0},{2,3},{3,2},{4,5},{5,4},{6,7},{7,6},{8,9},{9,8},{10,11... | collective-permute-start | bytes 4608008 | tf_op jit(solution)/shard_map/ppermute | solution.py:19
  124.5 35.1 %collective-permute-start.23 = (bf16[192,384]{1,0:T(8,128)(2,1)S(1)}, bf16[192,384]{1,0:T(8,128)(2,1)S(1)}, u32[]{:S(2)}, u32[]{:S(2)}) collective-permute-start(bf16[192,384]{1,0:T(8,128)(2,1)S(1)} %get-tuple-element.65), channel_id=1, source_target_pairs={{0,3},{1,11},{2,19},{3,27},{8,2},{9,10},{10,18},{11,26},{16,1},{17... | collective-permute-start | bytes 442376 | tf_op jit(solution)/shard_map/ppermute | solution.py:449
  135.8 23.8 %collective-permute-start.22 = (bf16[192,384]{1,0:T(8,128)(2,1)S(1)}, bf16[192,384]{1,0:T(8,128)(2,1)S(1)}, u32[]{:S(2)}, u32[]{:S(2)}) collective-permute-start(bf16[192,384]{1,0:T(8,128)(2,1)S(1)} %get-tuple-element.66), channel_id=1, source_target_pairs={{0,2},{1,10},{2,18},{3,26},{8,3},{9,11},{10,19},{11,27},{16,0},{17... | collective-permute-start | bytes 442376 | tf_op jit(solution)/shard_map/ppermute | solution.py:449
  136.4 23.3 %collective-permute-start.21 = (bf16[192,384]{1,0:T(8,128)(2,1)S(1)}, bf16[192,384]{1,0:T(8,128)(2,1)S(1)}, u32[]{:S(2)}, u32[]{:S(2)}) collective-permute-start(bf16[192,384]{1,0:T(8,128)(2,1)S(1)} %get-tuple-element.67), channel_id=1, source_target_pairs={{0,1},{1,9},{2,17},{3,25},{8,0},{9,8},{10,16},{11,24},{16,3},{17,1... | collective-permute-start | bytes 442376 | tf_op jit(solution)/shard_map/ppermute | solution.py:449
  136.4 24.3 %collective-permute-start.20 = (bf16[192,384]{1,0:T(8,128)(2,1)S(1)}, bf16[192,384]{1,0:T(8,128)(2,1)S(1)}, u32[]{:S(2)}, u32[]{:S(2)}) collective-permute-start(bf16[192,384]{1,0:T(8,128)(2,1)S(1)} %get-tuple-element.64), channel_id=1, source_target_pairs={{0,0},{1,8},{2,16},{3,24},{8,1},{9,9},{10,17},{11,25},{16,2},{17,1... | collective-permute-start | bytes 442376 | tf_op jit(solution)/shard_map/ppermute | solution.py:449
  160.8 6.9 %collective-permute-start.30 = (bf16[96,384]{1,0:T(8,128)(2,1)S(1)}, bf16[96,384]{1,0:T(8,128)(2,1)S(1)}, u32[]{:S(2)}, u32[]{:S(2)}) collective-permute-start(bf16[96,384]{1,0:T(8,128)(2,1)S(1)} %get-tuple-element.76), channel_id=1, source_target_pairs={{0,2},{1,3},{2,0},{3,1},{4,6},{5,7},{6,4},{7,5},{8,10},{9,11},{10,... | collective-permute-start | bytes 221192 | tf_op jit(solution)/shard_map/ppermute | solution.py:19
  161.0 64.7 %collective-permute-start.17 = (bf16[3,192,384]{2,1,0:T(8,128)(2,1)S(1)}, bf16[3,192,384]{2,1,0:T(8,128)(2,1)S(1)}, u32[]{:S(2)}, u32[]{:S(2)}) collective-permute-start(bf16[3,192,384]{2,1,0:T(8,128)(2,1)S(1)} %get-tuple-element.47), channel_id=1, source_target_pairs={{0,3},{1,11},{2,19},{3,27},{8,2},{9,10},{10,18},{11,26},{16,1},{17... | collective-permute-start | bytes 1327112 | tf_op jit(solution)/shard_map/ppermute | solution.py:449
  163.2 12.2 %collective-permute-start.26 = (bf16[96,384]{1,0:T(8,128)(2,1)S(1)}, bf16[96,384]{1,0:T(8,128)(2,1)S(1)}, u32[]{:S(2)}, u32[]{:S(2)}) collective-permute-start(bf16[96,384]{1,0:T(8,128)(2,1)S(1)} %get-tuple-element.77), channel_id=1, source_target_pairs={{0,24},{8,16},{16,8},{24,0},{1,25},{9,17},{17,9},{25,1},{2,26},{10... | collective-permute-start | bytes 221192 | tf_op jit(solution)/shard_map/ppermute | solution.py:19
  163.2 29.2 %collective-permute-start.25 = (bf16[96,384]{1,0:T(8,128)(2,1)S(1)}, bf16[96,384]{1,0:T(8,128)(2,1)S(1)}, u32[]{:S(2)}, u32[]{:S(2)}) collective-permute-start(bf16[96,384]{1,0:T(8,128)(2,1)S(1)} %get-tuple-element.77), channel_id=1, source_target_pairs={{0,16},{8,24},{16,0},{24,8},{1,17},{9,25},{17,1},{25,9},{2,18},{10... | collective-permute-start | bytes 221192 | tf_op jit(solution)/shard_map/ppermute | solution.py:19
  164.1 28.4 %collective-permute-start.24 = (bf16[96,384]{1,0:T(8,128)(2,1)S(1)}, bf16[96,384]{1,0:T(8,128)(2,1)S(1)}, u32[]{:S(2)}, u32[]{:S(2)}) collective-permute-start(bf16[96,384]{1,0:T(8,128)(2,1)S(1)} %get-tuple-element.77), channel_id=1, source_target_pairs={{0,8},{8,0},{16,24},{24,16},{1,9},{9,1},{17,25},{25,17},{2,10},{10... | collective-permute-start | bytes 221192 | tf_op jit(solution)/shard_map/ppermute | solution.py:19
  168.3 24.7 %collective-permute-start.33 = (bf16[2,96,384]{2,1,0:T(8,128)(2,1)}, bf16[2,96,384]{2,1,0:T(8,128)(2,1)}, u32[]{:S(2)}, u32[]{:S(2)}) collective-permute-start(bf16[2,96,384]{2,1,0:T(8,128)(2,1)} %get-tuple-element.73), channel_id=1, source_target_pairs={{0,24},{8,16},{16,8},{24,0},{1,25},{9,17},{17,9},{25,1},{2,26},{10... | collective-permute-start | bytes 442376 | tf_op jit(solution)/shard_map/ppermute | solution.py:19
  175.4 26.0 %collective-permute-start.32 = (bf16[2,96,384]{2,1,0:T(8,128)(2,1)}, bf16[2,96,384]{2,1,0:T(8,128)(2,1)}, u32[]{:S(2)}, u32[]{:S(2)}) collective-permute-start(bf16[2,96,384]{2,1,0:T(8,128)(2,1)} %get-tuple-element.73), channel_id=1, source_target_pairs={{0,16},{8,24},{16,0},{24,8},{1,17},{9,25},{17,1},{25,9},{2,18},{10... | collective-permute-start | bytes 442376 | tf_op jit(solution)/shard_map/ppermute | solution.py:19
  192.5 11.4 %collective-permute-start.31 = (bf16[2,96,384]{2,1,0:T(8,128)(2,1)}, bf16[2,96,384]{2,1,0:T(8,128)(2,1)}, u32[]{:S(2)}, u32[]{:S(2)}) collective-permute-start(bf16[2,96,384]{2,1,0:T(8,128)(2,1)} %get-tuple-element.73), channel_id=1, source_target_pairs={{0,8},{8,0},{16,24},{24,16},{1,9},{9,1},{17,25},{25,17},{2,10},{10... | collective-permute-start | bytes 442376 | tf_op jit(solution)/shard_map/ppermute | solution.py:19
  192.6 32.8 %collective-permute-start.27 = (bf16[4,96,384]{2,1,0:T(8,128)(2,1)S(1)}, bf16[4,96,384]{2,1,0:T(8,128)(2,1)S(1)}, u32[]{:S(2)}, u32[]{:S(2)}) collective-permute-start(bf16[4,96,384]{2,1,0:T(8,128)(2,1)S(1)} %get-tuple-element.69), channel_id=1, source_target_pairs={{0,4},{4,0},{1,5},{5,1},{2,6},{6,2},{3,7},{7,3},{8,12},{12,8},{9,1... | collective-permute-start | bytes 884744 | tf_op jit(solution)/shard_map/ppermute | solution.py:19
  193.0 33.7 %collective-permute-start.16 = (bf16[3,192,384]{2,1,0:T(8,128)(2,1)S(1)}, bf16[3,192,384]{2,1,0:T(8,128)(2,1)S(1)}, u32[]{:S(2)}, u32[]{:S(2)}) collective-permute-start(bf16[3,192,384]{2,1,0:T(8,128)(2,1)S(1)} %get-tuple-element.48), channel_id=1, source_target_pairs={{0,2},{1,10},{2,18},{3,26},{8,3},{9,11},{10,19},{11,27},{16,0},{17... | collective-permute-start | bytes 1327112 | tf_op jit(solution)/shard_map/ppermute | solution.py:449
  201.4 25.3 %collective-permute-start.15 = (bf16[3,192,384]{2,1,0:T(8,128)(2,1)S(1)}, bf16[3,192,384]{2,1,0:T(8,128)(2,1)S(1)}, u32[]{:S(2)}, u32[]{:S(2)}) collective-permute-start(bf16[3,192,384]{2,1,0:T(8,128)(2,1)S(1)} %get-tuple-element.49), channel_id=1, source_target_pairs={{0,1},{1,9},{2,17},{3,25},{8,0},{9,8},{10,16},{11,24},{16,3},{17,1... | collective-permute-start | bytes 1327112 | tf_op jit(solution)/shard_map/ppermute | solution.py:449
  203.8 55.3 %collective-permute-start.14 = (bf16[3,192,384]{2,1,0:T(8,128)(2,1)S(1)}, bf16[3,192,384]{2,1,0:T(8,128)(2,1)S(1)}, u32[]{:S(2)}, u32[]{:S(2)}) collective-permute-start(bf16[3,192,384]{2,1,0:T(8,128)(2,1)S(1)} %get-tuple-element.46), channel_id=1, source_target_pairs={{0,0},{1,8},{2,16},{3,24},{8,1},{9,9},{10,17},{11,25},{16,2},{17,1... | collective-permute-start | bytes 1327112 | tf_op jit(solution)/shard_map/ppermute | solution.py:449
  225.4 34.0 %collective-permute-start.34 = (bf16[4,2,96,384]{3,2,1,0:T(8,128)(2,1)S(1)}, bf16[4,2,96,384]{3,2,1,0:T(8,128)(2,1)S(1)}, u32[]{:S(2)}, u32[]{:S(2)}) collective-permute-start(bf16[4,2,96,384]{3,2,1,0:T(8,128)(2,1)S(1)} %get-tuple-element.61), channel_id=1, source_target_pairs={{0,4},{4,0},{1,5},{5,1},{2,6},{6,2},{3,7},{7,3},{8,12},{12,8},{9,1... | collective-permute-start | bytes 1769480 | tf_op jit(solution)/shard_map/ppermute | solution.py:19
  225.8 34.8 %collective-permute-start.28 = (bf16[2,4,96,384]{3,2,1,0:T(8,128)(2,1)S(1)}, bf16[2,4,96,384]{3,2,1,0:T(8,128)(2,1)S(1)}, u32[]{:S(2)}, u32[]{:S(2)}) collective-permute-start(bf16[2,4,96,384]{3,2,1,0:T(8,128)(2,1)S(1)} %get-tuple-element.63), channel_id=1, source_target_pairs={{0,2},{1,3},{2,0},{3,1},{4,6},{5,7},{6,4},{7,5},{8,10},{9,11},{10,... | collective-permute-start | bytes 1769480 | tf_op jit(solution)/shard_map/ppermute | solution.py:19
  260.6 18.7 %collective-permute-start.35 = (bf16[2,4,2,96,384]{4,3,2,1,0:T(8,128)(2,1)}, bf16[2,4,2,96,384]{4,3,2,1,0:T(8,128)(2,1)}, u32[]{:S(2)}, u32[]{:S(2)}) collective-permute-start(bf16[2,4,2,96,384]{4,3,2,1,0:T(8,128)(2,1)} %get-tuple-element.51), channel_id=1, source_target_pairs={{0,1},{1,0},{2,3},{3,2},{4,5},{5,4},{6,7},{7,6},{8,9},{9,8},{10,11... | collective-permute-start | bytes 3538952 | tf_op jit(solution)/shard_map/ppermute | solution.py:19
  261.8 19.0 %collective-permute-start.29 = (bf16[2,2,4,96,384]{4,3,2,1,0:T(8,128)(2,1)}, bf16[2,2,4,96,384]{4,3,2,1,0:T(8,128)(2,1)}, u32[]{:S(2)}, u32[]{:S(2)}) collective-permute-start(bf16[2,2,4,96,384]{4,3,2,1,0:T(8,128)(2,1)} %get-tuple-element.53), channel_id=1, source_target_pairs={{0,1},{1,0},{2,3},{3,2},{4,5},{5,4},{6,7},{7,6},{8,9},{9,8},{10,11... | collective-permute-start | bytes 3538952 | tf_op jit(solution)/shard_map/ppermute | solution.py:19
  263.1 12.5 %collective-permute-start.19 = (bf16[192,192]{1,0:T(8,128)(2,1)}, bf16[192,192]{1,0:T(8,128)(2,1)}, u32[]{:S(2)}, u32[]{:S(2)}) collective-permute-start(bf16[192,192]{1,0:T(8,128)(2,1)} %get-tuple-element.78), channel_id=1, source_target_pairs={{0,4},{1,12},{2,20},{3,28},{4,0},{5,8},{6,16},{7,24},{8,5},{9,13},... | collective-permute-start | bytes 221192 | tf_op jit(solution)/shard_map/ppermute | solution.py:492
  263.3 12.3 %collective-permute-start.18 = (bf16[192,192]{1,0:T(8,128)(2,1)S(1)}, bf16[192,192]{1,0:T(8,128)(2,1)}, u32[]{:S(2)}, u32[]{:S(2)}) collective-permute-start(bf16[192,192]{1,0:T(8,128)(2,1)S(1)} %get-tuple-element.79), channel_id=1, source_target_pairs={{0,0},{1,8},{2,16},{3,24},{4,4},{5,12},{6,20},{7,28},{8,1},{9,9},{... | collective-permute-start | bytes 221192 | tf_op jit(solution)/shard_map/ppermute | solution.py:492
  (19 other events, 143.9 us)

commit v2 on v1

--- a/solution.py
+++ b/solution.py
@@ -82,27 +82,52 @@
     return copies
 
 
-def correlation_kernel(levels, meta, *refs):
-    lefts, out, held, turned, sems = refs[:-4], refs[-4], refs[-3], refs[-2], refs[-1]
+def correlation_kernel(share, meta, *refs):
+    refs, (out, held, turned, sems) = refs[:-4], refs[-4:]
+    groups, half, width = out.shape
+    lefts, before = refs[:groups], refs[groups:]
     copies = load_left(lefts, held, sems)
-    groups = len(lefts) // 2
-    half, width = out.shape[1:]
     first, apart = meta[0] == 0, meta[1]
-    for copy in copies:
+    copies[0].wait()
+    own = held[0]
+    turned[...] = jnp.where(first, own[:, :half], own[:, half:]).T
+    for copy in copies[1:]:
         copy.wait()
-    for side in range(2):
-        own = held[side * groups]
-        turned[side] = jnp.where(first, own[:, :half], own[:, half:]).T
 
     def per_group(q, carry):
-        total = matmul(turned[0], held[q]) + matmul(turned[1], held[groups + q])
-        rows = lax.broadcasted_iota(jnp.int32, (half, width), 0) + jnp.where(first, 0, half)
-        columns = lax.broadcasted_iota(jnp.int32, (half, width), 1)
-        share = jnp.where((rows == columns) & (q == 0), 1.0 / levels, 0.0)
-        out[q ^ apart] = (total - share).astype(bf16)
+        total = matmul(turned[...], held[q])
+        if before:
+            rows = lax.broadcasted_iota(jnp.int32, (half, width), 0) + jnp.where(first, 0, half)
+            columns = lax.broadcasted_iota(jnp.int32, (half, width), 1)
+            total = total + before[0][q ^ apart] - jnp.where((rows == columns) & (q == 0), share, 0.0)
+        out[q ^ apart] = total.astype(out.dtype)
         return carry
 
     lax.fori_loop(0, groups, per_group, 0)
+
+
+def box_correlation(share, meta, lefts, before, half):
+    depth, width = lefts[0].shape
+    vmem = pl.BlockSpec(memory_space=pltpu.VMEM)
+    extra = [] if before is None else [before]
+    return pl.pallas_call(
+        functools.partial(correlation_kernel, share),
+        out_shape=jax.ShapeDtypeStruct((len(lefts), half, width), f32 if before is None else bf16),
+        in_specs=[pl.BlockSpec(memory_space=pltpu.SMEM)]
+        + [pl.BlockSpec(memory_space=pl.ANY)] * len(lefts)
+        + [vmem] * len(extra),
+        out_specs=vmem,
+        scratch_shapes=[
+            pltpu.VMEM((len(lefts), depth, width), bf16),
+            pltpu.VMEM((half, depth), bf16),
+            pltpu.SemaphoreType.DMA((len(lefts),)),
+        ],
+        compiler_params=params(32),
+        cost_estimate=pl.CostEstimate(
+            flops=2 * len(lefts) * depth * width * half, bytes_accessed=2 * len(lefts) * depth * width, transcendentals=0
+        ),
+        name="correlation",
+    )(meta, *lefts, *extra)
 
 
 def fock_kernel(meta, *refs):
@@ -131,33 +156,32 @@
     lax.fori_loop(0, groups, per_group, 0)
 
 
-def row_products(kernel, name, meta, lefts, right, shape, tall):
+def fock_rows(meta, lefts, right):
     depth, width = lefts[0].shape
-    smem = pl.BlockSpec(memory_space=pltpu.SMEM)
+    tall = right.shape[-1]
     anywhere = pl.BlockSpec(memory_space=pl.ANY)
-    scratch = [pltpu.VMEM((len(lefts), depth, width), bf16)]
-    if right is not None:
-        scratch.append(pltpu.VMEM(right.shape, bf16))
-    scratch += [pltpu.VMEM((2, tall, depth), bf16), pltpu.SemaphoreType.DMA((len(lefts) + 1,))]
-    operands = list(lefts) + ([] if right is None else [right])
     return pl.pallas_call(
-        kernel,
-        out_shape=jax.ShapeDtypeStruct(shape, bf16),
-        in_specs=[smem] + [anywhere] * len(operands),
+        fock_kernel,
+        out_shape=jax.ShapeDtypeStruct((len(lefts) // 2, 3, tall // 3, width), bf16),
+        in_specs=[pl.BlockSpec(memory_space=pltpu.SMEM)] + [anywhere] * (len(lefts) + 1),
         out_specs=pl.BlockSpec(memory_space=pltpu.VMEM),
-        scratch_shapes=scratch,
+        scratch_shapes=[
+            pltpu.VMEM((len(lefts), depth, width), bf16),
+            pltpu.VMEM(right.shape, bf16),
+            pltpu.VMEM((2, tall, depth), bf16),
+            pltpu.SemaphoreType.DMA((len(lefts) + 1,)),
+        ],
         compiler_params=params(40),
         cost_estimate=pl.CostEstimate(
             flops=2 * len(lefts) * depth * width * tall, bytes_accessed=2 * len(lefts) * depth * width, transcendentals=0
         ),
-        name=name,
-    )(meta, *operands)
+        name="fock",
+    )(meta, *lefts, right)
 
 
 def root_kernel(meta, top, low, offset, root, whole, rows_f, cols_b):
     level, pair, orb = meta[0], meta[1], meta[2]
-    fine, width = top.shape[4:]
-    coarse = 2 * fine
+    coarse, width = top.shape[4:]
     side = whole.shape[0]
     groups = side // width
     for core in range(2):
@@ -166,8 +190,9 @@
             for z in range(top.shape[3]):
                 for y in range(PAIR):
                     start = ((level ^ z) * PAIR + (pair ^ y)) * coarse
-                    whole[pl.ds(pl.multiple_of(start, fine), fine), lanes] = top[core, far, y, z]
-                    whole[pl.ds(pl.multiple_of(start + fine, fine), fine), lanes] = low[core, y, z, far]
+                    whole[pl.ds(pl.multiple_of(start, coarse), coarse), lanes] = top[core, far, y, z]
+                    start = ((level ^ (z + top.shape[3])) * PAIR + (pair ^ y)) * coarse
+                    whole[pl.ds(pl.multiple_of(start, coarse), coarse), lanes] = low[core, y, far, z]
     row0 = pl.multiple_of((level * PAIR + pair) * coarse, coarse)
     own_lanes = pl.ds(pl.multiple_of(orb * width, width), width)
     rows = whole[pl.ds(row0, coarse), :]
@@ -376,8 +401,10 @@
     other_pot = swap(later_pot, "pair", 1)
     matrices = block_matrices(deriv_blocks)
 
-    far, beside_rest, lower, upper, active, matrices = lax.optimization_barrier(
-        (far, beside_rest, lower, upper, active, matrices)
+    far, beside, beside_rest, lower, upper, lower_beside, upper_beside, other_pot, active, matrices = (
+        lax.optimization_barrier(
+            (far, beside, beside_rest, lower, upper, lower_beside, upper_beside, other_pot, active, matrices)
+        )
     )
 
     def unfold(packed):
@@ -388,16 +415,11 @@
         [jnp.where(first, beside_half, rest_half), jnp.where(first, rest_half, beside_half)], axis=2
     )
     cut = slots // 2
-    far_beside = {
-        q: jnp.concatenate([swap(beside_all[:cut], "orb", q), swap(far[q][cut:], "pair", 1)]) for q in far
-    }
+    cross = {q: (swap(beside_all[:cut], "orb", q), swap(far[q][cut:], "pair", 1)) for q in far}
     left_own = {0: active, 1: swap(active, "orb", 1), **far}
-    left_beside = {0: beside_all, 1: swap(beside_all, "orb", 1), **far_beside}
+    left_beside = {0: beside_all, 1: swap(beside_all, "orb", 1)}
     for q in far:
         left_own[q + 1] = swap(far[q], "orb", 1)
-        left_beside[q + 1] = swap(far_beside[q], "orb", 1)
-    flat = lambda block: block.reshape(slots * coefficients, block.shape[-1])
-    lefts = [flat(left_own[q]) for q in groups] + [flat(left_beside[q]) for q in groups]
 
     def facts_of(packed):
         return packed[:, fold, : facts.shape[1]].astype(f32).astype(jnp.int32)
@@ -442,12 +464,9 @@
     def natural(blocks):
         return jnp.concatenate([lax.dynamic_index_in_dim(blocks, orb ^ j, keepdims=False) for j in groups], axis=1)
 
-    def deliver(blocks):
-        got = []
-        for step in groups:
-            to = [(z * orb_count + o, o * orb_count + (z ^ step)) for z in range(level_count) for o in groups]
-            got.append(lax.ppermute(blocks[step], ("lvl", "orb"), to))
-        return got
+    def deliver(block, step):
+        to = [(z * orb_count + o, o * orb_count + (z ^ step)) for z in range(level_count) for o in groups]
+        return lax.ppermute(block, ("lvl", "orb"), to)
 
     def own_block(strip):
         strip = lax.all_gather(lax.psum(strip, "lvl"), ("orb", "pair"), axis=0, tiled=True)
@@ -460,12 +479,19 @@
     parts = [mine, beside, lower, lower_beside, upper, upper_beside]
     right = kinetic(parts, pot, matrices, table, scale, edge, coefficients)
 
-    shape = (orb_count, half, own_width)
-    blocks = row_products(
-        functools.partial(correlation_kernel, level_count), "correlation", meta, lefts, None, shape, half
-    )
+    cross, right, meta = lax.optimization_barrier((cross, right, meta))
+    for q in far:
+        left_beside[q] = jnp.concatenate(cross[q])
+        left_beside[q + 1] = swap(left_beside[q], "orb", 1)
+    flat = lambda block: block.reshape(slots * coefficients, block.shape[-1])
+    lefts_own = [flat(left_own[q]) for q in groups]
+    lefts_beside = [flat(left_beside[q]) for q in groups]
+
+    share = 1.0 / level_count
+    blocks = box_correlation(share, meta, lefts_own, None, half)
+    blocks = box_correlation(share, meta, lefts_beside, blocks, half)
     if square_grid:
-        offset = sum(block.astype(f32) for block in deliver(blocks))
+        offset = sum(deliver(blocks[step], step).astype(f32) for step in groups)
     else:
         offset = own_block(natural(blocks).astype(f32))
     row_ids = row0 + jnp.arange(box_rows, dtype=jnp.int32)
@@ -474,10 +500,21 @@
     small = offset.astype(bf16)
 
     right = right.reshape(2, slots * coefficients, 3 * half)
-    shape = (orb_count, 3, half, own_width)
-    blocks = row_products(fock_kernel, "fock", meta, lefts, right, shape, 3 * half)
+    blocks = fock_rows(meta, lefts_own + lefts_beside, right)
     if square_grid:
-        sums = sum(block.astype(f32) for block in deliver(blocks))
+        pieces = [small] + [swap(small, "lvl", z) for z in range(1, level_count)]
+        early = orb_count // 2
+        pieces, blocks = lax.optimization_barrier((pieces, blocks))
+        far_of = range(0, orb_count, 2)
+        top = jnp.stack(pieces[: level_count // 2])
+        low = jnp.stack(pieces[level_count // 2 :])
+        top = spread(spread(top, "pair", (0, 1)), "orb", far_of)
+        low = spread(spread(low, "orb", far_of), "pair", (0, 1))
+        got = [deliver(blocks[step], step) for step in range(early)]
+        top, low, blocks = lax.optimization_barrier((top, low, blocks))
+        got += [deliver(blocks[step], step) for step in range(early, orb_count)]
+        top, low = spread(top, "orb", (0, 1)), spread(low, "orb", (0, 1))
+        sums = sum(block.astype(f32) for block in got)
         share = sums[2].astype(bf16)
         pieces = []
         for over in range(PAIR):
@@ -500,10 +537,6 @@
         fock = fock + lax.dynamic_slice_in_dim(share, row0, box_rows, axis=1).T
 
     if square_grid:
-        levels_of, far_of = range(level_count), range(0, orb_count, 2)
-        top, low = small[: box_rows // 2], small[box_rows // 2 :]
-        top = spread(spread(spread(spread(top, "lvl", levels_of), "pair", (0, 1)), "orb", far_of), "orb", (0, 1))
-        low = spread(spread(spread(spread(low, "orb", far_of), "lvl", levels_of), "pair", (0, 1)), "orb", (0, 1))
         inverse_root = root_of(jnp.stack([level, pair, orb]).astype(jnp.int32), top, low, offset, all_width)
     else:
         gathered = lax.all_gather(small, "orb", axis=1, tiled=True)

time: 292 us -> 307 us (1.051)
  waiting for transfers between devices: 83.1 us -> 107 us
  starting transfers between devices: 96.3 us -> 79.4 us
  Pallas kernels: 61.4 us -> 68.1 us
    ppermute x8, starting transfers between devices: 51.4 us -> 15 us  [deliver(): return lax.ppermute(block, ('lvl', 'orb'), to)]
    ppermute x2, starting transfers between devices: 5.41 us -> 32 us  [body(): pieces.append(lax.ppermute(sent, BOX + ('orb',), to).astype(f32).T)]
    ppermute x8, waiting for transfers between devices: 33.5 us -> 45.9 us  [deliver(): return lax.ppermute(block, ('lvl', 'orb'), to)]
    ppermute x22 -> x19, starting transfers between devices: 28.6 us -> 21.1 us  [swap(): return lax.ppermute(value, axis, [(i, i ^ bit) for i in range(count)])]
    ppermute x22 -> x19, waiting for transfers between devices: 37.5 us -> 44.6 us  [swap(): return lax.ppermute(value, axis, [(i, i ^ bit) for i in range(count)])]
    ppermute x4, waiting for transfers between devices: 7.13 us -> 11.6 us  [shift(): lax.ppermute(value, axis, [(i, i + step) for i in range(count) if 0 <= i...]
    pallas_call x1, Pallas kernels: 24.4 us -> 28.6 us  [kinetic(): pl.pallas_call(functools.partial(kinetic_kernel, edge, slots), out_shape=...]
    another operation x8, other arithmetic: 7.57 us -> 3.66 us  [spread(): return jnp.stack([swap(value, axis, bit) if bit else value for bit in bits])]
  transfers between devices with their start and end apart: 36 -> 33, of which waited for: 9 -> 11; matrix products, arithmetic and copies ran while one was open for 14% -> 11% of each run, Pallas kernels for 14% -> 17%
where the time goes in v2:
time: 307 us
  waiting for transfers between devices  107 us (35%)
  starting transfers between devices  79.4 us (26%)
  Pallas kernels  68.1 us (22%)
  other arithmetic  23.5 us (8%)
  local copies, waits for them, and re-layouts  20.9 us (7%)
  matrix products  5.73 us (2%)
    ppermute x8, waiting for transfers between devices, deliver(): return lax.ppermute(block, ('lvl', 'orb'), to)  45.9 us
    ppermute x19, waiting for transfers between devices, swap(): return lax.ppermute(value, axis, [(i, i ^ bit) for i in range(count)])  44.6 us
    ppermute x2, starting transfers between devices, body(): pieces.append(lax.ppermute(sent, BOX + ('orb',), to).astype(f32).T)  32 us
    pallas_call x1, Pallas kernels, kinetic(): pl.pallas_call(functools.partial(kinetic_kernel, edge, slots), out_shape=...  28.6 us
    ppermute x19, starting transfers between devices, swap(): return lax.ppermute(value, axis, [(i, i ^ bit) for i in range(count)])  21.1 us
    pallas_call x1, Pallas kernels, fock_rows(): pl.pallas_call(fock_kernel, out_shape=jax.ShapeDtypeStruct((len(lefts) //...  17.9 us
    ppermute x8, starting transfers between devices, deliver(): return lax.ppermute(block, ('lvl', 'orb'), to)  15 us
    ppermute x4, waiting for transfers between devices, shift(): lax.ppermute(value, axis, [(i, i + step) for i in range(count) if 0 <= i...  11.6 us
  transfers between devices with their start and end apart: 33, of which 11 were waited for; matrix products, arithmetic and copies ran while one was open for 11% of the time, Pallas kernels for 17%

profile of v2, /device:TPU:2, one launch (start us, length us, event | category | flops | bytes accessed | tf_op | source)
XLA Modules:
  0.0 306.7 jit_solution(13424830758214034151)
XLA Ops:
  4.1 1.4 copy-done
  5.5 2.8 pack.1
  8.4 1.6 collective-permute-start.2
  9.9 4.4 %collective-permute-start.3 = (bf16[2,512,384]{2,1,0:T(8,128)(2,1)}, bf16[2,512,384]{2,1,0:T(8,128)(2,1)}, u32[]{:S(2)}, u32[]{:S(2)}) collective-permute-start(bf16[2,512,384]{2,1,0:T(8,128)(2,1)} %get-tuple-element.36.refs_0_), channel_id=1, source_target_pairs={{0,8},{8,16},{16,24},{1,9},{9,17},{17,25},{2,10},{10,18},{18,26},{... | collective-permute-start | bytes 2359304 | tf_op jit(solution)/shard_map/ppermute | solution.py:24
  22.2 1.4 fusion.9
  23.7 21.1 %collective-permute-done.1.refs_1_ = bf16[2,512,384]{2,1,0:T(8,128)(2,1)S(1)} collective-permute-done((bf16[2,512,384]{2,1,0:T(8,128)(2,1)}, bf16[2,512,384]{2,1,0:T(8,128)(2,1)S(1)}, u32[]{:S(2)}, u32[]{:S(2)}) %collective-permute-start.1) | collective-permute-done | bytes 786464 | tf_op jit(solution)/shard_map/ppermute | solution.py:19
  44.8 4.4 %collective-permute-start.5 = (bf16[2,512,384]{2,1,0:T(8,128)(2,1)S(1)}, bf16[2,512,384]{2,1,0:T(8,128)(2,1)}, u32[]{:S(2)}, u32[]{:S(2)}) collective-permute-start(bf16[2,512,384]{2,1,0:T(8,128)(2,1)S(1)} %collective-permute-done.1.refs_1_), channel_id=1, source_target_pairs={{0,8},{8,16},{16,24},{1,9},{9,17},{17,25},{2,10},{10,18},{18,26},{... | collective-permute-start | bytes 2359304 | tf_op jit(solution)/shard_map/ppermute | solution.py:24
  49.1 1.3 collective-permute-start.6
  51.2 1.3 fusion.refs_10_
  53.8 1.6 collective-permute-start.7
  56.2 1.5 collective-permute-done.7
  57.7 6.5 %collective-permute-done.5.refs_3_ = bf16[2,512,384]{2,1,0:T(8,128)(2,1)} collective-permute-done((bf16[2,512,384]{2,1,0:T(8,128)(2,1)S(1)}, bf16[2,512,384]{2,1,0:T(8,128)(2,1)}, u32[]{:S(2)}, u32[]{:S(2)}) %collective-permute-start.5) | collective-permute-done | bytes 786464 | tf_op jit(solution)/shard_map/ppermute | solution.py:24
  64.2 5.1 %collective-permute-done.6.refs_5_ = bf16[2,512,384]{2,1,0:T(8,128)(2,1)} collective-permute-done((bf16[2,512,384]{2,1,0:T(8,128)(2,1)S(1)}, bf16[2,512,384]{2,1,0:T(8,128)(2,1)}, u32[]{:S(2)}, u32[]{:S(2)}) %collective-permute-start.6) | collective-permute-done | bytes 786464 | tf_op jit(solution)/shard_map/ppermute | solution.py:24
  71.2 1.7 fusion.47
  73.5 1.4 fusion.13
  74.9 1.8 pad_maximum_fusion.2
  77.7 2.0 copy.57.refs_6_
  80.2 1.5 collective-permute-start.9
  82.4 28.6 %kinetic.1 = bf16[4,1000,576]{2,1,0:T(8,128)(2,1)} custom-call(s32[8,10]{1,0:T(8,128)S(1)} %stack.128.table, f32[8]{0:T(128)S(1)} %select_reduce_fusion.scale, bf16[2,512,384]{2,1,0:T(8,128)(2,1)} %get-tuple-element.36.refs_0_, bf16[2,512,384]{2,1,0:T(8,128)(2,1)S(1)} %collective-permute-done.1.refs_1_, bf16[2,512,384]{2,1,0:T(8,128)(2,1)} %collective-permute-done.3.refs_2_, ...), custom_call_target="tpu_custom_call" | custom-call | flops 20000000000 | bytes 40000000 | tf_op jit(solution)/shard_map/kinetic/pallas_call | solution.py:353
  111.0 2.1 constant_dynamic-update-slice_fusion.1
  113.1 2.1 constant_dynamic-update-slice_fusion
  115.2 2.1 pad_maximum_fusion.3.refs_0_.refs_4_
  117.3 5.3 %correlation.2.refs_4_ = f32[4,192,384]{2,1,0:T(8,128)S(1)} custom-call(s32[2]{0:T(128)S(1)} %pad_add_fusion.3.meta, bf16[2000,384]{1,0:T(8,128)(2,1)} %bitcast.31.refs_0_, bf16[2000,384]{1,0:T(8,128)(2,1)} %bitcast.32.refs_1_, bf16[2000,384]{1,0:T(8,128)(2,1)S(1)} %bitcast.116, bf16[2000,384]{1,0:T(8,128)(2,1)} %bitcast.34.refs_3_), custom_call_target="tpu_custom_call" | custom-call | flops 1179648000 | bytes 6144000 | tf_op jit(solution)/shard_map/correlation/pallas_call | solution.py:113
  122.6 5.6 %correlation.3 = bf16[4,192,384]{2,1,0:T(8,128)(2,1)S(1)} custom-call(s32[2]{0:T(128)S(1)} %pad_add_fusion.3.meta, bf16[2000,384]{1,0:T(8,128)(2,1)S(1)} %pad_maximum_fusion.3.refs_0_.refs_4_, bf16[2000,384]{1,0:T(8,128)(2,1)} %bitcast.28.refs_1_.refs_5_, bf16[2000,384]{1,0:T(8,128)(2,1)} %bitcast.29.refs_2_.refs_6_, ...), custom_call_target="tpu_custom_call" | custom-call | flops 1179648000 | bytes 6144000 | tf_op jit(solution)/shard_map/correlation/pallas_call | solution.py:113
  129.0 3.1 %collective-permute-start.14 = (bf16[192,384]{1,0:T(8,128)(2,1)}, bf16[192,384]{1,0:T(8,128)(2,1)}, u32[]{:S(2)}, u32[]{:S(2)}) collective-permute-start(bf16[192,384]{1,0:T(8,128)(2,1)} %get-tuple-element.92), channel_id=1, source_target_pairs={{0,0},{1,8},{2,16},{3,24},{8,1},{9,9},{10,17},{11,25},{16,2},{17,1... | collective-permute-start | bytes 442376 | tf_op jit(solution)/shard_map/ppermute | solution.py:469
  132.1 3.5 %collective-permute-start.15 = (bf16[192,384]{1,0:T(8,128)(2,1)S(1)}, bf16[192,384]{1,0:T(8,128)(2,1)}, u32[]{:S(2)}, u32[]{:S(2)}) collective-permute-start(bf16[192,384]{1,0:T(8,128)(2,1)S(1)} %get-tuple-element.95), channel_id=1, source_target_pairs={{0,1},{1,9},{2,17},{3,25},{8,0},{9,8},{10,16},{11,24},{16,3},{17,1... | collective-permute-start | bytes 442376 | tf_op jit(solution)/shard_map/ppermute | solution.py:469
  135.6 1.6 collective-permute-start.17
  137.1 14.8 %collective-permute-done.14 = bf16[192,384]{1,0:T(8,128)(2,1)} collective-permute-done((bf16[192,384]{1,0:T(8,128)(2,1)}, bf16[192,384]{1,0:T(8,128)(2,1)}, u32[]{:S(2)}, u32[]{:S(2)}) %collective-permute-start.14) | collective-permute-done | bytes 147488 | tf_op jit(solution)/shard_map/ppermute | solution.py:469
  151.9 1.9 convert_add_fusion.1
  153.9 6.9 %collective-permute-start.18 = (bf16[192,384]{1,0:T(8,128)(2,1)S(1)}, bf16[192,384]{1,0:T(8,128)(2,1)S(1)}, u32[]{:S(2)}, u32[]{:S(2)}) collective-permute-start(bf16[192,384]{1,0:T(8,128)(2,1)S(1)} %convert_element_type.190), channel_id=1, source_target_pairs={{0,8},{8,0},{16,24},{24,16},{1,9},{9,1},{17,25},{25,17},{2,10},{10... | collective-permute-start | bytes 442376 | tf_op jit(solution)/shard_map/ppermute | solution.py:19
  160.8 3.5 %collective-permute-start.19 = (bf16[192,384]{1,0:T(8,128)(2,1)S(1)}, bf16[192,384]{1,0:T(8,128)(2,1)S(1)}, u32[]{:S(2)}, u32[]{:S(2)}) collective-permute-start(bf16[192,384]{1,0:T(8,128)(2,1)S(1)} %convert_element_type.190), channel_id=1, source_target_pairs={{0,16},{8,24},{16,0},{24,8},{1,17},{9,25},{17,1},{25,9},{2,18},{10... | collective-permute-start | bytes 442376 | tf_op jit(solution)/shard_map/ppermute | solution.py:19
  164.3 17.9 %fock.1 = bf16[4,3,192,384]{3,2,1,0:T(8,128)(2,1)S(1)} custom-call(s32[2]{0:T(128)S(1)} %pad_add_fusion.3.meta, bf16[2000,384]{1,0:T(8,128)(2,1)} %bitcast.31.refs_0_, bf16[2000,384]{1,0:T(8,128)(2,1)} %bitcast.32.refs_1_, bf16[2000,384]{1,0:T(8,128)(2,1)S(1)} %bitcast.117, bf16[2000,384]{1,0:T(8,128)(2,1)} %bitcast.34.refs_3_, ...), custom_call_target="tpu_custom_call" | custom-call | flops 7077888000 | bytes 12288000 | tf_op jit(solution)/shard_map/fock/pallas_call | solution.py:163
  183.8 8.1 %collective-permute-done.25 = bf16[2,192,384]{2,1,0:T(8,128)(2,1)S(1)} collective-permute-done((bf16[2,192,384]{2,1,0:T(8,128)(2,1)S(1)}, bf16[2,192,384]{2,1,0:T(8,128)(2,1)S(1)}, u32[]{:S(2)}, u32[]{:S(2)}) %collective-permute-start.25) | collective-permute-done | bytes 294944 | tf_op jit(solution)/shard_map/ppermute | solution.py:19
  192.7 1.8 collective-permute-start.24
  195.3 3.1 %collective-permute-start.21 = (bf16[3,192,384]{2,1,0:T(8,128)(2,1)}, bf16[3,192,384]{2,1,0:T(8,128)(2,1)}, u32[]{:S(2)}, u32[]{:S(2)}) collective-permute-start(bf16[3,192,384]{2,1,0:T(8,128)(2,1)} %get-tuple-element.78), channel_id=1, source_target_pairs={{0,0},{1,8},{2,16},{3,24},{8,1},{9,9},{10,17},{11,25},{16,2},{17,1... | collective-permute-start | bytes 1327112 | tf_op jit(solution)/shard_map/ppermute | solution.py:469
  199.6 8.1 %collective-permute-done.26 = bf16[2,2,192,384]{3,2,1,0:T(8,128)(2,1)S(1)} collective-permute-done((bf16[2,2,192,384]{3,2,1,0:T(8,128)(2,1)S(1)}, bf16[2,2,192,384]{3,2,1,0:T(8,128)(2,1)S(1)}, u32[]{:S(2)}, u32[]{:S(2)}) %collective-permute-start.26) | collective-permute-done | bytes 589856 | tf_op jit(solution)/shard_map/ppermute | solution.py:19
  207.9 5.9 %collective-permute-done.24 = bf16[2,2,192,384]{3,2,1,0:T(8,128)(2,1)S(1)} collective-permute-done((bf16[2,2,192,384]{3,2,1,0:T(8,128)(2,1)S(1)}, bf16[2,2,192,384]{3,2,1,0:T(8,128)(2,1)S(1)}, u32[]{:S(2)}, u32[]{:S(2)}) %collective-permute-start.24) | collective-permute-done | bytes 589856 | tf_op jit(solution)/shard_map/ppermute | solution.py:19
  215.8 1.6 collective-permute-start.28
  217.5 31.1 %collective-permute-done.21 = bf16[3,192,384]{2,1,0:T(8,128)(2,1)} collective-permute-done((bf16[3,192,384]{2,1,0:T(8,128)(2,1)}, bf16[3,192,384]{2,1,0:T(8,128)(2,1)}, u32[]{:S(2)}, u32[]{:S(2)}) %collective-permute-start.21) | collective-permute-done | bytes 442400 | tf_op jit(solution)/shard_map/ppermute | solution.py:469
  248.7 1.6 convert_add_fusion
  251.1 31.8 %collective-permute-start.29 = (bf16[192,192]{1,0:T(8,128)(2,1)}, bf16[192,192]{1,0:T(8,128)(2,1)}, u32[]{:S(2)}, u32[]{:S(2)}) collective-permute-start(bf16[192,192]{1,0:T(8,128)(2,1)} %get-tuple-element.103), channel_id=1, source_target_pairs={{0,0},{1,8},{2,16},{3,24},{4,4},{5,12},{6,20},{7,28},{8,1},{9,9},{... | collective-permute-start | bytes 221192 | tf_op jit(solution)/shard_map/ppermute | solution.py:529
  285.9 3.1 %collective-permute-done.29 = bf16[192,192]{1,0:T(8,128)(2,1)} collective-permute-done((bf16[192,192]{1,0:T(8,128)(2,1)}, bf16[192,192]{1,0:T(8,128)(2,1)}, u32[]{:S(2)}, u32[]{:S(2)}) %collective-permute-start.29) | collective-permute-done | bytes 73760 | tf_op jit(solution)/shard_map/ppermute | solution.py:529
  289.0 2.0 collective-permute-done.30
  292.0 1.9 maximum_add_fusion
  293.8 1.9 copy.60
  295.7 1.5 pad_maximum_fusion.1.low
  297.3 1.5 pad_maximum_fusion.top
  298.8 7.9 %root.1 = f32[192,384]{1,0:T(8,128)} custom-call(s32[3]{0:T(128)S(1)} %pad_add_fusion.4.meta, bf16[2,2,2,2,192,384]{5,4,3,2,1,0:T(8,128)(2,1)S(1)} %pad_maximum_fusion.top, bf16[2,2,2,2,192,384]{5,4,3,2,1,0:T(8,128)(2,1)S(1)} %pad_maximum_fusion.1.low, f32[192,384]{1,0:T(8,128)S(1)} %get-tuple-element.73.offset), custom_call_target="tpu_custom_call" | custom-call | tf_op jit(solution)/shard_map/root/pallas_call | solution.py:225
  (132 shorter events, 30.6 us)
Async XLA Ops:
  0.6 18.6 %copy-start.7 = (f32[112,112]{0,1:T(8,128)S(1)}, f32[112,112]{0,1:T(8,128)}, u32[]{:S(2)}) copy-start(f32[112,112]{0,1:T(8,128)} %constant.149) | copy-start | bytes 150532
  0.6 18.4 %copy-start.3 = (bf16[3,10,10]{2,0,1:T(4,128)(2,1)S(1)}, bf16[3,10,10]{2,0,1:T(4,128)(2,1)}, u32[]{:S(2)}) copy-start(bf16[3,10,10]{2,0,1:T(4,128)(2,1)} %param.17) | copy-start | bytes 1804
  2.8 16.2 %copy-start.13 = (s32[2,1]{1,0:T(2,128)}, s32[2,1]{1,0:T(2,128)S(1)}, u32[]{:S(2)}) copy-start(s32[2,1]{1,0:T(2,128)S(1)} %compare_convert_fusion) | copy-start | bytes 28
  3.6 0.6 copy-start.14
  4.1 1.4 copy-start
  5.5 13.6 %copy-start.8 = (f32[112,112]{0,1:T(8,128)S(1)}, f32[112,112]{0,1:T(8,128)}, u32[]{:S(2)}) copy-start(f32[112,112]{0,1:T(8,128)} %constant.150) | copy-start | bytes 150532
  5.5 14.6 %copy-start.4 = (f32[160,160]{0,1:T(8,128)S(1)}, f32[160,160]{0,1:T(8,128)}, u32[]{:S(2)}) copy-start(f32[160,160]{0,1:T(8,128)} %constant.151) | copy-start | bytes 307204
  8.3 11.9 %copy-start.6 = (f32[112,112]{1,0:T(8,128)S(1)}, f32[112,112]{1,0:T(8,128)}, u32[]{:S(2)}) copy-start(f32[112,112]{1,0:T(8,128)} %constant.137.clone) | copy-start | bytes 150532
  8.4 11.9 %copy-start.11 = (bf16[112,10,1]{0,1,2:T(8,128)(2,1)S(1)}, bf16[112,10,1]{0,1,2:T(8,128)(2,1)}, u32[]{:S(2)}) copy-start(bf16[112,10,1]{0,1,2:T(8,128)(2,1)} %constant.153) | copy-start | bytes 6724
  8.4 12.3 %copy-start.5 = (f32[112,112]{1,0:T(8,128)S(1)}, f32[112,112]{1,0:T(8,128)}, u32[]{:S(2)}) copy-start(f32[112,112]{1,0:T(8,128)} %constant.134.clone) | copy-start | bytes 150532
  8.4 12.3 %copy-start.10 = (bf16[112,10,1]{0,1,2:T(8,128)(2,1)S(1)}, bf16[112,10,1]{0,1,2:T(8,128)(2,1)}, u32[]{:S(2)}) copy-start(bf16[112,10,1]{0,1,2:T(8,128)(2,1)} %constant.152) | copy-start | bytes 6724
  8.4 40.8 %collective-permute-start.2 = (bf16[2,512,384]{2,1,0:T(8,128)(2,1)}, bf16[2,512,384]{2,1,0:T(8,128)(2,1)}, u32[]{:S(2)}, u32[]{:S(2)}) collective-permute-start(bf16[2,512,384]{2,1,0:T(8,128)(2,1)} %get-tuple-element.36.refs_0_), channel_id=1, source_target_pairs={{0,4},{4,0},{1,5},{5,1},{2,6},{6,2},{3,7},{7,3},{8,12},{12,8},{9,1... | collective-permute-start | bytes 2359304 | tf_op jit(solution)/shard_map/ppermute | solution.py:19
  9.9 43.8 %collective-permute-start.3 = (bf16[2,512,384]{2,1,0:T(8,128)(2,1)}, bf16[2,512,384]{2,1,0:T(8,128)(2,1)}, u32[]{:S(2)}, u32[]{:S(2)}) collective-permute-start(bf16[2,512,384]{2,1,0:T(8,128)(2,1)} %get-tuple-element.36.refs_0_), channel_id=1, source_target_pairs={{0,8},{8,16},{16,24},{1,9},{9,17},{17,25},{2,10},{10,18},{18,26},{... | collective-permute-start | bytes 2359304 | tf_op jit(solution)/shard_map/ppermute | solution.py:24
  14.3 41.9 %collective-permute-start.4 = (bf16[2,512,384]{2,1,0:T(8,128)(2,1)}, bf16[2,512,384]{2,1,0:T(8,128)(2,1)}, u32[]{:S(2)}, u32[]{:S(2)}) collective-permute-start(bf16[2,512,384]{2,1,0:T(8,128)(2,1)} %get-tuple-element.36.refs_0_), channel_id=1, source_target_pairs={{8,0},{16,8},{24,16},{9,1},{17,9},{25,17},{10,2},{18,10},{26,18},{... | collective-permute-start | bytes 2359304 | tf_op jit(solution)/shard_map/ppermute | solution.py:24
  15.6 29.2 %collective-permute-start.1 = (bf16[2,512,384]{2,1,0:T(8,128)(2,1)}, bf16[2,512,384]{2,1,0:T(8,128)(2,1)S(1)}, u32[]{:S(2)}, u32[]{:S(2)}) collective-permute-start(bf16[2,512,384]{2,1,0:T(8,128)(2,1)} %get-tuple-element.34), channel_id=1, source_target_pairs={{0,4},{4,0},{1,5},{5,1},{2,6},{6,2},{3,7},{7,3},{8,12},{12,8},{9,1... | collective-permute-start | bytes 2359304 | tf_op jit(solution)/shard_map/ppermute | solution.py:19
  16.2 41.5 %collective-permute-start = (bf16[2,1000,384]{2,1,0:T(8,128)(2,1)}, bf16[2,1000,384]{2,1,0:T(8,128)(2,1)S(1)}, u32[]{:S(2)}, u32[]{:S(2)}) collective-permute-start(bf16[2,1000,384]{2,1,0:T(8,128)(2,1)} %get-tuple-element.53), channel_id=1, source_target_pairs={{0,2},{1,3},{2,0},{3,1},{4,6},{5,7},{6,4},{7,5},{8,10},{9,11},{10,... | collective-permute-start | bytes 4608008 | tf_op jit(solution)/shard_map/ppermute | solution.py:19
  20.1 31.2 %copy-start.9 = (bf16[160,10,1]{0,1,2:T(8,128)(2,1)S(1)}, bf16[160,10,1]{0,1,2:T(8,128)(2,1)}, u32[]{:S(2)}) copy-start(bf16[160,10,1]{0,1,2:T(8,128)(2,1)} %constant.154) | copy-start | bytes 9604
  44.8 19.4 %collective-permute-start.5 = (bf16[2,512,384]{2,1,0:T(8,128)(2,1)S(1)}, bf16[2,512,384]{2,1,0:T(8,128)(2,1)}, u32[]{:S(2)}, u32[]{:S(2)}) collective-permute-start(bf16[2,512,384]{2,1,0:T(8,128)(2,1)S(1)} %collective-permute-done.1.refs_1_), channel_id=1, source_target_pairs={{0,8},{8,16},{16,24},{1,9},{9,17},{17,25},{2,10},{10,18},{18,26},{... | collective-permute-start | bytes 2359304 | tf_op jit(solution)/shard_map/ppermute | solution.py:24
  49.1 20.1 %collective-permute-start.6 = (bf16[2,512,384]{2,1,0:T(8,128)(2,1)S(1)}, bf16[2,512,384]{2,1,0:T(8,128)(2,1)}, u32[]{:S(2)}, u32[]{:S(2)}) collective-permute-start(bf16[2,512,384]{2,1,0:T(8,128)(2,1)S(1)} %collective-permute-done.1.refs_1_), channel_id=1, source_target_pairs={{8,0},{16,8},{24,16},{9,1},{17,9},{25,17},{10,2},{18,10},{26,18},{... | collective-permute-start | bytes 2359304 | tf_op jit(solution)/shard_map/ppermute | solution.py:24
  53.8 3.9 %collective-permute-start.7 = (f32[2,1000]{1,0:T(2,128)}, f32[2,1000]{1,0:T(2,128)S(1)}, u32[]{:S(2)}, u32[]{:S(2)}) collective-permute-start(f32[2,1000]{1,0:T(2,128)} %param.16), channel_id=1, source_target_pairs={{0,4},{4,0},{1,5},{5,1},{2,6},{6,2},{3,7},{7,3},{8,12},{12,8},{9,1... | collective-permute-start | bytes 24008 | tf_op jit(solution)/shard_map/ppermute | solution.py:19
  73.5 3.2 %copy-start.1 = (bf16[2,1000,192]{2,1,0:T(8,128)(2,1)}, bf16[2,1000,192]{2,1,0:T(8,128)(2,1)S(1)}, u32[]{:S(2)}) copy-start(bf16[2,1000,192]{2,1,0:T(8,128)(2,1)S(1)} %get-tuple-element.76) | copy-start | bytes 2304004
  73.5 3.2 %copy-start.2 = (bf16[2,1000,192]{2,1,0:T(8,128)(2,1)}, bf16[2,1000,192]{2,1,0:T(8,128)(2,1)S(1)}, u32[]{:S(2)}) copy-start(bf16[2,1000,192]{2,1,0:T(8,128)(2,1)S(1)} %get-tuple-element.77) | copy-start | bytes 2304004
  76.7 1.0 copy-start.12
  77.6 39.7 %collective-permute-start.13 = (bf16[2,1000,384]{2,1,0:T(8,128)(2,1)S(1)}, bf16[2,1000,384]{2,1,0:T(8,128)(2,1)}, u32[]{:S(2)}, u32[]{:S(2)}) collective-permute-start(bf16[2,1000,384]{2,1,0:T(8,128)(2,1)S(1)} %collective-permute-done), channel_id=1, source_target_pairs={{0,1},{1,0},{2,3},{3,2},{4,5},{5,4},{6,7},{7,6},{8,9},{9,8},{10,11... | collective-permute-start | bytes 4608008 | tf_op jit(solution)/shard_map/ppermute | solution.py:19
  79.7 31.3 %collective-permute-start.8 = (bf16[1,1000,384]{2,1,0:T(8,128)(2,1)}, bf16[1,1000,384]{2,1,0:T(8,128)(2,1)}, u32[]{:S(2)}, u32[]{:S(2)}) collective-permute-start(bf16[1,1000,384]{2,1,0:T(8,128)(2,1)} %fusion.13), channel_id=1, source_target_pairs={{0,2},{1,3},{2,0},{3,1},{4,6},{5,7},{6,4},{7,5},{8,10},{9,11},{10,... | collective-permute-start | bytes 2304008 | tf_op jit(solution)/shard_map/ppermute | solution.py:19
  80.2 30.7 %collective-permute-start.9 = (bf16[1,1000,384]{2,1,0:T(8,128)(2,1)}, bf16[1,1000,384]{2,1,0:T(8,128)(2,1)}, u32[]{:S(2)}, u32[]{:S(2)}) collective-permute-start(bf16[1,1000,384]{2,1,0:T(8,128)(2,1)} %slice.105), channel_id=1, source_target_pairs={{0,4},{4,0},{1,5},{5,1},{2,6},{6,2},{3,7},{7,3},{8,12},{12,8},{9,1... | collective-permute-start | bytes 2304008 | tf_op jit(solution)/shard_map/ppermute | solution.py:19
  81.8 40.9 %collective-permute-start.10 = (bf16[2,1000,384]{2,1,0:T(8,128)(2,1)}, bf16[2,1000,384]{2,1,0:T(8,128)(2,1)}, u32[]{:S(2)}, u32[]{:S(2)}) collective-permute-start(bf16[2,1000,384]{2,1,0:T(8,128)(2,1)} %pad_maximum_fusion.2), channel_id=1, source_target_pairs={{0,1},{1,0},{2,3},{3,2},{4,5},{5,4},{6,7},{7,6},{8,9},{9,8},{10,11... | collective-permute-start | bytes 4608008 | tf_op jit(solution)/shard_map/ppermute | solution.py:19
  81.8 35.5 %collective-permute-start.12 = (bf16[2,1000,384]{2,1,0:T(8,128)(2,1)}, bf16[2,1000,384]{2,1,0:T(8,128)(2,1)}, u32[]{:S(2)}, u32[]{:S(2)}) collective-permute-start(bf16[2,1000,384]{2,1,0:T(8,128)(2,1)} %get-tuple-element.53), channel_id=1, source_target_pairs={{0,1},{1,0},{2,3},{3,2},{4,5},{5,4},{6,7},{7,6},{8,9},{9,8},{10,11... | collective-permute-start | bytes 4608008 | tf_op jit(solution)/shard_map/ppermute | solution.py:19
  115.2 7.5 %collective-permute-start.11 = (bf16[2,1000,384]{2,1,0:T(8,128)(2,1)}, bf16[2,1000,384]{2,1,0:T(8,128)(2,1)}, u32[]{:S(2)}, u32[]{:S(2)}) collective-permute-start(bf16[2,1000,384]{2,1,0:T(8,128)(2,1)} %constant_dynamic-update-slice_fusion), channel_id=1, source_target_pairs={{0,1},{1,0},{2,3},{3,2},{4,5},{5,4},{6,7},{7,6},{8,9},{9,8},{10,11... | collective-permute-start | bytes 4608008 | tf_op jit(solution)/shard_map/ppermute | solution.py:19
  129.0 22.9 %collective-permute-start.14 = (bf16[192,384]{1,0:T(8,128)(2,1)}, bf16[192,384]{1,0:T(8,128)(2,1)}, u32[]{:S(2)}, u32[]{:S(2)}) collective-permute-start(bf16[192,384]{1,0:T(8,128)(2,1)} %get-tuple-element.92), channel_id=1, source_target_pairs={{0,0},{1,8},{2,16},{3,24},{8,1},{9,9},{10,17},{11,25},{16,2},{17,1... | collective-permute-start | bytes 442376 | tf_op jit(solution)/shard_map/ppermute | solution.py:469
  132.1 19.8 %collective-permute-start.15 = (bf16[192,384]{1,0:T(8,128)(2,1)S(1)}, bf16[192,384]{1,0:T(8,128)(2,1)}, u32[]{:S(2)}, u32[]{:S(2)}) collective-permute-start(bf16[192,384]{1,0:T(8,128)(2,1)S(1)} %get-tuple-element.95), channel_id=1, source_target_pairs={{0,1},{1,9},{2,17},{3,25},{8,0},{9,8},{10,16},{11,24},{16,3},{17,1... | collective-permute-start | bytes 442376 | tf_op jit(solution)/shard_map/ppermute | solution.py:469
  135.6 16.3 %collective-permute-start.16 = (bf16[192,384]{1,0:T(8,128)(2,1)S(1)}, bf16[192,384]{1,0:T(8,128)(2,1)}, u32[]{:S(2)}, u32[]{:S(2)}) collective-permute-start(bf16[192,384]{1,0:T(8,128)(2,1)S(1)} %get-tuple-element.94), channel_id=1, source_target_pairs={{0,2},{1,10},{2,18},{3,26},{8,3},{9,11},{10,19},{11,27},{16,0},{17... | collective-permute-start | bytes 442376 | tf_op jit(solution)/shard_map/ppermute | solution.py:469
  135.6 16.3 %collective-permute-start.17 = (bf16[192,384]{1,0:T(8,128)(2,1)S(1)}, bf16[192,384]{1,0:T(8,128)(2,1)}, u32[]{:S(2)}, u32[]{:S(2)}) collective-permute-start(bf16[192,384]{1,0:T(8,128)(2,1)S(1)} %get-tuple-element.93), channel_id=1, source_target_pairs={{0,3},{1,11},{2,19},{3,27},{8,2},{9,10},{10,18},{11,26},{16,1},{17... | collective-permute-start | bytes 442376 | tf_op jit(solution)/shard_map/ppermute | solution.py:469
  153.9 28.3 %collective-permute-start.18 = (bf16[192,384]{1,0:T(8,128)(2,1)S(1)}, bf16[192,384]{1,0:T(8,128)(2,1)S(1)}, u32[]{:S(2)}, u32[]{:S(2)}) collective-permute-start(bf16[192,384]{1,0:T(8,128)(2,1)S(1)} %convert_element_type.190), channel_id=1, source_target_pairs={{0,8},{8,0},{16,24},{24,16},{1,9},{9,1},{17,25},{25,17},{2,10},{10... | collective-permute-start | bytes 442376 | tf_op jit(solution)/shard_map/ppermute | solution.py:19
  160.8 21.4 %collective-permute-start.19 = (bf16[192,384]{1,0:T(8,128)(2,1)S(1)}, bf16[192,384]{1,0:T(8,128)(2,1)S(1)}, u32[]{:S(2)}, u32[]{:S(2)}) collective-permute-start(bf16[192,384]{1,0:T(8,128)(2,1)S(1)} %convert_element_type.190), channel_id=1, source_target_pairs={{0,16},{8,24},{16,0},{24,8},{1,17},{9,25},{17,1},{25,9},{2,18},{10... | collective-permute-start | bytes 442376 | tf_op jit(solution)/shard_map/ppermute | solution.py:19
  164.3 17.9 %collective-permute-start.20 = (bf16[192,384]{1,0:T(8,128)(2,1)S(1)}, bf16[192,384]{1,0:T(8,128)(2,1)S(1)}, u32[]{:S(2)}, u32[]{:S(2)}) collective-permute-start(bf16[192,384]{1,0:T(8,128)(2,1)S(1)} %convert_element_type.190), channel_id=1, source_target_pairs={{0,24},{8,16},{16,8},{24,0},{1,25},{9,17},{17,9},{25,1},{2,26},{10... | collective-permute-start | bytes 442376 | tf_op jit(solution)/shard_map/ppermute | solution.py:19
  182.3 9.6 %collective-permute-start.25 = (bf16[2,192,384]{2,1,0:T(8,128)(2,1)S(1)}, bf16[2,192,384]{2,1,0:T(8,128)(2,1)S(1)}, u32[]{:S(2)}, u32[]{:S(2)}) collective-permute-start(bf16[2,192,384]{2,1,0:T(8,128)(2,1)S(1)} %get-tuple-element.97), channel_id=1, source_target_pairs={{0,2},{1,3},{2,0},{3,1},{4,6},{5,7},{6,4},{7,5},{8,10},{9,11},{10,... | collective-permute-start | bytes 884744 | tf_op jit(solution)/shard_map/ppermute | solution.py:19
  183.3 9.3 %collective-permute-start.23 = (bf16[2,192,384]{2,1,0:T(8,128)(2,1)S(1)}, bf16[2,192,384]{2,1,0:T(8,128)(2,1)S(1)}, u32[]{:S(2)}, u32[]{:S(2)}) collective-permute-start(bf16[2,192,384]{2,1,0:T(8,128)(2,1)S(1)} %get-tuple-element.99), channel_id=1, source_target_pairs={{0,4},{4,0},{1,5},{5,1},{2,6},{6,2},{3,7},{7,3},{8,12},{12,8},{9,1... | collective-permute-start | bytes 884744 | tf_op jit(solution)/shard_map/ppermute | solution.py:19
  192.0 15.8 %collective-permute-start.26 = (bf16[2,2,192,384]{3,2,1,0:T(8,128)(2,1)S(1)}, bf16[2,2,192,384]{3,2,1,0:T(8,128)(2,1)S(1)}, u32[]{:S(2)}, u32[]{:S(2)}) collective-permute-start(bf16[2,2,192,384]{3,2,1,0:T(8,128)(2,1)S(1)} %get-tuple-element.89), channel_id=1, source_target_pairs={{0,4},{4,0},{1,5},{5,1},{2,6},{6,2},{3,7},{7,3},{8,12},{12,8},{9,1... | collective-permute-start | bytes 1769480 | tf_op jit(solution)/shard_map/ppermute | solution.py:19
  192.7 21.1 %collective-permute-start.24 = (bf16[2,2,192,384]{3,2,1,0:T(8,128)(2,1)S(1)}, bf16[2,2,192,384]{3,2,1,0:T(8,128)(2,1)S(1)}, u32[]{:S(2)}, u32[]{:S(2)}) collective-permute-start(bf16[2,2,192,384]{3,2,1,0:T(8,128)(2,1)S(1)} %get-tuple-element.91), channel_id=1, source_target_pairs={{0,2},{1,3},{2,0},{3,1},{4,6},{5,7},{6,4},{7,5},{8,10},{9,11},{10,... | collective-permute-start | bytes 1769480 | tf_op jit(solution)/shard_map/ppermute | solution.py:19
  195.3 53.4 %collective-permute-start.21 = (bf16[3,192,384]{2,1,0:T(8,128)(2,1)}, bf16[3,192,384]{2,1,0:T(8,128)(2,1)}, u32[]{:S(2)}, u32[]{:S(2)}) collective-permute-start(bf16[3,192,384]{2,1,0:T(8,128)(2,1)} %get-tuple-element.78), channel_id=1, source_target_pairs={{0,0},{1,8},{2,16},{3,24},{8,1},{9,9},{10,17},{11,25},{16,2},{17,1... | collective-permute-start | bytes 1327112 | tf_op jit(solution)/shard_map/ppermute | solution.py:469
  198.4 50.3 %collective-permute-start.22 = (bf16[3,192,384]{2,1,0:T(8,128)(2,1)S(1)}, bf16[3,192,384]{2,1,0:T(8,128)(2,1)}, u32[]{:S(2)}, u32[]{:S(2)}) collective-permute-start(bf16[3,192,384]{2,1,0:T(8,128)(2,1)S(1)} %get-tuple-element.79), channel_id=1, source_target_pairs={{0,1},{1,9},{2,17},{3,25},{8,0},{9,8},{10,16},{11,24},{16,3},{17,1... | collective-permute-start | bytes 1327112 | tf_op jit(solution)/shard_map/ppermute | solution.py:469
  214.9 33.8 %collective-permute-start.27 = (bf16[3,192,384]{2,1,0:T(8,128)(2,1)}, bf16[3,192,384]{2,1,0:T(8,128)(2,1)}, u32[]{:S(2)}, u32[]{:S(2)}) collective-permute-start(bf16[3,192,384]{2,1,0:T(8,128)(2,1)} %get-tuple-element.80), channel_id=1, source_target_pairs={{0,2},{1,10},{2,18},{3,26},{8,3},{9,11},{10,19},{11,27},{16,0},{17... | collective-permute-start | bytes 1327112 | tf_op jit(solution)/shard_map/ppermute | solution.py:469
  215.8 32.9 %collective-permute-start.28 = (bf16[3,192,384]{2,1,0:T(8,128)(2,1)}, bf16[3,192,384]{2,1,0:T(8,128)(2,1)}, u32[]{:S(2)}, u32[]{:S(2)}) collective-permute-start(bf16[3,192,384]{2,1,0:T(8,128)(2,1)} %get-tuple-element.81), channel_id=1, source_target_pairs={{0,3},{1,11},{2,19},{3,27},{8,2},{9,10},{10,18},{11,26},{16,1},{17... | collective-permute-start | bytes 1327112 | tf_op jit(solution)/shard_map/ppermute | solution.py:469
  217.5 78.2 %collective-permute-start.32 = (bf16[2,2,2,192,384]{4,3,2,1,0:T(8,128)(2,1)S(1)}, bf16[2,2,2,192,384]{4,3,2,1,0:T(8,128)(2,1)}, u32[]{:S(2)}, u32[]{:S(2)}) collective-permute-start(bf16[2,2,2,192,384]{4,3,2,1,0:T(8,128)(2,1)S(1)} %pad_maximum_fusion.5), channel_id=1, source_target_pairs={{0,1},{1,0},{2,3},{3,2},{4,5},{5,4},{6,7},{7,6},{8,9},{9,8},{10,11... | collective-permute-start | bytes 3538952 | tf_op jit(solution)/shard_map/ppermute | solution.py:19
  248.7 48.6 %collective-permute-start.31 = (bf16[2,2,2,192,384]{4,3,2,1,0:T(8,128)(2,1)S(1)}, bf16[2,2,2,192,384]{4,3,2,1,0:T(8,128)(2,1)}, u32[]{:S(2)}, u32[]{:S(2)}) collective-permute-start(bf16[2,2,2,192,384]{4,3,2,1,0:T(8,128)(2,1)S(1)} %pad_maximum_fusion.4), channel_id=1, source_target_pairs={{0,1},{1,0},{2,3},{3,2},{4,5},{5,4},{6,7},{7,6},{8,9},{9,8},{10,11... | collective-permute-start | bytes 3538952 | tf_op jit(solution)/shard_map/ppermute | solution.py:19
  251.1 37.9 %collective-permute-start.29 = (bf16[192,192]{1,0:T(8,128)(2,1)}, bf16[192,192]{1,0:T(8,128)(2,1)}, u32[]{:S(2)}, u32[]{:S(2)}) collective-permute-start(bf16[192,192]{1,0:T(8,128)(2,1)} %get-tuple-element.103), channel_id=1, source_target_pairs={{0,0},{1,8},{2,16},{3,24},{4,4},{5,12},{6,20},{7,28},{8,1},{9,9},{... | collective-permute-start | bytes 221192 | tf_op jit(solution)/shard_map/ppermute | solution.py:529
  282.9 8.1 %collective-permute-start.30 = (bf16[192,192]{1,0:T(8,128)(2,1)S(1)}, bf16[192,192]{1,0:T(8,128)(2,1)}, u32[]{:S(2)}, u32[]{:S(2)}) collective-permute-start(bf16[192,192]{1,0:T(8,128)(2,1)S(1)} %get-tuple-element.102), channel_id=1, source_target_pairs={{0,4},{1,12},{2,20},{3,28},{4,0},{5,8},{6,16},{7,24},{8,5},{9,13},... | collective-permute-start | bytes 221192 | tf_op jit(solution)/shard_map/ppermute | solution.py:529
  (1 other events, 0.5 us)

commit v3 on v2

--- a/solution.py
+++ b/solution.py
@@ -76,107 +76,130 @@
 
 
 def load_left(lefts, held, sems):
-    copies = [pltpu.make_async_copy(left, held.at[i], sems.at[i]) for i, left in enumerate(lefts)]
+    copies = []
+    for q, pieces in enumerate(lefts):
+        row = 0
+        for piece in pieces:
+            rows, width = piece.shape
+            here = held.at[row : row + rows, q * width : (q + 1) * width]
+            copies.append(pltpu.make_async_copy(piece, here, sems.at[len(copies)]))
+            row += rows
     for copy in copies:
         copy.start()
     return copies
 
 
-def correlation_kernel(share, meta, *refs):
+def grouped(refs, counts):
+    refs = list(refs)
+    return [[refs.pop(0) for _ in range(count)] for count in counts]
+
+
+def correlation_kernel(share, counts, meta, *refs):
     refs, (out, held, turned, sems) = refs[:-4], refs[-4:]
     groups, half, width = out.shape
-    lefts, before = refs[:groups], refs[groups:]
+    lefts, before = grouped(refs, counts), refs[sum(counts) :]
     copies = load_left(lefts, held, sems)
-    first, apart = meta[0] == 0, meta[1]
-    copies[0].wait()
-    own = held[0]
+    first = meta[0] == 0
+    for copy in copies[: counts[0]]:
+        copy.wait()
+    own = held[:, :width]
     turned[...] = jnp.where(first, own[:, :half], own[:, half:]).T
-    for copy in copies[1:]:
+    for copy in copies[counts[0] :]:
         copy.wait()
-
-    def per_group(q, carry):
-        total = matmul(turned[...], held[q])
-        if before:
-            rows = lax.broadcasted_iota(jnp.int32, (half, width), 0) + jnp.where(first, 0, half)
-            columns = lax.broadcasted_iota(jnp.int32, (half, width), 1)
-            total = total + before[0][q ^ apart] - jnp.where((rows == columns) & (q == 0), share, 0.0)
-        out[q ^ apart] = total.astype(out.dtype)
-        return carry
-
-    lax.fori_loop(0, groups, per_group, 0)
+    for base in range(0, groups, 2):
+        wide = matmul(turned[...], held[:, base * width : (base + 2) * width])
+        for q in (base, base + 1):
+            total = wide[:, (q - base) * width : (q - base + 1) * width]
+            if before:
+                total = total + before[0][q]
+                if q == 0:
+                    rows = lax.broadcasted_iota(jnp.int32, (half, width), 0) + jnp.where(first, 0, half)
+                    columns = lax.broadcasted_iota(jnp.int32, (half, width), 1)
+                    total = total - jnp.where(rows == columns, share, 0.0)
+            out[q] = total.astype(out.dtype)
 
 
 def box_correlation(share, meta, lefts, before, half):
-    depth, width = lefts[0].shape
+    depth, width = sum(piece.shape[0] for piece in lefts[0]), lefts[0][0].shape[1]
+    counts = [len(pieces) for pieces in lefts]
     vmem = pl.BlockSpec(memory_space=pltpu.VMEM)
     extra = [] if before is None else [before]
     return pl.pallas_call(
-        functools.partial(correlation_kernel, share),
+        functools.partial(correlation_kernel, share, counts),
         out_shape=jax.ShapeDtypeStruct((len(lefts), half, width), f32 if before is None else bf16),
         in_specs=[pl.BlockSpec(memory_space=pltpu.SMEM)]
-        + [pl.BlockSpec(memory_space=pl.ANY)] * len(lefts)
+        + [pl.BlockSpec(memory_space=pl.ANY)] * sum(counts)
         + [vmem] * len(extra),
         out_specs=vmem,
         scratch_shapes=[
-            pltpu.VMEM((len(lefts), depth, width), bf16),
+            pltpu.VMEM((depth, len(lefts) * width), bf16),
             pltpu.VMEM((half, depth), bf16),
-            pltpu.SemaphoreType.DMA((len(lefts),)),
+            pltpu.SemaphoreType.DMA((sum(counts),)),
         ],
         compiler_params=params(32),
         cost_estimate=pl.CostEstimate(
             flops=2 * len(lefts) * depth * width * half, bytes_accessed=2 * len(lefts) * depth * width, transcendentals=0
         ),
         name="correlation",
-    )(meta, *lefts, *extra)
-
-
-def fock_kernel(meta, *refs):
-    lefts, right, out, held, raw, turned, sems = refs[:-6], refs[-6], refs[-5], refs[-4], refs[-3], refs[-2], refs[-1]
-    copies = load_left(lefts, held, sems)
-    last = pltpu.make_async_copy(right, raw, sems.at[len(lefts)])
-    last.start()
-    groups = len(lefts) // 2
-    half, width = out.shape[2:]
-    apart = meta[1]
-    last.wait()
+    )(meta, *[piece for pieces in lefts for piece in pieces], *extra)
+
+
+def fock_kernel(counts, *refs):
+    refs, (right, out, held, raw, turned, sems, last_sems) = refs[:-7], refs[-7:]
+    groups, _, half, width = out.shape
+    lefts = grouped(refs, counts)
+    lasts = [pltpu.make_async_copy(right.at[side], raw.at[side], last_sems.at[side]) for side in range(2)]
+    for copy in lasts:
+        copy.start()
+    copies = []
     for side in range(2):
+        blocks = lefts[side * groups : (side + 1) * groups]
+        copies += load_left(blocks, held.at[side], sems.at[side])
+    for side in range(2):
+        lasts[side].wait()
         turned[side] = raw[side].T
     for copy in copies:
         copy.wait()
 
-    def per_group(q, carry):
-        total = matmul(turned[0], held[q]) + matmul(turned[1], held[groups + q])
+    def two_groups(j, carry):
+        lanes = pl.ds(pl.multiple_of(j * 2 * width, 2 * width), 2 * width)
+        total = matmul(turned[0], held[0, :, lanes]) + matmul(turned[1], held[1, :, lanes])
         main = total[:half] + total[half : 2 * half]
         top = main.astype(bf16)
-        out[q ^ apart, 0] = top
-        out[q ^ apart, 1] = (main - top.astype(f32)).astype(bf16)
-        out[q ^ apart, 2] = total[2 * half :].astype(bf16)
+        low = (main - top.astype(f32)).astype(bf16)
+        fix = total[2 * half :].astype(bf16)
+        for q in range(2):
+            here = slice(q * width, (q + 1) * width)
+            out[2 * j + q, 0], out[2 * j + q, 1], out[2 * j + q, 2] = top[:, here], low[:, here], fix[:, here]
         return carry
 
-    lax.fori_loop(0, groups, per_group, 0)
-
-
-def fock_rows(meta, lefts, right):
-    depth, width = lefts[0].shape
-    tall = right.shape[-1]
+    lax.fori_loop(0, groups // 2, two_groups, 0)
+
+
+def fock_rows(lefts, right):
+    depth, width = sum(piece.shape[0] for piece in lefts[0]), lefts[0][0].shape[1]
+    counts = [len(pieces) for pieces in lefts]
+    groups, tall = len(lefts) // 2, right.shape[-1]
+    most = max(sum(counts[:groups]), sum(counts[groups:]))
     anywhere = pl.BlockSpec(memory_space=pl.ANY)
     return pl.pallas_call(
-        fock_kernel,
-        out_shape=jax.ShapeDtypeStruct((len(lefts) // 2, 3, tall // 3, width), bf16),
-        in_specs=[pl.BlockSpec(memory_space=pltpu.SMEM)] + [anywhere] * (len(lefts) + 1),
+        functools.partial(fock_kernel, counts),
+        out_shape=jax.ShapeDtypeStruct((groups, 3, tall // 3, width), bf16),
+        in_specs=[anywhere] * (sum(counts) + 1),
         out_specs=pl.BlockSpec(memory_space=pltpu.VMEM),
         scratch_shapes=[
-            pltpu.VMEM((len(lefts), depth, width), bf16),
+            pltpu.VMEM((2, depth, groups * width), bf16),
             pltpu.VMEM(right.shape, bf16),
             pltpu.VMEM((2, tall, depth), bf16),
-            pltpu.SemaphoreType.DMA((len(lefts) + 1,)),
+            pltpu.SemaphoreType.DMA((2, most)),
+            pltpu.SemaphoreType.DMA((2,)),
         ],
-        compiler_params=params(40),
+        compiler_params=params(44),
         cost_estimate=pl.CostEstimate(
             flops=2 * len(lefts) * depth * width * tall, bytes_accessed=2 * len(lefts) * depth * width, transcendentals=0
         ),
         name="fock",
-    )(meta, *lefts, right)
+    )(*[piece for pieces in lefts for piece in pieces], right)
 
 
 def root_kernel(meta, top, low, offset, root, whole, rows_f, cols_b):
@@ -186,13 +209,14 @@
     groups = side // width
     for core in range(2):
         for far in range(top.shape[1]):
-            lanes = pl.ds(pl.multiple_of((orb ^ (2 * far + core)) * width, width), width)
-            for z in range(top.shape[3]):
-                for y in range(PAIR):
-                    start = ((level ^ z) * PAIR + (pair ^ y)) * coarse
-                    whole[pl.ds(pl.multiple_of(start, coarse), coarse), lanes] = top[core, far, y, z]
-                    start = ((level ^ (z + top.shape[3])) * PAIR + (pair ^ y)) * coarse
-                    whole[pl.ds(pl.multiple_of(start, coarse), coarse), lanes] = low[core, y, far, z]
+            for y in range(PAIR):
+                start = ((orb ^ (2 * far + core)) * PAIR + (pair ^ y)) * coarse
+                rows = pl.ds(pl.multiple_of(start, coarse), coarse)
+                for z in range(top.shape[3]):
+                    lanes = pl.ds(pl.multiple_of((level ^ z) * width, width), width)
+                    whole[rows, lanes] = top[core, far, y, z]
+                    lanes = pl.ds(pl.multiple_of((level ^ (z + top.shape[3])) * width, width), width)
+                    whole[rows, lanes] = low[core, y, far, z]
     row0 = pl.multiple_of((level * PAIR + pair) * coarse, coarse)
     own_lanes = pl.ds(pl.multiple_of(orb * width, width), width)
     rows = whole[pl.ds(row0, coarse), :]
@@ -306,12 +330,11 @@
     def finish(t, carry):
         for i in range(edge):
             rows = slice(i * square, (i + 1) * square)
-            exact = pot[t, rows, :] * x[t, i, :square, :].astype(f32)
-            lost = exact.astype(bf16).astype(f32) - exact
-            whole = total[t, i, :square, :] + exact
+            weighted = (pot[t, rows, :] * x[t, i, :square, :].astype(f32)).astype(bf16)
+            whole = total[t, i, :square, :] + weighted.astype(f32)
             top = whole.astype(bf16)
             low = (whole - top.astype(f32)).astype(bf16)
-            fix = (total_fix[t, i, :square, :] + lost).astype(bf16)
+            fix = total_fix[t, i, :square, :].astype(bf16)
             out[t, rows, :] = jnp.concatenate([top, low, fix], axis=1)
         return carry
 
@@ -395,8 +418,8 @@
     far = {q: swap(active, "orb", q) for q in groups if q and q % 2 == 0}
     beside = swap(theirs, "pair", 1)
     lower, upper = shift(mine, "lvl", 1), shift(mine, "lvl", -1)
-    beside_rest = swap(mine, "pair", 1)
-    later_pot, beside = lax.optimization_barrier((potential, beside))
+    later_pot, later_mine, beside = lax.optimization_barrier((potential, mine, beside))
+    beside_rest = swap(later_mine, "pair", 1)
     lower_beside, upper_beside = shift(beside, "lvl", 1), shift(beside, "lvl", -1)
     other_pot = swap(later_pot, "pair", 1)
     matrices = block_matrices(deriv_blocks)
@@ -414,8 +437,9 @@
     beside_all = jnp.concatenate(
         [jnp.where(first, beside_half, rest_half), jnp.where(first, rest_half, beside_half)], axis=2
     )
-    cut = slots // 2
-    cross = {q: (swap(beside_all[:cut], "orb", q), swap(far[q][cut:], "pair", 1)) for q in far}
+    flat = lambda block: block.reshape(-1, block.shape[-1])
+    cut = -(-slots * coefficients // (2 * ROWS)) * ROWS
+    cross = {q: (swap(flat(beside_all)[:cut], "orb", q), swap(flat(far[q])[cut:], "pair", 1)) for q in far}
     left_own = {0: active, 1: swap(active, "orb", 1), **far}
     left_beside = {0: beside_all, 1: swap(beside_all, "orb", 1)}
     for q in far:
@@ -464,82 +488,86 @@
     def natural(blocks):
         return jnp.concatenate([lax.dynamic_index_in_dim(blocks, orb ^ j, keepdims=False) for j in groups], axis=1)
 
-    def deliver(block, step):
-        to = [(z * orb_count + o, o * orb_count + (z ^ step)) for z in range(level_count) for o in groups]
-        return lax.ppermute(block, ("lvl", "orb"), to)
+    def along_levels(blocks):
+        mine_block = lambda target: lax.dynamic_index_in_dim(blocks, orb ^ target, keepdims=False)
+        steps = range(1, level_count)
+        return mine_block(level), [swap(mine_block(level ^ step), "lvl", step) for step in steps]
+
+    def add(parts):
+        own, got = parts
+        return own.astype(f32) + sum(block.astype(f32) for block in got)
+
+    def turned_rows(strip):
+        pieces = []
+        for over in range(PAIR):
+            to_first = (pair ^ over) == 0
+            piece = jnp.where(to_first, strip[:, :half], strip[:, half:])
+            pieces.append((swap(piece, "pair", over) if over else piece).T)
+        own, other = pieces
+        return jnp.concatenate([jnp.where(first, own, other), jnp.where(first, other, own)], axis=1)
 
     def own_block(strip):
         strip = lax.all_gather(lax.psum(strip, "lvl"), ("orb", "pair"), axis=0, tiled=True)
         strip = lax.dynamic_slice_in_dim(strip, row0, box_rows, axis=0)
         return lax.dynamic_slice_in_dim(strip, col0, own_width, axis=1)
 
-    apart = orb ^ level if square_grid else 0 * orb
-    meta = jnp.stack([pair, apart]).astype(jnp.int32)
+    meta = jnp.stack([pair, level, orb]).astype(jnp.int32)
 
     parts = [mine, beside, lower, lower_beside, upper, upper_beside]
     right = kinetic(parts, pot, matrices, table, scale, edge, coefficients)
 
     cross, right, meta = lax.optimization_barrier((cross, right, meta))
+    lefts_own = [[flat(left_own[q])] for q in groups]
+    lefts_beside = {q: [flat(block)] for q, block in left_beside.items()}
     for q in far:
-        left_beside[q] = jnp.concatenate(cross[q])
-        left_beside[q + 1] = swap(left_beside[q], "orb", 1)
-    flat = lambda block: block.reshape(slots * coefficients, block.shape[-1])
-    lefts_own = [flat(left_own[q]) for q in groups]
-    lefts_beside = [flat(left_beside[q]) for q in groups]
+        lefts_beside[q] = list(cross[q])
+        lefts_beside[q + 1] = [swap(piece, "orb", 1) for piece in cross[q]]
+    lefts_beside = [lefts_beside[q] for q in groups]
 
     share = 1.0 / level_count
     blocks = box_correlation(share, meta, lefts_own, None, half)
     blocks = box_correlation(share, meta, lefts_beside, blocks, half)
+    right = right.reshape(2, slots * coefficients, 3 * half)
+    fock_blocks = fock_rows(lefts_own + lefts_beside, right)
     if square_grid:
-        offset = sum(deliver(blocks[step], step).astype(f32) for step in groups)
+        sent = along_levels(blocks)
+        sent, fock_blocks = lax.optimization_barrier((sent, fock_blocks))
+        offset_turned = add(sent)
+        small = offset_turned.astype(bf16)
+        offset = turned_rows(offset_turned)
     else:
         offset = own_block(natural(blocks).astype(f32))
     row_ids = row0 + jnp.arange(box_rows, dtype=jnp.int32)
     col_ids = col0 + jnp.arange(own_width, dtype=jnp.int32)
     correlation = offset + (row_ids[:, None] == col_ids[None, :]).astype(f32)
-    small = offset.astype(bf16)
-
-    right = right.reshape(2, slots * coefficients, 3 * half)
-    blocks = fock_rows(meta, lefts_own + lefts_beside, right)
     if square_grid:
         pieces = [small] + [swap(small, "lvl", z) for z in range(1, level_count)]
-        early = orb_count // 2
-        pieces, blocks = lax.optimization_barrier((pieces, blocks))
+        pieces, fock_blocks = lax.optimization_barrier((pieces, fock_blocks))
+        sent = along_levels(fock_blocks)
         far_of = range(0, orb_count, 2)
         top = jnp.stack(pieces[: level_count // 2])
         low = jnp.stack(pieces[level_count // 2 :])
         top = spread(spread(top, "pair", (0, 1)), "orb", far_of)
         low = spread(spread(low, "orb", far_of), "pair", (0, 1))
-        got = [deliver(blocks[step], step) for step in range(early)]
-        top, low, blocks = lax.optimization_barrier((top, low, blocks))
-        got += [deliver(blocks[step], step) for step in range(early, orb_count)]
         top, low = spread(top, "orb", (0, 1)), spread(low, "orb", (0, 1))
-        sums = sum(block.astype(f32) for block in got)
-        share = sums[2].astype(bf16)
-        pieces = []
-        for over in range(PAIR):
-            to_first = (pair ^ over) == 0
-            sent = jnp.where(to_first, share[:, :half], share[:, half:])
-            to = [
-                ((z * PAIR + y) * orb_count + o, (o * PAIR + (y ^ over)) * orb_count + z)
-                for z in range(level_count)
-                for y in range(PAIR)
-                for o in groups
-            ]
-            pieces.append(lax.ppermute(sent, BOX + ("orb",), to).astype(f32).T)
-        turned = jnp.concatenate(
-            [jnp.where(first, pieces[0], pieces[1]), jnp.where(first, pieces[1], pieces[0])], axis=1
-        )
-        fock = sums[0] + sums[1] + turned
+        sums = add(sent)
+        main = turned_rows(sums[0] + sums[1])
+        to = [
+            ((z * PAIR + y) * orb_count + o, (o * PAIR + y) * orb_count + z)
+            for z in range(level_count)
+            for y in range(PAIR)
+            for o in groups
+        ]
+        fock = main + lax.ppermute(sums[2].astype(bf16), BOX + ("orb",), to).astype(f32)
     else:
-        fock = own_block(natural(blocks[:, 0]).astype(f32) + natural(blocks[:, 1]).astype(f32))
-        share = lax.all_gather(lax.psum(natural(blocks[:, 2]).astype(f32), "lvl"), "pair", axis=0, tiled=True)
-        fock = fock + lax.dynamic_slice_in_dim(share, row0, box_rows, axis=1).T
+        main = natural(fock_blocks[:, 0]).astype(f32) + natural(fock_blocks[:, 1]).astype(f32)
+        main = lax.all_gather(lax.psum(main, "lvl"), "pair", axis=0, tiled=True)
+        fock = lax.dynamic_slice_in_dim(main, row0, box_rows, axis=1).T + own_block(natural(fock_blocks[:, 2]).astype(f32))
 
     if square_grid:
         inverse_root = root_of(jnp.stack([level, pair, orb]).astype(jnp.int32), top, low, offset, all_width)
     else:
-        gathered = lax.all_gather(small, "orb", axis=1, tiled=True)
+        gathered = lax.all_gather(offset.astype(bf16), "orb", axis=1, tiled=True)
         whole = lax.all_gather(gathered, BOX, axis=0, tiled=True)
         rows_of = lax.dynamic_slice_in_dim(whole, row0, box_rows, axis=0)
         cols_of = lax.dynamic_slice_in_dim(whole, col0, own_width, axis=1)

time: 307 us -> 262 us (0.85)
  waiting for transfers between devices: 107 us -> 56.1 us
  starting transfers between devices: 79.4 us -> 56.5 us
  local copies, waits for them, and re-layouts: 20.9 us -> 41.3 us
  other arithmetic: 23.5 us -> 34.2 us
  Pallas kernels: 68.1 us -> 64.2 us
    ppermute x10 -> x1, waiting for transfers between devices: 51 us -> 5.18 us  [body(): lax.ppermute(sums[2].astype(bf16), BOX + ('orb',), to).astype(f32)]
    ppermute x10 -> x1, starting transfers between devices: 47 us -> 2.07 us  [body(): lax.ppermute(sums[2].astype(bf16), BOX + ('orb',), to).astype(f32)]
    ppermute x19 -> x28, starting transfers between devices: 21.1 us -> 42.3 us  [swap(): return lax.ppermute(value, axis, [(i, i ^ bit) for i in range(count)])]
    another operation x0 -> x6, local copies, waits for them, and re-layouts: none -> 14.4 us  [spread(): return jnp.stack([swap(value, axis, bit) if bit else value for bit in bits])]
    another operation x8, other arithmetic: 3.66 us -> 16.8 us  [spread(): return jnp.stack([swap(value, axis, bit) if bit else value for bit in bits])]
    ppermute x4, waiting for transfers between devices: 11.6 us -> 0.22 us  [shift(): lax.ppermute(value, axis, [(i, i + step) for i in range(count) if 0 <= i...]
    ppermute x0 -> x5, local copies, waits for them, and re-layouts: none -> 9.68 us  [swap(): return lax.ppermute(value, axis, [(i, i ^ bit) for i in range(count)])]
    ppermute x19 -> x28, waiting for transfers between devices: 44.6 us -> 50.7 us  [swap(): return lax.ppermute(value, axis, [(i, i ^ bit) for i in range(count)])]
  transfers between devices with their start and end apart: 33 -> 33, of which waited for: 11 -> 9; matrix products, arithmetic and copies ran while one was open for 11% -> 21% of each run, Pallas kernels for 17% -> 19%
where the time goes in v3:
time: 262 us; the launch traced here: 259 us
  Pallas kernels  64.2 us (25%)
  starting transfers between devices  56.5 us (22%)
  waiting for transfers between devices  56.1 us (21%)
  local copies, waits for them, and re-layouts  41.3 us (16%)
  other arithmetic  34.2 us (13%)
  matrix products  4.85 us (2%)
    ppermute x28, waiting for transfers between devices, swap(): return lax.ppermute(value, axis, [(i, i ^ bit) for i in range(count)])  50.7 us
    ppermute x28, starting transfers between devices, swap(): return lax.ppermute(value, axis, [(i, i ^ bit) for i in range(count)])  42.3 us
    pallas_call x1, Pallas kernels, kinetic(): pl.pallas_call(functools.partial(kinetic_kernel, edge, slots), out_shape=...  30 us
    another operation x8, other arithmetic, spread(): return jnp.stack([swap(value, axis, bit) if bit else value for bit in bits])  16.8 us
    pallas_call x1, Pallas kernels, fock_rows(): pl.pallas_call(functools.partial(fock_kernel, counts), out_shape=jax.Shap...  14.6 us
    another operation x6, local copies, waits for them, and re-layouts, spread(): return jnp.stack([swap(value, axis, bit) if bit else value for bit in bits])  14.4 us
    ppermute x4, starting transfers between devices, shift(): lax.ppermute(value, axis, [(i, i + step) for i in range(count) if 0 <= i...  12.2 us
    ppermute x5, local copies, waits for them, and re-layouts, swap(): return lax.ppermute(value, axis, [(i, i ^ bit) for i in range(count)])  9.68 us
  transfers between devices with their start and end apart: 33, of which 9 were waited for; matrix products, arithmetic and copies ran while one was open for 21% of the time, Pallas kernels for 19%

profile of v3, /device:TPU:2, one launch (start us, length us, event | category | flops | bytes accessed | tf_op | source)
XLA Modules:
  0.0 259.0 jit_solution(2933987921185951487)
XLA Ops:
  3.7 1.4 copy-done.2
  5.1 2.9 %pack.1 = (bf16[2,1000,384]{2,1,0:T(8,128)(2,1)}, bf16[2,512,384]{2,1,0:T(8,128)(2,1)}, bf16[2,512,384]{2,1,0:T(8,128)(2,1)}) custom-call(s32[2]{0:T(128)S(1)} %pad_add_fusion.1.meta, bf16[2,1000,384]{2,1,0:T(8,128)(2,1)S(1)} %copy-done.2, f32[2,384]{1,0:T(2,128)S(1)} %pad.4.facts), custom_call_target="tpu_custom_call" | custom-call | tf_op jit(solution)/shard_map/pack/pallas_call | solution.py:68
  8.1 4.5 %collective-permute-start.3 = (bf16[2,512,384]{2,1,0:T(8,128)(2,1)}, bf16[2,512,384]{2,1,0:T(8,128)(2,1)}, u32[]{:S(2)}, u32[]{:S(2)}) collective-permute-start(bf16[2,512,384]{2,1,0:T(8,128)(2,1)} %get-tuple-element.40.refs_0_), channel_id=1, source_target_pairs={{0,8},{8,16},{16,24},{1,9},{9,17},{17,25},{2,10},{10,18},{18,26},{... | collective-permute-start | bytes 2359304 | tf_op jit(solution)/shard_map/ppermute | solution.py:24
  14.4 1.6 collective-permute-start.1
  22.9 10.5 %collective-permute-done.1.refs_1_ = bf16[2,512,384]{2,1,0:T(8,128)(2,1)S(1)} collective-permute-done((bf16[2,512,384]{2,1,0:T(8,128)(2,1)}, bf16[2,512,384]{2,1,0:T(8,128)(2,1)S(1)}, u32[]{:S(2)}, u32[]{:S(2)}) %collective-permute-start.1) | collective-permute-done | bytes 786464 | tf_op jit(solution)/shard_map/ppermute | solution.py:19
  33.4 5.1 %collective-permute-start.5 = (bf16[2,512,384]{2,1,0:T(8,128)(2,1)S(1)}, bf16[2,512,384]{2,1,0:T(8,128)(2,1)}, u32[]{:S(2)}, u32[]{:S(2)}) collective-permute-start(bf16[2,512,384]{2,1,0:T(8,128)(2,1)S(1)} %collective-permute-done.1.refs_1_), channel_id=1, source_target_pairs={{0,8},{8,16},{16,24},{1,9},{9,17},{17,25},{2,10},{10,18},{18,26},{... | collective-permute-start | bytes 2359304 | tf_op jit(solution)/shard_map/ppermute | solution.py:24
  39.9 1.6 collective-permute-start.2
  42.7 1.4 fusion.1.refs_8_
  45.5 12.2 %collective-permute-done.7 = f32[2,1000]{1,0:T(2,128)S(1)} collective-permute-done((f32[2,1000]{1,0:T(2,128)}, f32[2,1000]{1,0:T(2,128)S(1)}, u32[]{:S(2)}, u32[]{:S(2)}) %collective-permute-start.7) | collective-permute-done | bytes 8032 | tf_op jit(solution)/shard_map/ppermute | solution.py:19
  59.9 1.7 fusion.48
  62.2 1.8 pad_maximum_fusion.5
  65.2 1.4 collective-permute-start.8
  67.6 1.5 collective-permute-start.9
  69.2 2.0 copy.81.refs_6_
  71.7 30.0 %kinetic.1 = bf16[4,1000,576]{2,1,0:T(8,128)(2,1)} custom-call(s32[8,10]{1,0:T(8,128)S(1)} %stack.127.table, f32[8]{0:T(128)S(1)} %select_reduce_fusion.scale, bf16[2,512,384]{2,1,0:T(8,128)(2,1)} %get-tuple-element.40.refs_0_, bf16[2,512,384]{2,1,0:T(8,128)(2,1)S(1)} %collective-permute-done.1.refs_1_, bf16[2,512,384]{2,1,0:T(8,128)(2,1)} %collective-permute-done.3.refs_2_, ...), custom_call_target="tpu_custom_call" | custom-call | flops 20000000000 | bytes 40000000 | tf_op jit(solution)/shard_map/kinetic/pallas_call | solution.py:376
  102.4 2.1 pad_maximum_fusion.2.refs_0_.refs_4_
  104.6 4.3 %correlation.2.refs_6_ = f32[4,192,384]{2,1,0:T(8,128)S(1)} custom-call(s32[3]{0:T(128)S(1)} %add_add_fusion.1.meta, bf16[2000,384]{1,0:T(8,128)(2,1)} %bitcast.31.refs_0_, bf16[2000,384]{1,0:T(8,128)(2,1)} %bitcast.32.refs_1_, bf16[2000,384]{1,0:T(8,128)(2,1)S(1)} %bitcast.117, bf16[2000,384]{1,0:T(8,128)(2,1)} %bitcast.33.refs_3_), custom_call_target="tpu_custom_call" | custom-call | flops 1179648000 | bytes 6144000 | tf_op jit(solution)/shard_map/correlation/pallas_call | solution.py:127
  109.0 4.5 %correlation.3 = bf16[4,192,384]{2,1,0:T(8,128)(2,1)S(1)} custom-call(s32[3]{0:T(128)S(1)} %add_add_fusion.1.meta, bf16[2000,384]{1,0:T(8,128)(2,1)S(1)} %pad_maximum_fusion.2.refs_0_.refs_4_, bf16[2000,384]{1,0:T(8,128)(2,1)} %bitcast.30.refs_1_.refs_5_, bf16[1008,384]{1,0:T(8,128)(2,1)} %collective-permute-done.8.refs_2_.refs_6_, ...), custom_call_target="tpu_custom_call" | custom-call | flops 1179648000 | bytes 6144000 | tf_op jit(solution)/shard_map/correlation/pallas_call | solution.py:127
  114.6 4.3 %collective-permute-start.16 = (bf16[192,384]{0,1:T(8,128)(2,1)}, bf16[192,384]{0,1:T(8,128)(2,1)}, u32[]{:S(2)}, u32[]{:S(2)}) collective-permute-start(bf16[192,384]{0,1:T(8,128)(2,1)} %bitcast.36), channel_id=1, source_target_pairs={{0,16},{8,24},{16,0},{24,8},{1,17},{9,25},{17,1},{25,9},{2,18},{10... | collective-permute-start | bytes 442376 | tf_op jit(solution)/shard_map/ppermute | solution.py:19
  119.8 14.6 %fock.1 = bf16[4,3,192,384]{3,2,1,0:T(8,128)(2,1)} custom-call(bf16[2000,384]{1,0:T(8,128)(2,1)} %bitcast.31.refs_0_, bf16[2000,384]{1,0:T(8,128)(2,1)} %bitcast.32.refs_1_, bf16[2000,384]{1,0:T(8,128)(2,1)S(1)} %bitcast.118, bf16[2000,384]{1,0:T(8,128)(2,1)} %bitcast.33.refs_3_, bf16[2000,384]{1,0:T(8,128)(2,1)} %copy-done.1, ...), custom_call_target="tpu_custom_call" | custom-call | flops 7077888000 | bytes 12288000 | tf_op jit(solution)/shard_map/fock/pallas_call | solution.py:185
  134.6 1.3 fusion.46
  135.9 2.9 %collective-permute-start.18 = (bf16[192,384]{0,1:T(8,128)(2,1)S(1)}, bf16[192,384]{0,1:T(8,128)(2,1)S(1)}, u32[]{:S(2)}, u32[]{:S(2)}) collective-permute-start(bf16[192,384]{0,1:T(8,128)(2,1)S(1)} %get-tuple-element.65), channel_id=1, source_target_pairs={{0,8},{8,0},{16,24},{24,16},{1,9},{9,1},{17,25},{25,17},{2,10},{10... | collective-permute-start | bytes 442376 | tf_op jit(solution)/shard_map/ppermute | solution.py:19
  138.7 1.5 collective-permute-start.19
  141.7 4.5 %collective-permute-done.18 = bf16[192,384]{0,1:T(8,128)(2,1)S(1)} collective-permute-done((bf16[192,384]{0,1:T(8,128)(2,1)S(1)}, bf16[192,384]{0,1:T(8,128)(2,1)S(1)}, u32[]{:S(2)}, u32[]{:S(2)}) %collective-permute-start.18) | collective-permute-done | bytes 147488 | tf_op jit(solution)/shard_map/ppermute | solution.py:19
  146.2 9.7 %collective-permute-done.19 = bf16[192,384]{0,1:T(8,128)(2,1)S(1)} collective-permute-done((bf16[192,384]{0,1:T(8,128)(2,1)S(1)}, bf16[192,384]{0,1:T(8,128)(2,1)S(1)}, u32[]{:S(2)}, u32[]{:S(2)}) %collective-permute-start.19) | collective-permute-done | bytes 147488 | tf_op jit(solution)/shard_map/ppermute | solution.py:19
  157.0 2.2 collective-permute-start.23
  159.2 16.9 %collective-permute-start.22 = (bf16[3,192,384]{2,1,0:T(8,128)(2,1)}, bf16[3,192,384]{2,1,0:T(8,128)(2,1)}, u32[]{:S(2)}, u32[]{:S(2)}) collective-permute-start(bf16[3,192,384]{2,1,0:T(8,128)(2,1)} %get-tuple-element.81), channel_id=1, source_target_pairs={{0,16},{8,24},{16,0},{24,8},{1,17},{9,25},{17,1},{25,9},{2,18},{10... | collective-permute-start | bytes 1327112 | tf_op jit(solution)/shard_map/ppermute | solution.py:19
  179.5 5.1 %collective-permute-done.27 = bf16[2,192,384]{1,2,0:T(8,128)(2,1)S(1)} collective-permute-done((bf16[2,192,384]{1,2,0:T(8,128)(2,1)S(1)}, bf16[2,192,384]{1,2,0:T(8,128)(2,1)S(1)}, u32[]{:S(2)}, u32[]{:S(2)}) %collective-permute-start.27) | collective-permute-done | bytes 294944 | tf_op jit(solution)/shard_map/ppermute | solution.py:19
  186.0 1.5 collective-permute-start.28
  190.9 5.4 %collective-permute-done.22 = bf16[3,192,384]{2,1,0:T(8,128)(2,1)} collective-permute-done((bf16[3,192,384]{2,1,0:T(8,128)(2,1)}, bf16[3,192,384]{2,1,0:T(8,128)(2,1)}, u32[]{:S(2)}, u32[]{:S(2)}) %collective-permute-start.22) | collective-permute-done | bytes 442400 | tf_op jit(solution)/shard_map/ppermute | solution.py:19
  196.3 1.6 convert_add_fusion
  199.3 2.2 copy.96
  201.5 2.9 %fusion.45 = (bf16[1,2,2,2,192,384]{4,5,3,2,1,0:T(8,128)(2,1)S(1)}, bf16[2,2,2,192,384]{3,4,2,1,0:T(8,128)(2,1)}) fusion(bf16[1,2,2,192,384]{3,4,2,1,0:T(8,128)(2,1)} %bitcast.125, bf16[1,2,2,192,384]{3,4,2,1,0:T(8,128)(2,1)} %get-tuple-element.88), kind=kLoop, calls=%fused_computation.136 | loop fusion | flops 589824 | bytes 3538944 | tf_op jit(solution)/shard_map/stack | solution.py:36
  204.4 2.5 copy.97
  206.9 2.3 copy.100
  209.2 3.1 %fusion.44 = (bf16[1,2,2,2,192,384]{4,5,3,2,1,0:T(8,128)(2,1)}, bf16[2,2,2,192,384]{3,4,2,1,0:T(8,128)(2,1)}) fusion(bf16[1,2,2,192,384]{3,4,2,1,0:T(8,128)(2,1)} %bitcast.126, bf16[1,2,2,192,384]{3,4,2,1,0:T(8,128)(2,1)S(1)} %get-tuple-element.86), kind=kLoop, calls=%fused_computation.135 | loop fusion | flops 589824 | bytes 3538944 | tf_op jit(solution)/shard_map/stack | solution.py:36
  212.3 2.5 copy.101
  216.8 2.1 collective-permute-start.25
  218.9 3.3 %collective-permute-done.24 = f32[192,192]{0,1:T(8,128)S(1)} collective-permute-done((f32[192,192]{0,1:T(8,128)S(1)}, f32[192,192]{0,1:T(8,128)S(1)}, u32[]{:S(2)}, u32[]{:S(2)}) %collective-permute-start.24) | collective-permute-done | bytes 147488 | tf_op jit(solution)/shard_map/ppermute | solution.py:19
  222.7 5.2 %collective-permute-done.25 = bf16[192,384]{1,0:T(8,128)(2,1)S(1)} collective-permute-done((bf16[192,384]{1,0:T(8,128)(2,1)S(1)}, bf16[192,384]{1,0:T(8,128)(2,1)S(1)}, u32[]{:S(2)}, u32[]{:S(2)}) %collective-permute-start.25) | collective-permute-done | bytes 147488 | tf_op jit(solution)/shard_map/ppermute | solution.py:561
  228.8 2.5 copy.98
  231.3 3.7 %pad_maximum_fusion = bf16[2,2,2,2,192,384]{4,5,3,2,1,0:T(8,128)(2,1)} fusion(bf16[1,2,2,2,192,384]{4,5,3,2,1,0:T(8,128)(2,1)} %bitcast.123, bf16[1,2,2,2,192,384]{4,5,3,2,1,0:T(8,128)(2,1)S(1)} %get-tuple-element.84), kind=kLoop, calls=%fused_computation | loop fusion | flops 1179648 | bytes 4718592 | tf_op jit(solution)/shard_map/stack | solution.py:36
  234.9 3.4 %copy.103.top = bf16[2,2,2,2,192,384]{5,4,3,2,1,0:T(8,128)(2,1)S(1)} copy(bf16[2,2,2,2,192,384]{4,5,3,2,1,0:T(8,128)(2,1)} %pad_maximum_fusion) | data formatting | bytes 4718592 | tf_op jit(solution)/shard_map/stack | solution.py:36
  238.3 2.5 copy.102
  240.8 4.1 %pad_maximum_fusion.1 = bf16[2,2,2,2,192,384]{4,5,3,2,1,0:T(8,128)(2,1)} fusion(bf16[1,2,2,2,192,384]{4,5,3,2,1,0:T(8,128)(2,1)} %bitcast.124, bf16[1,2,2,2,192,384]{4,5,3,2,1,0:T(8,128)(2,1)} %get-tuple-element.82), kind=kLoop, calls=%fused_computation.1 | loop fusion | flops 1179648 | bytes 4718592 | tf_op jit(solution)/shard_map/stack | solution.py:36
  245.0 4.5 %copy.104.low = bf16[2,2,2,2,192,384]{5,4,3,2,1,0:T(8,128)(2,1)} copy(bf16[2,2,2,2,192,384]{4,5,3,2,1,0:T(8,128)(2,1)} %pad_maximum_fusion.1) | data formatting | bytes 4718592 | tf_op jit(solution)/shard_map/stack | solution.py:36
  249.5 1.7 copy-done
  251.2 7.9 %root.1 = f32[192,384]{1,0:T(8,128)} custom-call(s32[3]{0:T(128)S(1)} %add_add_fusion.2.meta, bf16[2,2,2,2,192,384]{5,4,3,2,1,0:T(8,128)(2,1)S(1)} %copy.103.top, bf16[2,2,2,2,192,384]{5,4,3,2,1,0:T(8,128)(2,1)S(1)} %copy-done, f32[192,384]{1,0:T(8,128)S(1)} %get-tuple-element.70.offset), custom_call_target="tpu_custom_call" | custom-call | tf_op jit(solution)/shard_map/root/pallas_call | solution.py:249
  (163 shorter events, 38.9 us)
Async XLA Ops:
  0.6 17.9 %copy-start.13 = (f32[112,112]{0,1:T(8,128)S(1)}, f32[112,112]{0,1:T(8,128)}, u32[]{:S(2)}) copy-start(f32[112,112]{0,1:T(8,128)} %constant.171) | copy-start | bytes 150532
  0.6 17.8 %copy-start.8 = (bf16[3,10,10]{2,0,1:T(4,128)(2,1)S(1)}, bf16[3,10,10]{2,0,1:T(4,128)(2,1)}, u32[]{:S(2)}) copy-start(bf16[3,10,10]{2,0,1:T(4,128)(2,1)} %param.17) | copy-start | bytes 1804
  1.4 13.0 %copy-start.20 = (s32[2,1]{1,0:T(2,128)}, s32[2,1]{1,0:T(2,128)S(1)}, u32[]{:S(2)}) copy-start(s32[2,1]{1,0:T(2,128)S(1)} %compare_convert_fusion) | copy-start | bytes 28
  2.2 12.3 %copy-start.21 = (s32[2,1]{1,0:T(2,128)}, s32[2,1]{1,0:T(2,128)S(1)}, u32[]{:S(2)}) copy-start(s32[2,1]{1,0:T(2,128)S(1)} %copy.68) | copy-start | bytes 28
  3.6 10.8 %copy-start.18 = (s32[2,6]{1,0:T(2,128)}, s32[2,6]{1,0:T(2,128)S(1)}, u32[]{:S(2)}) copy-start(s32[2,6]{1,0:T(2,128)S(1)} %reshape.359) | copy-start | bytes 148
  5.1 13.2 %copy-start.14 = (f32[112,112]{0,1:T(8,128)S(1)}, f32[112,112]{0,1:T(8,128)}, u32[]{:S(2)}) copy-start(f32[112,112]{0,1:T(8,128)} %constant.172) | copy-start | bytes 150532
  5.1 13.6 %copy-start.9 = (f32[160,160]{0,1:T(8,128)S(1)}, f32[160,160]{0,1:T(8,128)}, u32[]{:S(2)}) copy-start(f32[160,160]{0,1:T(8,128)} %constant.173) | copy-start | bytes 307204
  8.1 11.7 %copy-start.12 = (f32[112,112]{1,0:T(8,128)S(1)}, f32[112,112]{1,0:T(8,128)}, u32[]{:S(2)}) copy-start(f32[112,112]{1,0:T(8,128)} %constant.159.clone) | copy-start | bytes 150532
  8.1 11.7 %copy-start.17 = (bf16[112,10,1]{0,1,2:T(8,128)(2,1)S(1)}, bf16[112,10,1]{0,1,2:T(8,128)(2,1)}, u32[]{:S(2)}) copy-start(bf16[112,10,1]{0,1,2:T(8,128)(2,1)} %constant.175) | copy-start | bytes 6724
  8.1 12.0 %copy-start.11 = (f32[112,112]{1,0:T(8,128)S(1)}, f32[112,112]{1,0:T(8,128)}, u32[]{:S(2)}) copy-start(f32[112,112]{1,0:T(8,128)} %constant.156.clone) | copy-start | bytes 150532
  8.1 12.1 %copy-start.16 = (bf16[112,10,1]{0,1,2:T(8,128)(2,1)S(1)}, bf16[112,10,1]{0,1,2:T(8,128)(2,1)}, u32[]{:S(2)}) copy-start(bf16[112,10,1]{0,1,2:T(8,128)(2,1)} %constant.174) | copy-start | bytes 6724
  8.1 31.8 %collective-permute-start.3 = (bf16[2,512,384]{2,1,0:T(8,128)(2,1)}, bf16[2,512,384]{2,1,0:T(8,128)(2,1)}, u32[]{:S(2)}, u32[]{:S(2)}) collective-permute-start(bf16[2,512,384]{2,1,0:T(8,128)(2,1)} %get-tuple-element.40.refs_0_), channel_id=1, source_target_pairs={{0,8},{8,16},{16,24},{1,9},{9,17},{17,25},{2,10},{10,18},{18,26},{... | collective-permute-start | bytes 2359304 | tf_op jit(solution)/shard_map/ppermute | solution.py:24
  12.6 31.5 %collective-permute-start.4 = (bf16[2,512,384]{2,1,0:T(8,128)(2,1)}, bf16[2,512,384]{2,1,0:T(8,128)(2,1)}, u32[]{:S(2)}, u32[]{:S(2)}) collective-permute-start(bf16[2,512,384]{2,1,0:T(8,128)(2,1)} %get-tuple-element.40.refs_0_), channel_id=1, source_target_pairs={{8,0},{16,8},{24,16},{9,1},{17,9},{25,17},{10,2},{18,10},{26,18},{... | collective-permute-start | bytes 2359304 | tf_op jit(solution)/shard_map/ppermute | solution.py:24
  13.8 43.9 %collective-permute-start = (bf16[2,1000,384]{2,1,0:T(8,128)(2,1)}, bf16[2,1000,384]{2,1,0:T(8,128)(2,1)S(1)}, u32[]{:S(2)}, u32[]{:S(2)}) collective-permute-start(bf16[2,1000,384]{2,1,0:T(8,128)(2,1)} %get-tuple-element.57), channel_id=1, source_target_pairs={{0,2},{1,3},{2,0},{3,1},{4,6},{5,7},{6,4},{7,5},{8,10},{9,11},{10,... | collective-permute-start | bytes 4608008 | tf_op jit(solution)/shard_map/ppermute | solution.py:19
  14.4 19.0 %collective-permute-start.1 = (bf16[2,512,384]{2,1,0:T(8,128)(2,1)}, bf16[2,512,384]{2,1,0:T(8,128)(2,1)S(1)}, u32[]{:S(2)}, u32[]{:S(2)}) collective-permute-start(bf16[2,512,384]{2,1,0:T(8,128)(2,1)} %get-tuple-element.38), channel_id=1, source_target_pairs={{0,4},{4,0},{1,5},{5,1},{2,6},{6,2},{3,7},{7,3},{8,12},{12,8},{9,1... | collective-permute-start | bytes 2359304 | tf_op jit(solution)/shard_map/ppermute | solution.py:19
  18.7 23.5 %copy-start.15 = (bf16[160,10,1]{0,1,2:T(8,128)(2,1)S(1)}, bf16[160,10,1]{0,1,2:T(8,128)(2,1)}, u32[]{:S(2)}) copy-start(bf16[160,10,1]{0,1,2:T(8,128)(2,1)} %constant.176) | copy-start | bytes 9604
  18.8 23.5 %copy-start.10 = (f32[160,160]{1,0:T(8,128)S(1)}, f32[160,160]{1,0:T(8,128)}, u32[]{:S(2)}) copy-start(f32[160,160]{1,0:T(8,128)} %constant.162.clone) | copy-start | bytes 307204
  33.4 24.3 %collective-permute-start.5 = (bf16[2,512,384]{2,1,0:T(8,128)(2,1)S(1)}, bf16[2,512,384]{2,1,0:T(8,128)(2,1)}, u32[]{:S(2)}, u32[]{:S(2)}) collective-permute-start(bf16[2,512,384]{2,1,0:T(8,128)(2,1)S(1)} %collective-permute-done.1.refs_1_), channel_id=1, source_target_pairs={{0,8},{8,16},{16,24},{1,9},{9,17},{17,25},{2,10},{10,18},{18,26},{... | collective-permute-start | bytes 2359304 | tf_op jit(solution)/shard_map/ppermute | solution.py:24
  38.6 19.3 %collective-permute-start.6 = (bf16[2,512,384]{2,1,0:T(8,128)(2,1)S(1)}, bf16[2,512,384]{2,1,0:T(8,128)(2,1)}, u32[]{:S(2)}, u32[]{:S(2)}) collective-permute-start(bf16[2,512,384]{2,1,0:T(8,128)(2,1)S(1)} %collective-permute-done.1.refs_1_), channel_id=1, source_target_pairs={{8,0},{16,8},{24,16},{9,1},{17,9},{25,17},{10,2},{18,10},{26,18},{... | collective-permute-start | bytes 2359304 | tf_op jit(solution)/shard_map/ppermute | solution.py:24
  39.9 17.8 %collective-permute-start.2 = (bf16[2,512,384]{2,1,0:T(8,128)(2,1)}, bf16[2,512,384]{2,1,0:T(8,128)(2,1)}, u32[]{:S(2)}, u32[]{:S(2)}) collective-permute-start(bf16[2,512,384]{2,1,0:T(8,128)(2,1)} %get-tuple-element.40.refs_0_), channel_id=1, source_target_pairs={{0,4},{4,0},{1,5},{5,1},{2,6},{6,2},{3,7},{7,3},{8,12},{12,8},{9,1... | collective-permute-start | bytes 2359304 | tf_op jit(solution)/shard_map/ppermute | solution.py:19
  44.1 13.6 %collective-permute-start.7 = (f32[2,1000]{1,0:T(2,128)}, f32[2,1000]{1,0:T(2,128)S(1)}, u32[]{:S(2)}, u32[]{:S(2)}) collective-permute-start(f32[2,1000]{1,0:T(2,128)} %param.16), channel_id=1, source_target_pairs={{0,4},{4,0},{1,5},{5,1},{2,6},{6,2},{3,7},{7,3},{8,12},{12,8},{9,1... | collective-permute-start | bytes 24008 | tf_op jit(solution)/shard_map/ppermute | solution.py:19
  64.0 5.2 %copy-start.19 = (f32[2,1000]{1,0:T(2,128)S(1)}, f32[2,1000]{1,0:T(2,128)}, u32[]{:S(2)}) copy-start(f32[2,1000]{1,0:T(2,128)} %param.16) | copy-start | bytes 24004
  65.2 36.6 %collective-permute-start.8 = (bf16[1008,384]{1,0:T(8,128)(2,1)}, bf16[1008,384]{1,0:T(8,128)(2,1)}, u32[]{:S(2)}, u32[]{:S(2)}) collective-permute-start(bf16[1008,384]{1,0:T(8,128)(2,1)} %fusion.13), channel_id=1, source_target_pairs={{0,2},{1,3},{2,0},{3,1},{4,6},{5,7},{6,4},{7,5},{8,10},{9,11},{10,... | collective-permute-start | bytes 2322440 | tf_op jit(solution)/shard_map/ppermute | solution.py:19
  66.6 38.0 %collective-permute-start.14 = (bf16[2,1000,384]{2,1,0:T(8,128)(2,1)S(1)}, bf16[2,1000,384]{2,1,0:T(8,128)(2,1)}, u32[]{:S(2)}, u32[]{:S(2)}) collective-permute-start(bf16[2,1000,384]{2,1,0:T(8,128)(2,1)S(1)} %collective-permute-done), channel_id=1, source_target_pairs={{0,1},{1,0},{2,3},{3,2},{4,5},{5,4},{6,7},{7,6},{8,9},{9,8},{10,11... | collective-permute-start | bytes 4608008 | tf_op jit(solution)/shard_map/ppermute | solution.py:19
  67.6 34.2 %collective-permute-start.9 = (bf16[992,384]{1,0:T(8,128)(2,1)}, bf16[992,384]{1,0:T(8,128)(2,1)}, u32[]{:S(2)}, u32[]{:S(2)}) collective-permute-start(bf16[992,384]{1,0:T(8,128)(2,1)} %slice.111), channel_id=1, source_target_pairs={{0,4},{4,0},{1,5},{5,1},{2,6},{6,2},{3,7},{7,3},{8,12},{12,8},{9,1... | collective-permute-start | bytes 2285576 | tf_op jit(solution)/shard_map/ppermute | solution.py:19
  71.1 37.8 %collective-permute-start.10 = (bf16[2,1000,384]{2,1,0:T(8,128)(2,1)}, bf16[2,1000,384]{2,1,0:T(8,128)(2,1)}, u32[]{:S(2)}, u32[]{:S(2)}) collective-permute-start(bf16[2,1000,384]{2,1,0:T(8,128)(2,1)} %pad_maximum_fusion.5), channel_id=1, source_target_pairs={{0,1},{1,0},{2,3},{3,2},{4,5},{5,4},{6,7},{7,6},{8,9},{9,8},{10,11... | collective-permute-start | bytes 4608008 | tf_op jit(solution)/shard_map/ppermute | solution.py:19
  71.4 33.2 %collective-permute-start.13 = (bf16[2,1000,384]{2,1,0:T(8,128)(2,1)}, bf16[2,1000,384]{2,1,0:T(8,128)(2,1)}, u32[]{:S(2)}, u32[]{:S(2)}) collective-permute-start(bf16[2,1000,384]{2,1,0:T(8,128)(2,1)} %get-tuple-element.57), channel_id=1, source_target_pairs={{0,1},{1,0},{2,3},{3,2},{4,5},{5,4},{6,7},{7,6},{8,9},{9,8},{10,11... | collective-permute-start | bytes 4608008 | tf_op jit(solution)/shard_map/ppermute | solution.py:19
  101.8 7.2 %collective-permute-start.11 = (bf16[1008,384]{1,0:T(8,128)(2,1)}, bf16[1008,384]{1,0:T(8,128)(2,1)}, u32[]{:S(2)}, u32[]{:S(2)}) collective-permute-start(bf16[1008,384]{1,0:T(8,128)(2,1)} %collective-permute-done.8.refs_2_.refs_6_), channel_id=1, source_target_pairs={{0,1},{1,0},{2,3},{3,2},{4,5},{5,4},{6,7},{7,6},{8,9},{9,8},{10,11... | collective-permute-start | bytes 2322440 | tf_op jit(solution)/shard_map/ppermute | solution.py:19
  102.0 6.9 %collective-permute-start.12 = (bf16[992,384]{1,0:T(8,128)(2,1)}, bf16[992,384]{1,0:T(8,128)(2,1)}, u32[]{:S(2)}, u32[]{:S(2)}) collective-permute-start(bf16[992,384]{1,0:T(8,128)(2,1)} %collective-permute-done.9.refs_3_.refs_7_), channel_id=1, source_target_pairs={{0,1},{1,0},{2,3},{3,2},{4,5},{5,4},{6,7},{7,6},{8,9},{9,8},{10,11... | collective-permute-start | bytes 2285576 | tf_op jit(solution)/shard_map/ppermute | solution.py:19
  113.7 20.9 %collective-permute-start.15 = (bf16[192,384]{0,1:T(8,128)(2,1)S(1)}, bf16[192,384]{0,1:T(8,128)(2,1)}, u32[]{:S(2)}, u32[]{:S(2)}) collective-permute-start(bf16[192,384]{0,1:T(8,128)(2,1)S(1)} %bitcast.138), channel_id=1, source_target_pairs={{0,8},{8,0},{16,24},{24,16},{1,9},{9,1},{17,25},{25,17},{2,10},{10... | collective-permute-start | bytes 442376 | tf_op jit(solution)/shard_map/ppermute | solution.py:19
  114.6 20.0 %collective-permute-start.16 = (bf16[192,384]{0,1:T(8,128)(2,1)}, bf16[192,384]{0,1:T(8,128)(2,1)}, u32[]{:S(2)}, u32[]{:S(2)}) collective-permute-start(bf16[192,384]{0,1:T(8,128)(2,1)} %bitcast.36), channel_id=1, source_target_pairs={{0,16},{8,24},{16,0},{24,8},{1,17},{9,25},{17,1},{25,9},{2,18},{10... | collective-permute-start | bytes 442376 | tf_op jit(solution)/shard_map/ppermute | solution.py:19
  119.7 14.9 %collective-permute-start.17 = (bf16[192,384]{0,1:T(8,128)(2,1)}, bf16[192,384]{0,1:T(8,128)(2,1)}, u32[]{:S(2)}, u32[]{:S(2)}) collective-permute-start(bf16[192,384]{0,1:T(8,128)(2,1)} %bitcast.37), channel_id=1, source_target_pairs={{0,24},{8,16},{16,8},{24,0},{1,25},{9,17},{17,9},{25,1},{2,26},{10... | collective-permute-start | bytes 442376 | tf_op jit(solution)/shard_map/ppermute | solution.py:19
  134.4 21.5 %copy-start.6 = (bf16[4,3,192,384]{3,2,1,0:T(8,128)(2,1)S(1)}, bf16[4,3,192,384]{3,2,1,0:T(8,128)(2,1)}, u32[]{:S(2)}) copy-start(bf16[4,3,192,384]{3,2,1,0:T(8,128)(2,1)} %fock.1) | copy-start | bytes 5308420
  135.9 10.3 %collective-permute-start.18 = (bf16[192,384]{0,1:T(8,128)(2,1)S(1)}, bf16[192,384]{0,1:T(8,128)(2,1)S(1)}, u32[]{:S(2)}, u32[]{:S(2)}) collective-permute-start(bf16[192,384]{0,1:T(8,128)(2,1)S(1)} %get-tuple-element.65), channel_id=1, source_target_pairs={{0,8},{8,0},{16,24},{24,16},{1,9},{9,1},{17,25},{25,17},{2,10},{10... | collective-permute-start | bytes 442376 | tf_op jit(solution)/shard_map/ppermute | solution.py:19
  138.7 17.2 %collective-permute-start.19 = (bf16[192,384]{0,1:T(8,128)(2,1)S(1)}, bf16[192,384]{0,1:T(8,128)(2,1)S(1)}, u32[]{:S(2)}, u32[]{:S(2)}) collective-permute-start(bf16[192,384]{0,1:T(8,128)(2,1)S(1)} %get-tuple-element.65), channel_id=1, source_target_pairs={{0,16},{8,24},{16,0},{24,8},{1,17},{9,25},{17,1},{25,9},{2,18},{10... | collective-permute-start | bytes 442376 | tf_op jit(solution)/shard_map/ppermute | solution.py:19
  140.2 15.7 %collective-permute-start.20 = (bf16[192,384]{0,1:T(8,128)(2,1)S(1)}, bf16[192,384]{0,1:T(8,128)(2,1)S(1)}, u32[]{:S(2)}, u32[]{:S(2)}) collective-permute-start(bf16[192,384]{0,1:T(8,128)(2,1)S(1)} %get-tuple-element.65), channel_id=1, source_target_pairs={{0,24},{8,16},{16,8},{24,0},{1,25},{9,17},{17,9},{25,1},{2,26},{10... | collective-permute-start | bytes 442376 | tf_op jit(solution)/shard_map/ppermute | solution.py:19
  141.2 36.9 %collective-permute-start.26 = (f32[192,192]{0,1:T(8,128)S(1)}, f32[192,192]{0,1:T(8,128)S(1)}, u32[]{:S(2)}, u32[]{:S(2)}) collective-permute-start(f32[192,192]{0,1:T(8,128)S(1)} %slice_select_fusion), channel_id=1, source_target_pairs={{0,4},{4,0},{1,5},{5,1},{2,6},{6,2},{3,7},{7,3},{8,12},{12,8},{9,1... | collective-permute-start | bytes 442376 | tf_op jit(solution)/shard_map/ppermute | solution.py:19
  157.0 33.9 %collective-permute-start.23 = (bf16[3,192,384]{2,1,0:T(8,128)(2,1)}, bf16[3,192,384]{2,1,0:T(8,128)(2,1)}, u32[]{:S(2)}, u32[]{:S(2)}) collective-permute-start(bf16[3,192,384]{2,1,0:T(8,128)(2,1)} %get-tuple-element.80), channel_id=1, source_target_pairs={{0,24},{8,16},{16,8},{24,0},{1,25},{9,17},{17,9},{25,1},{2,26},{10... | collective-permute-start | bytes 1327112 | tf_op jit(solution)/shard_map/ppermute | solution.py:19
  159.2 37.1 %collective-permute-start.22 = (bf16[3,192,384]{2,1,0:T(8,128)(2,1)}, bf16[3,192,384]{2,1,0:T(8,128)(2,1)}, u32[]{:S(2)}, u32[]{:S(2)}) collective-permute-start(bf16[3,192,384]{2,1,0:T(8,128)(2,1)} %get-tuple-element.81), channel_id=1, source_target_pairs={{0,16},{8,24},{16,0},{24,8},{1,17},{9,25},{17,1},{25,9},{2,18},{10... | collective-permute-start | bytes 1327112 | tf_op jit(solution)/shard_map/ppermute | solution.py:19
  176.1 20.2 %collective-permute-start.21 = (bf16[3,192,384]{2,1,0:T(8,128)(2,1)S(1)}, bf16[3,192,384]{2,1,0:T(8,128)(2,1)}, u32[]{:S(2)}, u32[]{:S(2)}) collective-permute-start(bf16[3,192,384]{2,1,0:T(8,128)(2,1)S(1)} %get-tuple-element.79), channel_id=1, source_target_pairs={{0,8},{8,0},{16,24},{24,16},{1,9},{9,1},{17,25},{25,17},{2,10},{10... | collective-permute-start | bytes 1327112 | tf_op jit(solution)/shard_map/ppermute | solution.py:19
  176.7 7.8 %collective-permute-start.27 = (bf16[2,192,384]{1,2,0:T(8,128)(2,1)S(1)}, bf16[2,192,384]{1,2,0:T(8,128)(2,1)S(1)}, u32[]{:S(2)}, u32[]{:S(2)}) collective-permute-start(bf16[2,192,384]{1,2,0:T(8,128)(2,1)S(1)} %get-tuple-element.103), channel_id=1, source_target_pairs={{0,4},{4,0},{1,5},{5,1},{2,6},{6,2},{3,7},{7,3},{8,12},{12,8},{9,1... | collective-permute-start | bytes 884744 | tf_op jit(solution)/shard_map/ppermute | solution.py:19
  178.1 9.4 %collective-permute-start.30 = (bf16[2,192,384]{1,2,0:T(8,128)(2,1)}, bf16[2,192,384]{1,2,0:T(8,128)(2,1)S(1)}, u32[]{:S(2)}, u32[]{:S(2)}) collective-permute-start(bf16[2,192,384]{1,2,0:T(8,128)(2,1)} %get-tuple-element.101), channel_id=1, source_target_pairs={{0,2},{1,3},{2,0},{3,1},{4,6},{5,7},{6,4},{7,5},{8,10},{9,11},{10,... | collective-permute-start | bytes 884744 | tf_op jit(solution)/shard_map/ppermute | solution.py:19
  186.0 13.3 %collective-permute-start.28 = (bf16[2,2,192,384]{3,2,1,0:T(8,128)(2,1)S(1)}, bf16[2,2,192,384]{3,2,1,0:T(8,128)(2,1)}, u32[]{:S(2)}, u32[]{:S(2)}) collective-permute-start(bf16[2,2,192,384]{3,2,1,0:T(8,128)(2,1)S(1)} %copy.95), channel_id=1, source_target_pairs={{0,2},{1,3},{2,0},{3,1},{4,6},{5,7},{6,4},{7,5},{8,10},{9,11},{10,... | collective-permute-start | bytes 1769480 | tf_op jit(solution)/shard_map/ppermute | solution.py:19
  190.5 16.4 %collective-permute-start.31 = (bf16[2,2,192,384]{3,2,1,0:T(8,128)(2,1)}, bf16[2,2,192,384]{3,2,1,0:T(8,128)(2,1)}, u32[]{:S(2)}, u32[]{:S(2)}) collective-permute-start(bf16[2,2,192,384]{3,2,1,0:T(8,128)(2,1)} %copy.99), channel_id=1, source_target_pairs={{0,4},{4,0},{1,5},{5,1},{2,6},{6,2},{3,7},{7,3},{8,12},{12,8},{9,1... | collective-permute-start | bytes 1769480 | tf_op jit(solution)/shard_map/ppermute | solution.py:19
  206.9 21.9 %collective-permute-start.29 = (bf16[2,2,2,192,384]{4,3,2,1,0:T(8,128)(2,1)}, bf16[2,2,2,192,384]{4,3,2,1,0:T(8,128)(2,1)}, u32[]{:S(2)}, u32[]{:S(2)}) collective-permute-start(bf16[2,2,2,192,384]{4,3,2,1,0:T(8,128)(2,1)} %copy.97), channel_id=1, source_target_pairs={{0,1},{1,0},{2,3},{3,2},{4,5},{5,4},{6,7},{7,6},{8,9},{9,8},{10,11... | collective-permute-start | bytes 3538952 | tf_op jit(solution)/shard_map/ppermute | solution.py:19
  214.8 23.5 %collective-permute-start.32 = (bf16[2,2,2,192,384]{4,3,2,1,0:T(8,128)(2,1)}, bf16[2,2,2,192,384]{4,3,2,1,0:T(8,128)(2,1)}, u32[]{:S(2)}, u32[]{:S(2)}) collective-permute-start(bf16[2,2,2,192,384]{4,3,2,1,0:T(8,128)(2,1)} %copy.101), channel_id=1, source_target_pairs={{0,1},{1,0},{2,3},{3,2},{4,5},{5,4},{6,7},{7,6},{8,9},{9,8},{10,11... | collective-permute-start | bytes 3538952 | tf_op jit(solution)/shard_map/ppermute | solution.py:19
  215.3 6.9 %collective-permute-start.24 = (f32[192,192]{0,1:T(8,128)S(1)}, f32[192,192]{0,1:T(8,128)S(1)}, u32[]{:S(2)}, u32[]{:S(2)}) collective-permute-start(f32[192,192]{0,1:T(8,128)S(1)} %broadcast_select_fusion.2), channel_id=1, source_target_pairs={{0,4},{4,0},{1,5},{5,1},{2,6},{6,2},{3,7},{7,3},{8,12},{12,8},{9,1... | collective-permute-start | bytes 442376 | tf_op jit(solution)/shard_map/ppermute | solution.py:19
  216.8 11.1 %collective-permute-start.25 = (bf16[192,384]{1,0:T(8,128)(2,1)S(1)}, bf16[192,384]{1,0:T(8,128)(2,1)S(1)}, u32[]{:S(2)}, u32[]{:S(2)}) collective-permute-start(bf16[192,384]{1,0:T(8,128)(2,1)S(1)} %fusion.15), channel_id=1, source_target_pairs={{0,0},{1,8},{2,16},{3,24},{4,4},{5,12},{6,20},{7,28},{8,1},{9,9},{... | collective-permute-start | bytes 442376 | tf_op jit(solution)/shard_map/ppermute | solution.py:561
  (8 other events, 17.0 us)
